TPU v7x, 32 devices: a whole 2x2x4 slice. The times are simulated.
32 devices in a mesh: dp: 4 (over z), lat: 2 (over core), lon: 4 (over y, x).
Axes of the slice: x: 2, y: 2, z: 4, core: 2. Of those that a mesh axis runs over, the one named last changes fastest.
Arguments:
- inputs: bfloat16 [48, 32, 64, 128], P('dp', 'lat', 'lon'), may hold values from -24 to 24
- lead_time: int32 [48], P('dp'), may hold values from 1 to 20
- cotangent: bfloat16 [48, 32, 64, 128], P('dp', 'lat', 'lon'), may hold values from -6 to 6
- conv_weight: float32 [2, 1152, 128], P(None, 'dp'), may hold values from -0.1875 to 0.1875
- conv_first: float32 [2, 1152, 128], P(None, 'dp'), may hold values from -0.01171875 to 0.01171875
- conv_second: float32 [2, 1152, 128], P(None, 'dp'), may hold values from 0 to 1, as said below
- vectors: float32 [6, 128], P(None, 'dp'), may hold values from -2 to 5, as said below
- vec_first: float32 [6, 128], P(None, 'dp'), may hold values from -0.005859375 to 0.005859375
- vec_second: float32 [6, 128], P(None, 'dp'), may hold values from 0 to 1, as said below
Outputs:
- outputs: bfloat16 [48, 32, 64, 128], P('dp', 'lat', 'lon')
- grad_inputs: bfloat16 [48, 32, 64, 128], P('dp', 'lat', 'lon')
- grad_norm: float32 [], replicated
- conv_new: float32 [2, 1152, 128], P(None, 'dp')
- conv_first_new: float32 [2, 1152, 128], P(None, 'dp')
- conv_second_new: float32 [2, 1152, 128], P(None, 'dp')
- conv_low: bfloat16 [2, 1152, 128], P(None, 'dp')
- vec_new: float32 [6, 128], P(None, 'dp')
- vec_first_new: float32 [6, 128], P(None, 'dp')
- vec_second_new: float32 [6, 128], P(None, 'dp')
Inputs may be any that keep to these rules, and one draw needn't show every extreme that they name: `conv_second`: positive. `vectors`: rows 1 and 4 are positive. `vec_second`: positive.
All inputs are finite; a program needn't handle non-finite values.
Results may differ from a plain program's by a relative error of at most 0.01.
Values may be sent and summed in bfloat16 or wider, within the bound.
No kernel may reach another device: no remote copies, remote signals or barrier semaphores. Data moves between devices by JAX's collectives and lax.ppermute only.
A program may use at most 128 MiB of HBM per device.

v0:
```python
import jax
import jax.numpy as jnp
from jax import lax
from jax.sharding import PartitionSpec as P

MB = 3
STEP = 5


EPS = 1e-05
CLIP = 1.0
BETA_ONE = 0.5
BETA_TWO = 0.5
RATE_CONV = 0.03
RATE_VEC = 0.3
DECAY_CONV = 0.01
ADAM_EPS = 1e-08


def with_halo(block, sides, width, periodic):
    for axis, dim in sides:
        count = lax.axis_size(axis)
        forward = [(i, i + 1) for i in range(count - 1)]
        if periodic:
            forward.append((count - 1, 0))
        backward = [(target, source) for source, target in forward]
        low = lax.ppermute(
            lax.slice_in_dim(block, block.shape[dim] - width, None, axis=dim), axis, forward
        )
        high = lax.ppermute(lax.slice_in_dim(block, 0, width, axis=dim), axis, backward)
        block = jnp.concatenate([low, block, high], axis=dim)
    return block


def grow_input_part(grid_low):
    widened = with_halo(grid_low, (("lon", 2),), 1, True)
    return with_halo(widened, (("lat", 1),), 1, False)


def grow_forward(grid_low):
    widened = with_halo(grid_low, (("lon", 2),), 1, True)
    return with_halo(widened, (("lat", 1),), 1, False)


def grow_backward(grid_low):
    widened = with_halo(grid_low, (("lon", 2),), 1, True)
    return with_halo(widened, (("lat", 1),), 1, False)


def kernel_of(weight):
    channels = weight.shape[1]
    return weight.reshape(channels, 3, 3, channels).transpose(1, 2, 0, 3)


def flipped(kernel):
    return kernel[::-1, ::-1].transpose(0, 1, 3, 2)


def convolve(padded, kernel):
    return lax.conv_general_dilated(
        padded,
        kernel,
        (1, 1),
        "VALID",
        dimension_numbers=("NHWC", "HWIO", "NHWC"),
        preferred_element_type=jnp.float32,
    )


def weight_grad(padded, grad_low):
    height = grad_low.shape[1]
    breadth = grad_low.shape[2]
    tap_terms = []
    for row_off in range(3):
        for col_off in range(3):
            window = padded[:, row_off : row_off + height, col_off : col_off + breadth, :]
            tap_terms.append(
                lax.dot_general(
                    window,
                    grad_low,
                    (((0, 1, 2), (0, 1, 2)), ((), ())),
                    preferred_element_type=jnp.float32,
                )
            )
    stacked = jnp.stack(tap_terms, axis=1)
    return stacked.reshape(-1, stacked.shape[2])


def batch_norm(active, gain_row, shift_row, count):
    totals = lax.psum(
        (jnp.sum(active, axis=(0, 1, 2)), jnp.sum(active * active, axis=(0, 1, 2))),
        ("dp", "lat", "lon"),
    )
    mean_val = totals[0] / count
    inverse = lax.rsqrt(totals[1] / count - mean_val * mean_val + EPS)
    normed = (active - mean_val) * inverse
    return (normed * gain_row + shift_row, normed, inverse)


def norm_backward(grad_in, normed, inverse, gain_row, count):
    totals = lax.psum(
        (jnp.sum(grad_in, axis=(0, 1, 2)), jnp.sum(grad_in * normed, axis=(0, 1, 2))),
        ("dp", "lat", "lon"),
    )
    active_grad = inverse * gain_row * (grad_in - totals[0] / count - normed * (totals[1] / count))
    return (active_grad, totals[1], totals[0])


def gelu_back(pre_act, upstream):
    unused, pullback = jax.vjp(jax.nn.gelu, pre_act)
    return pullback(upstream)[0]


def assemble(bias_rows, gain_rows, shift_rows):
    return jnp.stack(
        [bias_rows[0], gain_rows[0], shift_rows[0], bias_rows[1], gain_rows[1], shift_rows[1]]
    )


def adam_step(weight, first, second, grad, rate, decay):
    first_new = BETA_ONE * first + (1.0 - BETA_ONE) * grad
    second_new = BETA_TWO * second + (1.0 - BETA_TWO) * grad * grad
    first_hat = first_new / (1.0 - BETA_ONE**STEP)
    second_hat = second_new / (1.0 - BETA_TWO**STEP)
    weight_new = weight - rate * (first_hat / (jnp.sqrt(second_hat) + ADAM_EPS) + decay * weight)
    return (weight_new, first_new, second_new)


def body(
    inputs,
    lead_time,
    cotangent,
    conv_weight,
    conv_first,
    conv_second,
    vectors,
    vec_first,
    vec_second,
):
    rows_batch = inputs.shape[0] // MB
    count = float(
        rows_batch
        * inputs.shape[1]
        * inputs.shape[2]
        * lax.axis_size("dp")
        * lax.axis_size("lat")
        * lax.axis_size("lon")
    )
    lead_scale = 0.5 * jnp.sqrt(lead_time.astype(jnp.float32))
    local_low = (conv_weight.astype(jnp.bfloat16), vectors.astype(jnp.bfloat16))
    channels = conv_weight.shape[2]
    grad_conv = jnp.zeros((2, conv_weight.shape[1] * lax.axis_size("dp"), channels), jnp.float32)
    grad_bias = jnp.zeros((2, channels), jnp.float32)
    grad_gain = jnp.zeros((2, channels), jnp.float32)
    grad_shift = jnp.zeros((2, channels), jnp.float32)
    outputs_list = []
    grads_list = []
    for batch_index in range(MB):
        weights, params = (
            lax.all_gather(local_low[0], "dp", axis=1, tiled=True),
            lax.all_gather(local_low[1], "dp", axis=1, tiled=True),
        )
        params = params.astype(jnp.float32)
        kernel_one = kernel_of(weights[0])
        kernel_two = kernel_of(weights[1])
        row_start = batch_index * rows_batch
        row_stop = row_start + rows_batch
        sample_in = inputs[row_start:row_stop]
        padded_in = grow_input_part(sample_in)
        pre_one = convolve(padded_in, kernel_one) + params[0]
        norm_one, normed_one, inverse_one = batch_norm(
            jax.nn.gelu(pre_one), params[1], params[2], count
        )
        padded_mid = grow_forward(norm_one.astype(jnp.bfloat16))
        pre_two = convolve(padded_mid, kernel_two) + params[3]
        norm_two, normed_two, inverse_two = batch_norm(
            jax.nn.gelu(pre_two), params[4], params[5], count
        )
        outputs_list.append((sample_in.astype(jnp.float32) + norm_two).astype(jnp.bfloat16))
        grad_out = (
            cotangent[row_start:row_stop].astype(jnp.float32)
            * lead_scale[row_start:row_stop, None, None, None]
        )
        act_two, gain_two, shift_two = norm_backward(
            grad_out, normed_two, inverse_two, params[4], count
        )
        grad_two = gelu_back(pre_two, act_two).astype(jnp.bfloat16)
        mid_grad = convolve(grow_backward(grad_two), flipped(kernel_two))
        act_one, gain_one, shift_one = norm_backward(
            mid_grad, normed_one, inverse_one, params[1], count
        )
        grad_one = gelu_back(pre_one, act_one).astype(jnp.bfloat16)
        input_grad = grad_out + convolve(grow_backward(grad_one), flipped(kernel_one))
        grads_list.append(input_grad.astype(jnp.bfloat16))
        grad_conv = grad_conv + jnp.stack(
            [weight_grad(padded_in, grad_one), weight_grad(padded_mid, grad_two)]
        )
        grad_bias = grad_bias + jnp.stack(
            [
                jnp.sum(grad_one, axis=(0, 1, 2), dtype=jnp.float32),
                jnp.sum(grad_two, axis=(0, 1, 2), dtype=jnp.float32),
            ]
        )
        grad_gain = grad_gain + jnp.stack([gain_one, gain_two])
        grad_shift = grad_shift + jnp.stack([shift_one, shift_two])
    columns = vectors.shape[1]
    col_start = lax.axis_index("dp") * columns
    own_rows = conv_weight.shape[1]
    conv_total, bias_total = lax.psum((grad_conv, grad_bias), ("dp", "lat", "lon"))
    vec_total = assemble(bias_total, grad_gain, grad_shift)
    grad_norm = jnp.sqrt(jnp.sum(conv_total * conv_total) + jnp.sum(vec_total * vec_total))
    conv_own = lax.dynamic_slice_in_dim(conv_total, lax.axis_index("dp") * own_rows, own_rows, 1)
    vec_own = lax.dynamic_slice_in_dim(vec_total, col_start, columns, 1)
    clip_factor = jnp.minimum(1.0, CLIP / (grad_norm + 1e-06))
    conv_new, conv_first_new, conv_second_new = adam_step(
        conv_weight, conv_first, conv_second, conv_own * clip_factor, RATE_CONV, DECAY_CONV
    )
    vec_new, vec_first_new, vec_second_new = adam_step(
        vectors, vec_first, vec_second, vec_own * clip_factor, RATE_VEC, 0.0
    )
    outputs = jnp.concatenate(outputs_list, axis=0)
    grad_inputs = jnp.concatenate(grads_list, axis=0)
    return (
        outputs,
        grad_inputs,
        grad_norm,
        conv_new,
        conv_first_new,
        conv_second_new,
        conv_new.astype(jnp.bfloat16),
        vec_new,
        vec_first_new,
        vec_second_new,
    )


def solution(mesh):
    in_specs = (
        P("dp", "lat", "lon", None),
        P("dp"),
        P("dp", "lat", "lon", None),
        P(None, "dp", None),
        P(None, "dp", None),
        P(None, "dp", None),
        P(None, "dp"),
        P(None, "dp"),
        P(None, "dp"),
    )
    out_specs = (
        P("dp", "lat", "lon", None),
        P("dp", "lat", "lon", None),
        P(),
        P(None, "dp", None),
        P(None, "dp", None),
        P(None, "dp", None),
        P(None, "dp", None),
        P(None, "dp"),
        P(None, "dp"),
        P(None, "dp"),
    )
    return jax.shard_map(body, mesh=mesh, in_specs=in_specs, out_specs=out_specs, check_vma=False)
```

profile of v0, /device:TPU:0, one launch (start us, length us, event | category | flops | bytes accessed | tf_op | source)
XLA Modules:
  0.0 862.4 jit_solution(3652635132821725213)
XLA Ops:
  7.2 1.4 fusion.319
  8.6 3.9 collective-permute-start.9
  12.6 2.9 collective-permute-start.17
  15.5 2.9 collective-permute-start.1
  19.7 12.1 %all-gather = bf16[4,32,6]{1,2,0:T(8,128)(2,1)S(1)} all-gather(bf16[1,32,6]{1,2,0:T(8,128)(2,1)S(1)} %convert_bitcast_fusion), channel_id=1, replica_groups=mesh['dp'=4,'lat'=2,'lon'=4] {'dp'}, dimensions={0}, use_global_device_ids=true | all-gather | bytes 1920 | tf_op jit(solution)/shard_map/all_gather | solution.py:161
  32.5 15.8 %all_gather.4 = bf16[2,1152,128]{2,1,0:T(8,128)(2,1)S(1)} all-gather(bf16[2,288,128]{2,1,0:T(8,128)(2,1)S(1)} %convert_element_type.99), channel_id=1, replica_groups=mesh['dp'=4,'lat'=2,'lon'=4] {'dp'}, dimensions={1}, use_global_device_ids=true | all-gather | bytes 737280 | tf_op jit(solution)/shard_map/all_gather | solution.py:160
  53.1 3.0 collective-permute-start.10
  57.5 3.0 collective-permute-start.18
  62.5 4.2 collective-permute-start.2
  69.1 1.4 select_reduce_fusion.16
  70.5 2.0 fusion.13
  72.4 39.2 %all-reduce.10 = (f32[128]{0:T(128)S(1)}, f32[128]{0:T(128)S(1)}) all-reduce(f32[128]{0:T(128)S(1)} %get-tuple-element.43, f32[128]{0:T(128)S(1)} %get-tuple-element.42), channel_id=1, replica_groups=mesh['dp'=4,'lat'=2,'lon'=4] {'dp','lat','lon'}, use_global_device_ids=true, to_apply=%region_11.0 | all-reduce | flops 256 | bytes 2048 | tf_op jit(solution)/shard_map/psum | solution.py:90
  112.9 2.3 collective-permute-start.13
  117.9 2.0 pad_maximum_fusion.2
  122.7 3.5 collective-permute-start.14
  130.0 1.4 select_reduce_fusion.14
  131.3 1.4 copy.207
  132.7 41.0 %all-reduce.9 = (f32[128]{0:T(128)S(1)}, f32[128]{0:T(128)S(1)}) all-reduce(f32[128]{0:T(128)S(1)} %get-tuple-element.41, f32[128]{0:T(128)S(1)} %get-tuple-element.40), channel_id=1, replica_groups=mesh['dp'=4,'lat'=2,'lon'=4] {'dp','lat','lon'}, use_global_device_ids=true, to_apply=%region_15.0 | all-reduce | flops 256 | bytes 2048 | tf_op jit(solution)/shard_map/psum | solution.py:90
  175.6 1.4 copy.209
  176.9 1.4 copy.208
  178.3 1.3 copy.206
  180.5 39.5 %all-reduce.8 = (f32[128]{0:T(128)S(1)}, f32[128]{0:T(128)S(1)}) all-reduce(f32[128]{0:T(128)S(1)} %get-tuple-element.51, f32[128]{0:T(128)S(1)} %get-tuple-element.50), channel_id=1, replica_groups=mesh['dp'=4,'lat'=2,'lon'=4] {'dp','lat','lon'}, use_global_device_ids=true, to_apply=%region_35.0 | all-reduce | flops 256 | bytes 2048 | tf_op jit(solution)/shard_map/psum | solution.py:101
  222.8 2.2 collective-permute-start.33
  227.8 1.8 collective-permute-done.32
  231.0 3.2 collective-permute-start.34
  237.3 3.1 select_reduce_fusion.4
  240.3 39.8 %all-reduce.7 = (f32[128]{0:T(128)S(1)}, f32[128]{0:T(128)S(1)}) all-reduce(f32[128]{0:T(128)S(1)} %get-tuple-element.56, f32[128]{0:T(128)S(1)} %get-tuple-element.57), channel_id=1, replica_groups=mesh['dp'=4,'lat'=2,'lon'=4] {'dp','lat','lon'}, use_global_device_ids=true, to_apply=%region_19.0 | all-reduce | flops 256 | bytes 2048 | tf_op jit(solution)/shard_map/psum | solution.py:90
  281.4 3.4 collective-permute-start.21
  286.4 3.2 collective-permute-done.20
  290.9 3.0 collective-permute-start.22
  298.3 1.4 select_reduce_fusion.10
  299.7 1.4 copy.223
  301.0 37.8 %all-reduce.6 = (f32[128]{0:T(128)S(1)}, f32[128]{0:T(128)S(1)}) all-reduce(f32[128]{0:T(128)S(1)} %get-tuple-element.45, f32[128]{0:T(128)S(1)} %get-tuple-element.44), channel_id=1, replica_groups=mesh['dp'=4,'lat'=2,'lon'=4] {'dp','lat','lon'}, use_global_device_ids=true, to_apply=%region_23.0 | all-reduce | flops 256 | bytes 2048 | tf_op jit(solution)/shard_map/psum | solution.py:90
  340.2 1.4 copy.225
  342.9 1.4 copy.222
  345.5 40.7 %all-reduce.5 = (f32[128]{0:T(128)S(1)}, f32[128]{0:T(128)S(1)}) all-reduce(f32[128]{0:T(128)S(1)} %get-tuple-element.53, f32[128]{0:T(128)S(1)} %get-tuple-element.52), channel_id=1, replica_groups=mesh['dp'=4,'lat'=2,'lon'=4] {'dp','lat','lon'}, use_global_device_ids=true, to_apply=%region_43.0 | all-reduce | flops 256 | bytes 2048 | tf_op jit(solution)/shard_map/psum | solution.py:101
  388.9 3.2 collective-permute-start.41
  398.1 3.6 collective-permute-start.42
  407.1 2.2 select_reduce_fusion.1
  409.3 38.3 %all-reduce.4 = (f32[128]{0:T(128)S(1)}, f32[128]{0:T(128)S(1)}, f32[128]{0:T(128)S(1)}, f32[128]{0:T(128)S(1)}) all-reduce(f32[128]{0:T(128)S(1)} %get-tuple-element.35, f32[128]{0:T(128)S(1)} %get-tuple-element.34, f32[128]{0:T(128)S(1)} %copy-done.160, ...), channel_id=1, replica_groups=mesh['dp'=4,'lat'=2,'lon'=4] {'dp','lat','lon'}, use_global_device_ids=true, to_apply=%region_45.0 | all-reduce | flops 512 | bytes 4096 | tf_op jit(solution)/shard_map/psum | solution.py:101
  447.7 5.7 select_reduce_fusion.20
  453.5 40.7 %all-reduce.3 = (f32[128]{0:T(128)S(1)}, f32[128]{0:T(128)S(1)}) all-reduce(f32[128]{0:T(128)S(1)} %get-tuple-element.39, f32[128]{0:T(128)S(1)} %get-tuple-element.38), channel_id=1, replica_groups=mesh['dp'=4,'lat'=2,'lon'=4] {'dp','lat','lon'}, use_global_device_ids=true, to_apply=%region_3.0 | all-reduce | flops 256 | bytes 2048 | tf_op jit(solution)/shard_map/psum | solution.py:90
  496.9 3.2 collective-permute-start.5
  501.0 2.9 collective-permute-start.45
  504.9 2.9 collective-permute-start.37
  522.3 1.4 copy.257
  526.2 3.0 collective-permute-start.6
  531.2 3.0 collective-permute-start.46
  536.9 4.4 collective-permute-start.38
  542.7 1.4 select_reduce_fusion.18
  546.7 39.0 %all-reduce.2 = (f32[128]{0:T(128)S(1)}, f32[128]{0:T(128)S(1)}) all-reduce(f32[128]{0:T(128)S(1)} %get-tuple-element.37, f32[128]{0:T(128)S(1)} %get-tuple-element.36), channel_id=1, replica_groups=mesh['dp'=4,'lat'=2,'lon'=4] {'dp','lat','lon'}, use_global_device_ids=true, to_apply=%region_7.0 | all-reduce | flops 256 | bytes 2048 | tf_op jit(solution)/shard_map/psum | solution.py:90
  597.5 1.4 copy.193
  598.8 1.4 copy.192
  602.4 40.9 %all-reduce.1 = (f32[128]{0:T(128)S(1)}, f32[128]{0:T(128)S(1)}) all-reduce(f32[128]{0:T(128)S(1)} %get-tuple-element.49, f32[128]{0:T(128)S(1)} %get-tuple-element.48), channel_id=1, replica_groups=mesh['dp'=4,'lat'=2,'lon'=4] {'dp','lat','lon'}, use_global_device_ids=true, to_apply=%region_27.0 | all-reduce | flops 256 | bytes 2048 | tf_op jit(solution)/shard_map/psum | solution.py:101
  646.1 3.2 collective-permute-start.25
  657.0 3.0 collective-permute-start.26
  665.2 39.2 %all-reduce = (f32[128]{0:T(128)S(1)}, f32[128]{0:T(128)S(1)}) all-reduce(f32[128]{0:T(128)S(1)} %get-tuple-element.31, f32[128]{0:T(128)S(1)} %get-tuple-element.30), channel_id=1, replica_groups=mesh['dp'=4,'lat'=2,'lon'=4] {'dp','lat','lon'}, use_global_device_ids=true, to_apply=%region_29.0 | all-reduce | flops 256 | bytes 2048 | tf_op jit(solution)/shard_map/psum | solution.py:101
  705.5 2.5 collective-permute-start.29
  712.9 2.9 fusion.18
  716.5 41.3 %psum.207 = f32[2,128]{1,0:T(2,128)S(1)} all-reduce(f32[2,128]{1,0:T(2,128)S(1)} %fusion.273), channel_id=1, replica_groups=mesh['dp'=4,'lat'=2,'lon'=4] {'dp','lat','lon'}, use_global_device_ids=true, to_apply=%region_56.0 | all-reduce | flops 256 | bytes 2048 | tf_op jit(solution)/shard_map/psum | solution.py:209
  759.3 3.0 collective-permute-start.30
  767.9 79.7 %all-reduce.13.cloned.1.call-done = f32[2,1152,128]{2,1,0:T(8,128)} async-done(((f32[2,1152,128]{2,1,0:T(8,128)}), f32[2,1152,128]{2,1,0:T(8,128)}) %all-reduce.13.cloned.1.call-update) | async-done | bytes 1179664 | tf_op jit(solution)/shard_map/psum | solution.py:209
  847.6 2.2 multiply_reduce_fusion
  851.9 2.1 fusion.310
  (683 shorter events, 133.8 us)
Async XLA Ops:
  7.2 840.4 %all-reduce.13.cloned.1.call-start = ((), (), s32[]{:S(2)}) async-start(), calls=%async_computation | async-start | bytes 2359296 | tf_op jit(solution)/shard_map/psum | solution.py:209
  8.6 43.0 %collective-permute-start.9 = (bf16[4,16,1,128]{3,2,1,0:T(2,128)(2,1)S(1)}, bf16[4,16,1,128]{3,2,1,0:T(2,128)(2,1)S(1)}, u32[]{:S(2)}, u32[]{:S(2)}) collective-permute-start(bf16[4,16,1,128]{3,2,1,0:T(2,128)(2,1)S(1)} %get-tuple-element.130), channel_id=1, source_target_pairs={{1,0},{2,1},{3,2},{0,3},{5,4},{6,5},{7,6},{4,7},{9,8},{10,9},{11,1... | collective-permute-start | bytes 49160 | tf_op jit(solution)/shard_map/ppermute | solution.py:30
  12.6 39.1 %collective-permute-start.8 = (bf16[4,16,1,128]{3,2,1,0:T(2,128)(2,1)S(1)}, bf16[4,16,1,128]{3,2,1,0:T(2,128)(2,1)S(1)}, u32[]{:S(2)}, u32[]{:S(2)}) collective-permute-start(bf16[4,16,1,128]{3,2,1,0:T(2,128)(2,1)S(1)} %get-tuple-element.131), channel_id=1, source_target_pairs={{0,1},{1,2},{2,3},{3,0},{4,5},{5,6},{6,7},{7,4},{8,9},{9,10},{10,1... | collective-permute-start | bytes 49160 | tf_op jit(solution)/shard_map/ppermute | solution.py:27
  12.6 40.5 %collective-permute-start.17 = (bf16[4,16,1,128]{3,2,1,0:T(2,128)(2,1)S(1)}, bf16[4,16,1,128]{3,2,1,0:T(2,128)(2,1)S(1)}, u32[]{:S(2)}, u32[]{:S(2)}) collective-permute-start(bf16[4,16,1,128]{3,2,1,0:T(2,128)(2,1)S(1)} %get-tuple-element.133), channel_id=1, source_target_pairs={{1,0},{2,1},{3,2},{0,3},{5,4},{6,5},{7,6},{4,7},{9,8},{10,9},{11,1... | collective-permute-start | bytes 49160 | tf_op jit(solution)/shard_map/ppermute | solution.py:30
  15.5 40.6 %collective-permute-start.16 = (bf16[4,16,1,128]{3,2,1,0:T(2,128)(2,1)S(1)}, bf16[4,16,1,128]{3,2,1,0:T(2,128)(2,1)S(1)}, u32[]{:S(2)}, u32[]{:S(2)}) collective-permute-start(bf16[4,16,1,128]{3,2,1,0:T(2,128)(2,1)S(1)} %get-tuple-element.134), channel_id=1, source_target_pairs={{0,1},{1,2},{2,3},{3,0},{4,5},{5,6},{6,7},{7,4},{8,9},{9,10},{10,1... | collective-permute-start | bytes 49160 | tf_op jit(solution)/shard_map/ppermute | solution.py:27
  15.5 41.9 %collective-permute-start.1 = (bf16[4,16,1,128]{3,2,1,0:T(2,128)(2,1)S(1)}, bf16[4,16,1,128]{3,2,1,0:T(2,128)(2,1)S(1)}, u32[]{:S(2)}, u32[]{:S(2)}) collective-permute-start(bf16[4,16,1,128]{3,2,1,0:T(2,128)(2,1)S(1)} %get-tuple-element.132), channel_id=1, source_target_pairs={{1,0},{2,1},{3,2},{0,3},{5,4},{6,5},{7,6},{4,7},{9,8},{10,9},{11,1... | collective-permute-start | bytes 49160 | tf_op jit(solution)/shard_map/ppermute | solution.py:30
  31.9 306.9 %copy-start.100 = (f32[128,6]{0,1:T(8,128)}, f32[128,6]{0,1:T(8,128)S(1)}, u32[]{:S(2)}) copy-start(f32[128,6]{0,1:T(8,128)S(1)} %reshape.256) | copy-start | bytes 9220
  32.4 79.7 %copy-start.108 = (f32[128]{0:T(128)}, f32[128]{0:T(128)S(1)}, u32[]{:S(2)}) copy-start(f32[128]{0:T(128)S(1)} %get-tuple-element.201) | copy-start | bytes 1540
  32.4 248.2 %copy-start.106 = (f32[128]{0:T(128)}, f32[128]{0:T(128)S(1)}, u32[]{:S(2)}) copy-start(f32[128]{0:T(128)S(1)} %get-tuple-element.200) | copy-start | bytes 1540
  32.4 306.4 %copy-start.103 = (f32[128]{0:T(128)}, f32[128]{0:T(128)S(1)}, u32[]{:S(2)}) copy-start(f32[128]{0:T(128)S(1)} %get-tuple-element.198) | copy-start | bytes 1540
  32.4 306.4 %copy-start.105 = (f32[128]{0:T(128)}, f32[128]{0:T(128)S(1)}, u32[]{:S(2)}) copy-start(f32[128]{0:T(128)S(1)} %get-tuple-element.199) | copy-start | bytes 1540
  51.7 8.8 %collective-permute-start = (bf16[4,16,1,128]{3,2,1,0:T(2,128)(2,1)S(1)}, bf16[4,16,1,128]{3,2,1,0:T(2,128)(2,1)S(1)}, u32[]{:S(2)}, u32[]{:S(2)}) collective-permute-start(bf16[4,16,1,128]{3,2,1,0:T(2,128)(2,1)S(1)} %get-tuple-element.129), channel_id=1, source_target_pairs={{0,1},{1,2},{2,3},{3,0},{4,5},{5,6},{6,7},{7,4},{8,9},{9,10},{10,1... | collective-permute-start | bytes 49160 | tf_op jit(solution)/shard_map/ppermute | solution.py:27
  51.8 10.7 %collective-permute-start.11 = (bf16[4,1,18,128]{3,2,1,0:T(8,128)(2,1)S(1)}, bf16[4,1,18,128]{3,2,1,0:T(8,128)(2,1)S(1)}, u32[]{:S(2)}, u32[]{:S(2)}) collective-permute-start(bf16[4,1,18,128]{3,2,1,0:T(8,128)(2,1)S(1)} %get-tuple-element.172), channel_id=1, source_target_pairs={{4,0},{5,1},{6,2},{7,3},{12,8},{13,9},{14,10},{15,11},{20,16},{21,... | collective-permute-start | bytes 55304 | tf_op jit(solution)/shard_map/ppermute | solution.py:30
  53.1 13.6 %collective-permute-start.10 = (bf16[4,1,18,128]{3,2,1,0:T(8,128)(2,1)S(1)}, bf16[4,1,18,128]{3,2,1,0:T(8,128)(2,1)S(1)}, u32[]{:S(2)}, u32[]{:S(2)}) collective-permute-start(bf16[4,1,18,128]{3,2,1,0:T(8,128)(2,1)S(1)} %get-tuple-element.171), channel_id=1, source_target_pairs={{0,4},{1,5},{2,6},{3,7},{8,12},{9,13},{10,14},{11,15},{16,20},{17,... | collective-permute-start | bytes 55304 | tf_op jit(solution)/shard_map/ppermute | solution.py:27
  56.1 11.5 %collective-permute-start.19 = (bf16[4,1,18,128]{3,2,1,0:T(8,128)(2,1)S(1)}, bf16[4,1,18,128]{3,2,1,0:T(8,128)(2,1)S(1)}, u32[]{:S(2)}, u32[]{:S(2)}) collective-permute-start(bf16[4,1,18,128]{3,2,1,0:T(8,128)(2,1)S(1)} %get-tuple-element.168), channel_id=1, source_target_pairs={{4,0},{5,1},{6,2},{7,3},{12,8},{13,9},{14,10},{15,11},{20,16},{21,... | collective-permute-start | bytes 55304 | tf_op jit(solution)/shard_map/ppermute | solution.py:30
  57.5 10.2 %collective-permute-start.18 = (bf16[4,1,18,128]{3,2,1,0:T(8,128)(2,1)S(1)}, bf16[4,1,18,128]{3,2,1,0:T(8,128)(2,1)S(1)}, u32[]{:S(2)}, u32[]{:S(2)}) collective-permute-start(bf16[4,1,18,128]{3,2,1,0:T(8,128)(2,1)S(1)} %get-tuple-element.167), channel_id=1, source_target_pairs={{0,4},{1,5},{2,6},{3,7},{8,12},{9,13},{10,14},{11,15},{16,20},{17,... | collective-permute-start | bytes 55304 | tf_op jit(solution)/shard_map/ppermute | solution.py:27
  61.1 56.8 %collective-permute-start.3 = (bf16[4,1,18,128]{3,2,1,0:T(8,128)(2,1)}, bf16[4,1,18,128]{3,2,1,0:T(8,128)(2,1)}, u32[]{:S(2)}, u32[]{:S(2)}) collective-permute-start(bf16[4,1,18,128]{3,2,1,0:T(8,128)(2,1)} %get-tuple-element.164), channel_id=1, source_target_pairs={{4,0},{5,1},{6,2},{7,3},{12,8},{13,9},{14,10},{15,11},{20,16},{21,... | collective-permute-start | bytes 55304 | tf_op jit(solution)/shard_map/ppermute | solution.py:30
  62.5 55.5 %collective-permute-start.2 = (bf16[4,1,18,128]{3,2,1,0:T(8,128)(2,1)}, bf16[4,1,18,128]{3,2,1,0:T(8,128)(2,1)}, u32[]{:S(2)}, u32[]{:S(2)}) collective-permute-start(bf16[4,1,18,128]{3,2,1,0:T(8,128)(2,1)} %get-tuple-element.163), channel_id=1, source_target_pairs={{0,4},{1,5},{2,6},{3,7},{8,12},{9,13},{10,14},{11,15},{16,20},{17,... | collective-permute-start | bytes 55304 | tf_op jit(solution)/shard_map/ppermute | solution.py:27
  112.9 8.4 collective-permute-start.13
  115.2 6.1 collective-permute-start.12
  121.4 6.0 collective-permute-start.15
  122.7 4.7 collective-permute-start.14
  222.8 5.0 collective-permute-start.33
  225.0 4.6 collective-permute-start.32
  229.7 4.8 collective-permute-start.35
  231.0 4.3 collective-permute-start.34
  237.2 43.4 %copy-start.109 = (f32[128]{0:T(128)S(1)}, f32[128]{0:T(128)}, u32[]{:S(2)}) copy-start(f32[128]{0:T(128)} %copy-done.108) | copy-start | bytes 1540
  281.4 5.0 collective-permute-start.21
  284.8 4.8 collective-permute-start.20
  289.6 7.3 collective-permute-start.23
  290.9 6.0 collective-permute-start.22
  388.9 6.5 collective-permute-start.41
  392.1 4.6 collective-permute-start.40
  396.8 7.8 collective-permute-start.43
  398.1 6.5 collective-permute-start.42
  447.7 47.8 %copy-start.107 = (f32[128]{0:T(128)S(1)}, f32[128]{0:T(128)}, u32[]{:S(2)}) copy-start(f32[128]{0:T(128)} %copy-done.106) | copy-start | bytes 1540
  447.7 47.8 %copy-start.110 = (f32[128]{0:T(128)S(1)}, f32[128]{0:T(128)}, u32[]{:S(2)}) copy-start(f32[128]{0:T(128)} %copy-done.108) | copy-start | bytes 1540
  453.5 42.6 %copy-start.3 = (f32[16,32,3,128]{3,1,2,0:T(8,128)}, f32[16,32,3,128]{3,1,2,0:T(8,128)S(1)}, u32[]{:S(2)}) copy-start(f32[16,32,3,128]{3,1,2,0:T(8,128)S(1)} %get-tuple-element.223) | copy-start | bytes 2359300
  496.9 27.9 %collective-permute-start.5 = (bf16[4,16,1,128]{3,2,1,0:T(2,128)(2,1)}, bf16[4,16,1,128]{3,2,1,0:T(2,128)(2,1)S(1)}, u32[]{:S(2)}, u32[]{:S(2)}) collective-permute-start(bf16[4,16,1,128]{3,2,1,0:T(2,128)(2,1)} %get-tuple-element.188), channel_id=1, source_target_pairs={{1,0},{2,1},{3,2},{0,3},{5,4},{6,5},{7,6},{4,7},{9,8},{10,9},{11,1... | collective-permute-start | bytes 49160 | tf_op jit(solution)/shard_map/ppermute | solution.py:30
  500.1 24.7 %collective-permute-start.4 = (bf16[4,16,1,128]{3,2,1,0:T(2,128)(2,1)}, bf16[4,16,1,128]{3,2,1,0:T(2,128)(2,1)S(1)}, u32[]{:S(2)}, u32[]{:S(2)}) collective-permute-start(bf16[4,16,1,128]{3,2,1,0:T(2,128)(2,1)} %get-tuple-element.187), channel_id=1, source_target_pairs={{0,1},{1,2},{2,3},{3,0},{4,5},{5,6},{6,7},{7,4},{8,9},{9,10},{10,1... | collective-permute-start | bytes 49160 | tf_op jit(solution)/shard_map/ppermute | solution.py:27
  501.0 25.1 %collective-permute-start.45 = (bf16[4,16,1,128]{3,2,1,0:T(2,128)(2,1)}, bf16[4,16,1,128]{3,2,1,0:T(2,128)(2,1)}, u32[]{:S(2)}, u32[]{:S(2)}) collective-permute-start(bf16[4,16,1,128]{3,2,1,0:T(2,128)(2,1)} %get-tuple-element.186), channel_id=1, source_target_pairs={{1,0},{2,1},{3,2},{0,3},{5,4},{6,5},{7,6},{4,7},{9,8},{10,9},{11,1... | collective-permute-start | bytes 49160 | tf_op jit(solution)/shard_map/ppermute | solution.py:30
  504.0 25.2 %collective-permute-start.44 = (bf16[4,16,1,128]{3,2,1,0:T(2,128)(2,1)}, bf16[4,16,1,128]{3,2,1,0:T(2,128)(2,1)}, u32[]{:S(2)}, u32[]{:S(2)}) collective-permute-start(bf16[4,16,1,128]{3,2,1,0:T(2,128)(2,1)} %get-tuple-element.185), channel_id=1, source_target_pairs={{0,1},{1,2},{2,3},{3,0},{4,5},{5,6},{6,7},{7,4},{8,9},{9,10},{10,1... | collective-permute-start | bytes 49160 | tf_op jit(solution)/shard_map/ppermute | solution.py:27
  504.9 26.3 %collective-permute-start.37 = (bf16[4,16,1,128]{3,2,1,0:T(2,128)(2,1)}, bf16[4,16,1,128]{3,2,1,0:T(2,128)(2,1)}, u32[]{:S(2)}, u32[]{:S(2)}) collective-permute-start(bf16[4,16,1,128]{3,2,1,0:T(2,128)(2,1)} %get-tuple-element.184), channel_id=1, source_target_pairs={{1,0},{2,1},{3,2},{0,3},{5,4},{6,5},{7,6},{4,7},{9,8},{10,9},{11,1... | collective-permute-start | bytes 49160 | tf_op jit(solution)/shard_map/ppermute | solution.py:30
  524.7 9.5 %collective-permute-start.36 = (bf16[4,16,1,128]{3,2,1,0:T(2,128)(2,1)S(1)}, bf16[4,16,1,128]{3,2,1,0:T(2,128)(2,1)S(1)}, u32[]{:S(2)}, u32[]{:S(2)}) collective-permute-start(bf16[4,16,1,128]{3,2,1,0:T(2,128)(2,1)S(1)} %copy-done.99), channel_id=1, source_target_pairs={{0,1},{1,2},{2,3},{3,0},{4,5},{5,6},{6,7},{7,4},{8,9},{9,10},{10,1... | collective-permute-start | bytes 49160 | tf_op jit(solution)/shard_map/ppermute | solution.py:27
  524.8 12.0 %collective-permute-start.7 = (bf16[4,1,18,128]{3,2,1,0:T(8,128)(2,1)S(1)}, bf16[4,1,18,128]{3,2,1,0:T(8,128)(2,1)S(1)}, u32[]{:S(2)}, u32[]{:S(2)}) collective-permute-start(bf16[4,1,18,128]{3,2,1,0:T(8,128)(2,1)S(1)} %get-tuple-element.162), channel_id=1, source_target_pairs={{4,0},{5,1},{6,2},{7,3},{12,8},{13,9},{14,10},{15,11},{20,16},{21,... | collective-permute-start | bytes 55304 | tf_op jit(solution)/shard_map/ppermute | solution.py:30
  526.2 15.1 %collective-permute-start.6 = (bf16[4,1,18,128]{3,2,1,0:T(8,128)(2,1)S(1)}, bf16[4,1,18,128]{3,2,1,0:T(8,128)(2,1)S(1)}, u32[]{:S(2)}, u32[]{:S(2)}) collective-permute-start(bf16[4,1,18,128]{3,2,1,0:T(8,128)(2,1)S(1)} %get-tuple-element.161), channel_id=1, source_target_pairs={{0,4},{1,5},{2,6},{3,7},{8,12},{9,13},{10,14},{11,15},{16,20},{17,... | collective-permute-start | bytes 55304 | tf_op jit(solution)/shard_map/ppermute | solution.py:27
  529.9 14.1 %collective-permute-start.47 = (bf16[4,1,18,128]{3,2,1,0:T(8,128)(2,1)S(1)}, bf16[4,1,18,128]{3,2,1,0:T(8,128)(2,1)S(1)}, u32[]{:S(2)}, u32[]{:S(2)}) collective-permute-start(bf16[4,1,18,128]{3,2,1,0:T(8,128)(2,1)S(1)} %get-tuple-element.160), channel_id=1, source_target_pairs={{4,0},{5,1},{6,2},{7,3},{12,8},{13,9},{14,10},{15,11},{20,16},{21,... | collective-permute-start | bytes 55304 | tf_op jit(solution)/shard_map/ppermute | solution.py:30
  531.2 12.8 %collective-permute-start.46 = (bf16[4,1,18,128]{3,2,1,0:T(8,128)(2,1)S(1)}, bf16[4,1,18,128]{3,2,1,0:T(8,128)(2,1)S(1)}, u32[]{:S(2)}, u32[]{:S(2)}) collective-permute-start(bf16[4,1,18,128]{3,2,1,0:T(8,128)(2,1)S(1)} %get-tuple-element.159), channel_id=1, source_target_pairs={{0,4},{1,5},{2,6},{3,7},{8,12},{9,13},{10,14},{11,15},{16,20},{17,... | collective-permute-start | bytes 55304 | tf_op jit(solution)/shard_map/ppermute | solution.py:27
  535.6 57.7 %collective-permute-start.39 = (bf16[4,1,18,128]{3,2,1,0:T(8,128)(2,1)}, bf16[4,1,18,128]{3,2,1,0:T(8,128)(2,1)}, u32[]{:S(2)}, u32[]{:S(2)}) collective-permute-start(bf16[4,1,18,128]{3,2,1,0:T(8,128)(2,1)} %get-tuple-element.158), channel_id=1, source_target_pairs={{4,0},{5,1},{6,2},{7,3},{12,8},{13,9},{14,10},{15,11},{20,16},{21,... | collective-permute-start | bytes 55304 | tf_op jit(solution)/shard_map/ppermute | solution.py:30
  536.9 56.4 %collective-permute-start.38 = (bf16[4,1,18,128]{3,2,1,0:T(8,128)(2,1)}, bf16[4,1,18,128]{3,2,1,0:T(8,128)(2,1)}, u32[]{:S(2)}, u32[]{:S(2)}) collective-permute-start(bf16[4,1,18,128]{3,2,1,0:T(8,128)(2,1)} %get-tuple-element.157), channel_id=1, source_target_pairs={{0,4},{1,5},{2,6},{3,7},{8,12},{9,13},{10,14},{11,15},{16,20},{17,... | collective-permute-start | bytes 55304 | tf_op jit(solution)/shard_map/ppermute | solution.py:27
  646.1 9.5 %collective-permute-start.25 = (bf16[4,16,1,128]{3,1,2,0:T(8,128)(2,1)S(1)}, bf16[4,16,1,128]{3,1,2,0:T(8,128)(2,1)S(1)}, u32[]{:S(2)}, u32[]{:S(2)}) collective-permute-start(bf16[4,16,1,128]{3,1,2,0:T(8,128)(2,1)S(1)} %get-tuple-element.182), channel_id=1, source_target_pairs={{1,0},{2,1},{3,2},{0,3},{5,4},{6,5},{7,6},{4,7},{9,8},{10,9},{11,1... | collective-permute-start | bytes 49160 | tf_op jit(solution)/shard_map/ppermute | solution.py:30
  649.3 6.3 collective-permute-start.24
  655.7 6.6 collective-permute-start.27
  657.0 5.3 collective-permute-start.26
  705.5 52.4 %collective-permute-start.29 = (bf16[4,16,1,128]{3,2,1,0:T(2,128)(2,1)S(1)}, bf16[4,16,1,128]{3,2,1,0:T(2,128)(2,1)S(1)}, u32[]{:S(2)}, u32[]{:S(2)}) collective-permute-start(bf16[4,16,1,128]{3,2,1,0:T(2,128)(2,1)S(1)} %get-tuple-element.180), channel_id=1, source_target_pairs={{1,0},{2,1},{3,2},{0,3},{5,4},{6,5},{7,6},{4,7},{9,8},{10,9},{11,1... | collective-permute-start | bytes 49160 | tf_op jit(solution)/shard_map/ppermute | solution.py:30
  708.0 49.9 %collective-permute-start.28 = (bf16[4,16,1,128]{3,2,1,0:T(2,128)(2,1)S(1)}, bf16[4,16,1,128]{3,2,1,0:T(2,128)(2,1)S(1)}, u32[]{:S(2)}, u32[]{:S(2)}) collective-permute-start(bf16[4,16,1,128]{3,2,1,0:T(2,128)(2,1)S(1)} %get-tuple-element.179), channel_id=1, source_target_pairs={{0,1},{1,2},{2,3},{3,0},{4,5},{5,6},{6,7},{7,4},{8,9},{9,10},{10,1... | collective-permute-start | bytes 49160 | tf_op jit(solution)/shard_map/ppermute | solution.py:27
  758.0 4.9 collective-permute-start.31
  759.3 3.9 collective-permute-start.30
  766.8 84.4 %copy-start.102 = (f32[6,32]{1,0:T(8,128)S(1)}, f32[6,32]{1,0:T(8,128)}, u32[]{:S(2)}) copy-start(f32[6,32]{1,0:T(8,128)} %param.15) | copy-start | bytes 2308
  766.8 84.4 %copy-start.122 = (f32[6,32]{1,0:T(8,128)S(1)}, f32[6,32]{1,0:T(8,128)}, u32[]{:S(2)}) copy-start(f32[6,32]{1,0:T(8,128)} %param.16) | copy-start | bytes 2308
  766.8 84.4 %copy-start.123 = (f32[6,32]{1,0:T(8,128)S(1)}, f32[6,32]{1,0:T(8,128)}, u32[]{:S(2)}) copy-start(f32[6,32]{1,0:T(8,128)} %param.17) | copy-start | bytes 2308
  766.8 85.1 %copy-start.26 = (f32[2,288,128]{2,1,0:T(8,128)S(1)}, f32[2,288,128]{2,1,0:T(8,128)}, u32[]{:S(2)}) copy-start(f32[2,288,128]{2,1,0:T(8,128)} %param.12) | copy-start | bytes 884740
  766.8 85.1 %copy-start.81 = (f32[2,288,128]{2,1,0:T(8,128)S(1)}, f32[2,288,128]{2,1,0:T(8,128)}, u32[]{:S(2)}) copy-start(f32[2,288,128]{2,1,0:T(8,128)} %param.13) | copy-start | bytes 884740
  766.8 85.1 %copy-start.82 = (f32[2,288,128]{2,1,0:T(8,128)S(1)}, f32[2,288,128]{2,1,0:T(8,128)}, u32[]{:S(2)}) copy-start(f32[2,288,128]{2,1,0:T(8,128)} %param.14) | copy-start | bytes 884740
  (165 other events, 1254.0 us)
Sparse Core Ops, SparseCore 0:
  716.1 131.4 all-reduce.12
where the time goes:
time: 872 us; the launch traced here: 862 us
  blocking collectives  505 us (58%)
  starting transfers between devices  91.7 us (11%)
  waiting for transfers between devices  87.7 us (10%)
  local copies, waits for them, and re-layouts  68.9 us (8%)
  other arithmetic  44.9 us (5%)
  matrix products  43.8 us (5%)
  between operations  20.2 us (2%)
    psum x6, blocking collectives, batch_norm(): lax.psum((jnp.sum(active, axis=(0, 1, 2)), jnp.sum(active * active, axis=...  237 us
    psum x5, blocking collectives, norm_backward(): lax.psum((jnp.sum(grad_in, axis=(0, 1, 2)), jnp.sum(grad_in * normed, axi...  199 us
    psum x1, waiting for transfers between devices, body(): lax.psum((grad_conv, grad_bias), ('dp', 'lat', 'lon'))  79.7 us
    ppermute x24, starting transfers between devices, with_halo(): lax.ppermute(lax.slice_in_dim(block, 0, width, axis=dim), axis, backward)  51.1 us
    psum x1, blocking collectives, body(): lax.psum((grad_conv, grad_bias), ('dp', 'lat', 'lon'))  41.3 us
    ppermute x24, starting transfers between devices, with_halo(): lax.ppermute(lax.slice_in_dim(block, block.shape[dim] - width, None, axis...  40.6 us
    conv_general_dilated x12, matrix products, convolve(): lax.conv_general_dilated(padded, kernel, (1, 1), 'VALID', dimension_numbe...  23 us
    unnamed x379, local copies, waits for them, and re-layouts  21.4 us
  transfers between devices with their start and end apart: 49, of which 6 were waited for; matrix products, arithmetic and copies ran while one was open for 9% of the time, Pallas kernels for 0%

commit v1 on v0

v1 whole, which is shorter than its diff:
```python
import math

import jax
import jax.numpy as jnp
from jax import lax
from jax.experimental import pallas as pl
from jax.experimental.pallas import tpu as pltpu
from jax.sharding import PartitionSpec as P

MB = 3
STEP = 5
EPS = 1e-05
CLIP = 1.0
BETA_ONE = 0.5
BETA_TWO = 0.5
RATE_CONV = 0.03
RATE_VEC = 0.3
DECAY_CONV = 0.01
ADAM_EPS = 1e-08
ALL = ("dp", "lat", "lon")
F32 = jnp.float32
BF16 = jnp.bfloat16
GELU_A = math.sqrt(2.0 / math.pi)
GELU_B = GELU_A * 0.044715

S, R, C = 12, 16, 128
TI = S * R
NH = S + 1
TH = 8 * (NH + NH % 2)
T = TI + TH
W3 = 3 * C
PER = S // MB
FLAT = 24 + 24 * S
VM = pl.BlockSpec(memory_space=pltpu.VMEM)


def call(kernel, outs, args, scratch=(), flops=0, limit=16, scalars=0):
    return pl.pallas_call(
        kernel,
        out_shape=tuple(jax.ShapeDtypeStruct(shape, kind) for shape, kind in outs),
        in_specs=[pl.BlockSpec(memory_space=pltpu.SMEM)] * scalars + [VM] * (len(args) - scalars),
        out_specs=tuple([VM] * len(outs)),
        scratch_shapes=list(scratch),
        compiler_params=pltpu.CompilerParams(vmem_limit_bytes=limit << 20),
        cost_estimate=pl.CostEstimate(
            flops=flops,
            transcendentals=0,
            bytes_accessed=sum(math.prod(a.shape) * a.dtype.itemsize for a in args),
        ),
    )(*args)


def own_row(row):
    return jnp.where(lax.axis_index("lat") == 0, row, R - 1 - row)


def own_tap(tap):
    return jnp.where(lax.axis_index("lat") == 0, tap, 2 - tap)


def act(v):
    return 0.5 * v * (1.0 + jnp.tanh(v * (GELU_A + GELU_B * (v * v))))


def act_both(v):
    sq = v * v
    tan = jnp.tanh(v * (GELU_A + GELU_B * sq))
    half = 0.5 * (1.0 + tan)
    value = v * half
    slope = half + value * (1.0 - tan) * (GELU_A + (3.0 * GELU_B) * sq)
    return value, slope


def fold(v):
    return jnp.sum(v.reshape(v.shape[0] // 8, 8, C), axis=0)


def down(v):
    return jnp.sum(v, axis=0, keepdims=True)


def batch_sums(values):
    return [fold(values[PER * R * m : PER * R * (m + 1)]) for m in range(MB)]


def build(flat, out, place, tile, side):
    for n in range(S):
        value = tile(n)
        flat[16 + 24 * n : 32 + 24 * n, :] = value
        out[place + (slice(16 * n, 16 * n + 16), slice(C, 2 * C))] = value.astype(BF16)
    whole = out.shape[-2] == T
    for p in range(TH // 16):
        pair = [side(h) if h < NH else jnp.zeros((8, C), F32) for h in (2 * p, 2 * p + 1)]
        for h, value in zip((2 * p, 2 * p + 1), pair):
            if h < NH:
                flat[8 + 24 * h : 16 + 24 * h, :] = value
        if whole:
            at = TI + 16 * p
            out[place + (slice(at, at + 16), slice(C, 2 * C))] = jnp.concatenate(pair, axis=0).astype(BF16)
    emit_sides(flat, out, place)


def emit_sides(flat, out, place):
    for kx in (0, 2):
        columns = slice(C * kx, C * kx + C)
        for n in range(S):
            at = 15 + 24 * n + kx
            out[place + (slice(16 * n, 16 * n + 16), columns)] = flat[at : at + 16, :].astype(BF16)
        if out.shape[-2] != T:
            continue
        for p in range(TH // 16):
            at = 7 + 48 * p + kx
            first = flat[at : at + 8, :]
            second = flat[at + 24 : at + 32, :] if 2 * p + 1 < NH else jnp.zeros((8, C), F32)
            out[place + (slice(TI + 16 * p, TI + 16 * p + 16), columns)] = jnp.concatenate(
                [first, second], axis=0
            ).astype(BF16)


def place_of(i, odd):
    return (i + odd, 1 - odd)


def sided(rows):
    mixed = {}
    for h in range(NH):
        low, high = max(h - 1, 0) // PER, min(h, S - 1) // PER
        if low != high:
            mixed[h] = jnp.concatenate(
                [jnp.broadcast_to(rows[low], (4, C)), jnp.broadcast_to(rows[high], (4, C))], axis=0
            )
    return (
        lambda n: rows[n // PER],
        lambda h: mixed[h] if h in mixed else rows[min(h, S - 1) // PER],
    )


def put_all(ref, rows):
    block = jnp.concatenate(rows, axis=0)
    ref[...] = jnp.broadcast_to(block[None], ref.shape)


def taken(ref, count):
    total = jnp.sum(ref[...], axis=0)
    return [total[i : i + 1] for i in range(count)]


def vec_rows(ref):
    return [ref[i : i + 1, :] for i in range(6)]


def norm_of(sums, count):
    means = [sums[m] * (1.0 / count) for m in range(MB)]
    inverses = [lax.rsqrt(sums[MB + m] * (1.0 / count) - means[m] * means[m] + EPS) for m in range(MB)]
    return means, inverses


def fill_forward(block, pieces):
    size, count = C // len(pieces), len(pieces)
    zero = jnp.zeros((C, C), BF16)
    for kx in range(3):
        block[C * kx : C * kx + C, C:] = zero
        block[C * (9 + kx) : C * (10 + kx), :C] = zero
        for ky in range(3):
            source = pl.multiple_of((3 * own_tap(ky) + kx) * size, size)
            for k, piece in enumerate(pieces):
                owner = lax.rem(lax.axis_index("dp") + (count - k), count) if count > 1 else 0
                part = piece[pl.ds(source, size), :]
                for a in range(2):
                    top = pl.multiple_of((3 * (ky + a) + kx) * C + owner * size, size)
                    block[pl.ds(top, size), a * C : a * C + C] = part


def fill_backward(block, forward):
    zero = jnp.zeros((C, C), BF16)
    for kx in range(3):
        block[C * kx : C * kx + C, C:] = zero
        block[C * (9 + kx) : C * (10 + kx), :C] = zero
        for ky in range(3):
            source = (3 * (2 - ky) + 2 - kx) * C
            part = forward[source : source + C, :C].T
            for a in range(2):
                top = (3 * (ky + a) + kx) * C
                block[top : top + C, a * C : a * C + C] = part


def conv_rows(ref, low, high, weight, rows=T):
    pairs = [
        jnp.concatenate([ref[i, 0, :rows], ref[i, 1, :rows], ref[i + 1, 0, :rows], ref[i + 1, 1, :rows]], axis=1)
        for i in range(low, high)
    ]
    got = jnp.dot(jnp.concatenate(pairs, axis=0), weight, preferred_element_type=F32)
    return [
        got[n * rows : n * rows + rows, a * C : a * C + C] for n in range(high - low) for a in range(2)
    ]


def added(total, new):
    return new if total is None else [old + more for old, more in zip(total, new)]


def prep_kernel(x, cot, weight, vectors, m1, m2, lat_out):
    size = weight.shape[1] // 9
    for t in range(9):
        m1[size * t : size * t + size, :] = weight[0, pl.ds(t, size, stride=9), :].astype(BF16)
        m2[size * t : size * t + size, :] = weight[1, pl.ds(t, size, stride=9), :].astype(BF16)
    width = vectors.shape[1]
    pick = lax.broadcasted_iota(jnp.int32, (width, C), 1) - lax.axis_index("dp") * width
    pick = jnp.where(pick == lax.broadcasted_iota(jnp.int32, (width, C), 0), 1.0, 0.0).astype(BF16)
    placed = jnp.dot(vectors[...].astype(BF16), pick, preferred_element_type=F32)
    m1[size * 9 :, :] = jnp.concatenate([placed, jnp.zeros((10, C), F32)], axis=0).astype(BF16)
    for k in range(4):
        source = own_row(R - 1 - k)
        for s in range(S):
            lat_out[k, s] = x[s, source]
            if k < 2:
                lat_out[4 + k, s] = cot[s, source]


def edge_kernel(x, cot, lat_in, x_r, x_l, c_r, c_l):
    def cut(tiles, right, left, row):
        for m in range(MB):
            four = [tiles(s).astype(F32) for s in range(PER * m, PER * m + PER)]
            right[row, m] = jnp.concatenate([v[R - 4 :] for v in four], axis=0).astype(BF16)
            left[row, m] = jnp.concatenate([v[:4] for v in four], axis=0).astype(BF16)

    @pl.loop(0, R)
    def _(row):
        source = own_row(row)
        cut(lambda s: x[s, source], x_r, x_l, row)
        cut(lambda s: cot[s, source], c_r, c_l, row)

    for k in range(4):
        cut(lambda s: lat_in[k, s], x_r, x_l, R + k)
        if k < 2:
            cut(lambda s: lat_in[4 + k, s], c_r, c_l, R + k)


def fill_sides(flat, from_left, from_right, row, scale=None):
    for m in range(MB):
        left = from_left[row, m].astype(F32)
        right = from_right[row, m].astype(F32)
        for n in range(PER):
            s = PER * m + n
            low, high = left[4 * n : 4 * n + 4], right[4 * n : 4 * n + 4]
            if scale is not None:
                low, high = low * scale[s], high * scale[s]
            flat[12 + 24 * s : 16 + 24 * s, :] = low
            flat[32 + 24 * s : 36 + 24 * s, :] = high


def shift_kernel(x, lat_in, from_left, from_right, out, *flats):
    for flat in flats:
        flat[...] = jnp.zeros(flat.shape, F32)
    for edge in (0, R + 5):
        out[edge // 2, edge % 2] = jnp.zeros((T, W3), BF16)

    def one(flat, row, tile, place):
        for n in range(S):
            value = tile(n)
            flat[16 + 24 * n : 32 + 24 * n, :] = value.astype(F32)
            out[place + (slice(16 * n, 16 * n + 16), slice(C, 2 * C))] = value
        fill_sides(flat, from_left, from_right, row)
        for p in range(TH // 16):
            at = 8 + 48 * p
            second = flat[at + 24 : at + 32, :] if 2 * p + 1 < NH else jnp.zeros((8, C), F32)
            out[place + (slice(TI + 16 * p, TI + 16 * p + 16), slice(C, 2 * C))] = jnp.concatenate(
                [flat[at : at + 8, :], second], axis=0
            ).astype(BF16)
        emit_sides(flat, out, place)

    @pl.loop(0, R // 2)
    def _(i):
        for odd in range(2):
            source = own_row(2 * i + odd)
            one(flats[odd], 2 * i + odd, lambda n: x[n, source], place_of(i, odd))

    for k in range(4):
        one(flats[k % 2], R + k, lambda n: lat_in[k, n], place_of((R + k) // 2, k % 2))


def lead_kernel(lead, cot, lat_in, from_left, from_right, dn, sums, *flats):
    scale = [0.5 * jnp.sqrt(jnp.full((1, C), lead[n], jnp.int32).astype(F32)) for n in range(S)]
    for flat in flats:
        flat[...] = jnp.zeros(flat.shape, F32)

    def one(flat, row, tile):
        values = [tile(n).astype(F32) * scale[n] for n in range(S)]
        for n in range(S):
            dn[row, 16 * n : 16 * n + 16, :] = values[n]
        fill_sides(flat, from_left, from_right, row, scale)
        for h in range(NH):
            dn[row, TI + 8 * h : TI + 8 * h + 8, :] = flat[8 + 24 * h : 16 + 24 * h, :]
        dn[row, TI + 8 * NH :, :] = jnp.zeros((TH - 8 * NH, C), F32)
        return [sum(fold(values[n]) for n in range(PER * m, PER * m + PER)) for m in range(MB)]

    def body(i, total):
        for odd in range(2):
            source = own_row(2 * i + odd)
            total = added(total, one(flats[odd], 2 * i + odd, lambda n: cot[n, source]))
        return total

    total = lax.fori_loop(0, R // 2, body, [jnp.zeros((8, C), F32)] * MB)
    for k in range(2):
        one(flats[k], R + k, lambda n: lat_in[4 + k, n])
    sums[...] = jnp.concatenate([down(v) for v in total] + [jnp.zeros((8 - MB, C), F32)], axis=0)


def block_kernel(*rest):
    pieces, (block, vec) = rest[:-2], rest[-2:]
    fill_forward(block, pieces)
    total = pieces[0][-16:, :].astype(F32)
    for piece in pieces[1:]:
        total = total + piece[-16:, :].astype(F32)
    vec[...] = total


def weight_kernel(block_one, *rest):
    pieces, (block_two, two_back, one_back) = rest[:-3], rest[-3:]
    fill_forward(block_two, pieces)
    fill_backward(two_back, block_two)
    fill_backward(one_back, block_one)


def first_kernel(x_all, block, vec, pre, sums):
    bias = vec[0:1, :]
    total = None
    for low, high in ((0, 5), (5, 10)):
        for n, v in enumerate(conv_rows(x_all, low, high, block[...])):
            row = 2 * low + n
            pre[row] = v + bias
            if row < R:
                value = act(v[:TI] + bias)
                total = added(total, batch_sums(value) + batch_sums(value * value))
    put_all(sums, [down(v) for v in total] + [jnp.zeros((2, C), F32)])


def second_kernel(count, pre, sums_in, dn, dn_sums, block, vec_in, n_all, pre_two, sums, *flats):
    vec = vec_rows(vec_in)
    means, inverses = norm_of(taken(sums_in, 2 * MB), count)
    gains = [inverses[m] * vec[1] for m in range(MB)]
    gain, gain_side = sided(gains)
    shift, shift_side = sided([vec[2] - means[m] * gains[m] for m in range(MB)])
    for flat in flats:
        flat[...] = jnp.zeros(flat.shape, F32)
    n_all[0, 0] = jnp.zeros((T, W3), BF16)

    def one(i, odd):
        row = 2 * i + odd
        build(
            flats[odd],
            n_all,
            place_of(i, odd),
            lambda n: act(pre[row, 16 * n : 16 * n + 16, :]) * gain(n) + shift(n),
            lambda h: act(pre[row, TI + 8 * h : TI + 8 * h + 8, :]) * gain_side(h) + shift_side(h),
        )

    @pl.loop(0, R // 2 + 1)
    def _(i):
        for odd in range(2):
            one(i, odd)

    one(R // 2 + 1, 0)
    total = None
    for low, high in ((0, 5), (5, 9)):
        for n, v in enumerate(conv_rows(n_all, low, high, block[...])):
            row = 2 * low + n
            pre_two[row] = v + vec[3]
            if row < R:
                value = act(v[:TI] + vec[3])
                new = batch_sums(value) + batch_sums(value * value) + batch_sums(value * dn[row, :TI, :])
                total = added(total, new)
    block_out = jnp.concatenate([down(v) for v in total] + [dn_sums[0:MB, :]], axis=0)
    for g in range(3):
        part = block_out[4 * g : 4 * g + 4]
        for n in range(sums.shape[0]):
            sums[n, g] = part


def second_stats(sums_in, count):
    total = jnp.sum(sums_in[...], axis=0)
    rows = [total[i // 4, i % 4 : i % 4 + 1, :] for i in range(4 * MB)]
    means, inverses = norm_of(rows[: 2 * MB], count)
    dots, plain = rows[2 * MB : 3 * MB], rows[3 * MB :]
    dgain = [inverses[m] * (dots[m] - means[m] * plain[m]) for m in range(MB)]
    return means, inverses, dgain, plain


def back_terms(means, inverses, gain, dgain, dshift, count):
    lin = [inverses[m] * gain for m in range(MB)]
    slope = [-lin[m] * inverses[m] * (dgain[m] * (1.0 / count)) for m in range(MB)]
    const = [-lin[m] * (dshift[m] * (1.0 / count)) - slope[m] * means[m] for m in range(MB)]
    return [sided(rows) for rows in (lin, const, slope)]


def build_back(flat, out, place, pre, incoming, row, terms):
    def at(start, size, which, index):
        value, deriv = act_both(pre[row, start : start + size, :])
        lin, const, slope = [term[which](index) for term in terms]
        return deriv * (lin * incoming[row, start : start + size, :] + const + slope * value)

    build(
        flat,
        out,
        place,
        lambda n: at(16 * n, 16, 0, n),
        lambda h: at(TI + 8 * h, 8, 1, h),
    )


def back_two_kernel(count, pre_two, dn, sums_in, pre, block, vec, grad, mid, sums, g_all, *flats):
    means, inverses, dgain, dshift = second_stats(sums_in, count)
    terms = back_terms(means, inverses, vec[4:5, :], dgain, dshift, count)
    for flat in flats:
        flat[...] = jnp.zeros(flat.shape, F32)
    for edge in (0, R + 3):
        g_all[edge // 2, edge % 2] = jnp.zeros((T, W3), BF16)

    def body(i, total):
        for odd in range(2):
            place = place_of(i, odd)
            build_back(flats[odd], g_all, place, pre_two, dn, 2 * i + odd, terms)
            own = g_all[place + (slice(0, TI), slice(C, 2 * C))]
            grad[2 * i + odd] = own
            total = total + fold(own.astype(F32))
        return total

    bias = lax.fori_loop(0, R // 2, body, jnp.zeros((8, C), F32))
    for odd in range(2):
        build_back(flats[odd], g_all, place_of(R // 2, odd), pre_two, dn, R + odd, terms)
    total = None
    for low, high in ((0, 5), (5, 9)):
        for n, v in enumerate(conv_rows(g_all, low, high, block[...])):
            row = 2 * low + n
            mid[row] = v
            if row < R:
                own = v[:TI]
                total = added(total, batch_sums(own) + batch_sums(own * act(pre[row, :TI, :])))
    put_all(sums, [down(v) for v in total] + [down(bias), jnp.zeros((1, C), F32)])


def wgrad(inner, grad, ky):
    total = None
    for low in range(0, R, 4):
        left = jnp.concatenate([grad(row) for row in range(low, low + 4)], axis=0)
        right = jnp.concatenate(
            [inner[(row + ky) // 2, (row + ky) % 2, :TI] for row in range(low, low + 4)], axis=0
        )
        part = lax.dot_general(left, right, (((0,), (0,)), ((), ())), preferred_element_type=F32)
        total = part if total is None else total + part
    return total


def split_out(ky, got, keep, send):
    lat = lax.axis_index("lat")
    for kx in range(3):
        tap = 3 * own_tap(ky) + kx
        for d in range(4):
            for half in range(2):
                start = C * kx + 32 * d + 16 * half

                def store(ref):
                    for n in range(4):
                        ref[4 * d + n, pl.ds(4 * tap, 4), :] = got[start + 4 * n : start + 4 * n + 4]

                pl.when(lat == half)(lambda: store(keep))
                pl.when(lat != half)(lambda: store(send))


def plain_out(ky, got, out):
    for kx in range(3):
        out[3 * own_tap(ky) + kx] = got[C * kx : C * kx + C, :]


def wgrad_out(split, inner, grad, outs):
    for ky in range(3):
        got = wgrad(inner, grad, ky)
        got = jnp.concatenate([got[:, C * kx : C * kx + C].T for kx in range(3)], axis=0)
        (split_out if split else plain_out)(ky, got, *outs)


def wgrad_two_kernel(split, inner, grad, *outs):
    wgrad_out(split, inner, lambda row: grad[row], outs)


def output_kernel(count, x, pre_two, sums_in, vec_in, out):
    vec = vec_rows(vec_in)
    means, inverses, _, _ = second_stats(sums_in, count)
    gains = [inverses[m] * vec[4] for m in range(MB)]
    shifts = [vec[5] - means[m] * gains[m] for m in range(MB)]

    @pl.loop(0, R)
    def _(row):
        source = own_row(row)
        for s in range(S):
            value = act(pre_two[row, 16 * s : 16 * s + 16, :])
            out[s, source] = (x[s, source].astype(F32) + value * gains[s // PER] + shifts[s // PER]).astype(BF16)


def first_back_stats(first_in, sums_in, count):
    means, inverses = norm_of(taken(first_in, 2 * MB), count)
    rows = taken(sums_in, 2 * MB + 1)
    dshift = rows[:MB]
    dgain = [inverses[m] * (rows[MB + m] - means[m] * dshift[m]) for m in range(MB)]
    return means, inverses, dgain, dshift, rows[2 * MB]


def back_one_kernel(split, count, pre, mid, first_in, sums_in, x_all, vec, g_inner, bias, *rest):
    outs, flats = rest[:-2], rest[-2:]
    means, inverses, dgain, dshift, _ = first_back_stats(first_in, sums_in, count)
    terms = back_terms(means, inverses, vec[1:2, :], dgain, dshift, count)
    for flat in flats:
        flat[...] = jnp.zeros(flat.shape, F32)
    g_inner[0, 0] = jnp.zeros((TI, W3), BF16)

    def body(i, total):
        for odd in range(2):
            place = place_of(i, odd)
            build_back(flats[odd], g_inner, place, pre, mid, 2 * i + odd, terms)
            total = total + fold(g_inner[place + (slice(None), slice(C, 2 * C))].astype(F32))
        return total

    total = lax.fori_loop(0, R // 2, body, jnp.zeros((8, C), F32))
    build_back(flats[0], g_inner, place_of(R // 2, 0), pre, mid, R, terms)
    bias[...] = jnp.concatenate([down(total), jnp.zeros((7, C), F32)], axis=0)
    wgrad_out(split, x_all, lambda row: g_inner[(row + 1) // 2, (row + 1) % 2, :, C : 2 * C], outs)


def input_grad_kernel(g_inner, dn, block, out):
    for row, v in enumerate(conv_rows(g_inner, 0, R // 2, block[...], TI)):
        source = own_row(row)
        value = v + dn[row, :TI, :]
        for n in range(S):
            out[n, source] = value[16 * n : 16 * n + 16].astype(BF16)


def merge_kernel(keep_one, got_one, keep_two, got_two, out):
    for n in range(out.shape[0]):
        out[n] = jnp.concatenate(
            [keep_one[n] + got_one[n], keep_two[n] + got_two[n], jnp.zeros((8, C), F32)], axis=0
        ).astype(BF16)


def owned_kernel(parts, bias, chunk, sums):
    total = parts[0].astype(F32)
    for n in range(1, parts.shape[0]):
        total = total + parts[n].astype(F32)
    own = total[:72]
    chunk[...] = jnp.broadcast_to(own[None], chunk.shape)
    put_all(sums, [down(fold(own * own)), bias[0:1, :]])


def adam(weight, first, second, grad, rate, decay):
    first_new = BETA_ONE * first + (1.0 - BETA_ONE) * grad
    second_new = BETA_TWO * second + (1.0 - BETA_TWO) * grad * grad
    first_hat = first_new * (1.0 / (1.0 - BETA_ONE**STEP))
    second_hat = second_new * (1.0 / (1.0 - BETA_TWO**STEP))
    weight_new = weight - rate * (first_hat / (jnp.sqrt(second_hat) + ADAM_EPS) + decay * weight)
    return weight_new, first_new, second_new


def vector_grads(first_in, second_in, third_in, bias_one, count):
    _, _, dgain_two, dshift_two = second_stats(second_in, count)
    _, _, dgain_one, dshift_one, bias_two = first_back_stats(first_in, third_in, count)
    rows = [bias_one, sum(dgain_one), sum(dshift_one), bias_two, sum(dgain_two), sum(dshift_two)]
    return jnp.concatenate(rows, axis=0)


def update_kernel(
    count,
    chunks,
    sums_in,
    first_in,
    second_in,
    third_in,
    weight,
    first,
    second,
    vectors,
    vec_first,
    vec_second,
    norm_out,
    weight_new,
    first_new,
    second_new,
    weight_low,
    vectors_new,
    vec_first_new,
    vec_second_new,
    grad,
):
    total = jnp.sum(sums_in[...], axis=0)
    vec_grad = vector_grads(first_in, second_in, third_in, total[1:2], count)
    square = jnp.sum(total[0:1], axis=1, keepdims=True) + jnp.sum(
        down(vec_grad * vec_grad), axis=1, keepdims=True
    )
    norm = jnp.sqrt(square)
    norm_out[...] = norm
    clip = jnp.minimum(1.0, CLIP / (norm + 1e-06))
    for k in range(2):
        for n in range(8):
            for t in range(9):
                part = chunks[n, 36 * k + 4 * t : 36 * k + 4 * t + 4, :]
                grad[k, pl.ds(36 * n + t, 4, stride=9), :] = part
        new = adam(weight[k], first[k], second[k], grad[k] * clip, RATE_CONV, DECAY_CONV)
        weight_new[k], first_new[k], second_new[k] = new
        weight_low[k] = new[0].astype(BF16)
    width = vectors.shape[1]
    turned = pltpu.roll(
        jnp.concatenate([vec_grad, jnp.zeros((2, C), F32)], axis=0),
        lax.rem(C - lax.axis_index("dp") * width, C),
        axis=1,
    )
    new = adam(vectors[...], vec_first[...], vec_second[...], turned[:6, :width] * clip, RATE_VEC, 0.0)
    vectors_new[...], vec_first_new[...], vec_second_new[...] = new


def spread(block, axes):
    return lax.all_to_all(block, axes, 0, 0, tiled=True)


def turn(block, axis, by):
    size = lax.axis_size(axis)
    return lax.ppermute(block, axis, [(i, (i + by) % size) for i in range(size)])


def body(inputs, lead_time, cotangent, conv_weight, conv_first, conv_second, vectors, vec_first, vec_second):
    devices = lax.axis_size("dp") * lax.axis_size("lat") * lax.axis_size("lon")
    groups = lax.axis_size("dp")
    split = groups == 4 and lax.axis_size("lon") == 4
    count = float(PER * R * R * devices)
    size = conv_weight.shape[1] // 9
    flats = [pltpu.VMEM((FLAT, C), F32)] * 2
    conv_flops = 2 * T * 12 * C * 2 * C

    m1, m2, lat_out = call(
        prep_kernel,
        [((9 * size + 16, C), BF16), ((9 * size, C), BF16), ((6, S, R, C), BF16)],
        (inputs, cotangent, conv_weight, vectors),
    )
    lat_in = turn(lat_out, "lat", 1)

    def gathered(block):
        if split:
            return [block] + [turn(block, "dp", k) for k in range(1, groups)]
        whole = lax.all_gather(block, "dp")
        taps = whole[:, : 9 * size].reshape(groups, 9, size, C).transpose(1, 0, 2, 3).reshape(9 * C, C)
        if block.shape[0] == 9 * size:
            return [taps]
        return [jnp.concatenate([taps, jnp.sum(whole[:, 9 * size :], axis=0)], axis=0)]

    w1 = gathered(m1)
    x_r, x_l, c_r, c_l = call(
        edge_kernel,
        [((R + 4, MB, 16, C), BF16)] * 2 + [((R + 2, MB, 16, C), BF16)] * 2,
        (inputs, cotangent, lat_in),
    )
    x_left, x_right = turn(x_r, "lon", 1), turn(x_l, "lon", -1)
    w2 = gathered(m2)
    c_left, c_right = turn(c_r, "lon", 1), turn(c_l, "lon", -1)
    (x_all,) = call(
        shift_kernel, [((11, 2, T, W3), BF16)], (inputs, lat_in, x_left, x_right), flats, flops=10**8
    )
    block_one, vec = call(block_kernel, [((12 * C, 2 * C), BF16), ((16, C), F32)], w1, flops=10**8)
    pre_one, sums_one = call(
        first_kernel,
        [((R + 4, T, C), F32), ((devices, 8, C), F32)],
        (x_all, block_one, vec),
        flops=conv_flops * 10,
    )
    dn, dn_sums = call(
        lead_kernel,
        [((R + 2, T, C), F32), ((8, C), F32)],
        (lead_time, cotangent, lat_in, c_left, c_right),
        flats,
        flops=10**8,
        scalars=1,
    )
    block_two, two_back, one_back = call(
        weight_kernel, [((12 * C, 2 * C), BF16)] * 3, (block_one, *w2), flops=10**8
    )
    sums_one, dn, block_two = lax.optimization_barrier((sums_one, dn, block_two))
    got_one = spread(sums_one, ALL)
    n_all, pre_two, sums_two = call(
        lambda *refs: second_kernel(count, *refs),
        [((10, 2, T, W3), BF16), ((R + 2, T, C), F32), ((devices, 3, 4, C), F32)],
        (pre_one, got_one, dn, dn_sums, block_two, vec),
        flats,
        flops=conv_flops * 9,
    )
    got_two = spread(sums_two, ALL)
    grad_two, mid, sums_three = call(
        lambda *refs: back_two_kernel(count, *refs),
        [((R, TI, C), BF16), ((R + 2, T, C), F32), ((devices, 8, C), F32)],
        (pre_two, dn, got_two, pre_one, two_back, vec),
        [pltpu.VMEM((10, 2, T, W3), BF16)] + flats,
        flops=conv_flops * 9,
    )
    got_three = spread(sums_three, ALL)
    got_three, n_all, pre_two, dn = lax.optimization_barrier((got_three, n_all, pre_two, dn))
    grad_kinds = [((16, 36, C), F32)] * 2 if split else [((9, C, C), F32)]
    two_out = call(
        lambda *refs: wgrad_two_kernel(split, *refs), grad_kinds, (n_all, grad_two), flops=conv_flops * 8
    )
    g_inner, bias_one, *one_out = call(
        lambda *refs: back_one_kernel(split, count, *refs),
        [((9, 2, TI, W3), BF16), ((8, C), F32)] + grad_kinds,
        (pre_one, mid, got_one, got_three, x_all, vec),
        flats,
        flops=conv_flops * 9,
    )
    (outputs,) = call(
        lambda *refs: output_kernel(count, *refs),
        [((S, R, R, C), BF16)],
        (inputs, pre_two, got_two, vec),
        flops=10**8,
    )
    (grad_inputs,) = call(
        input_grad_kernel,
        [((S, R, R, C), BF16)],
        (g_inner, dn, one_back),
        flops=conv_flops * 6,
    )
    if split:
        lat_one, lat_two = turn(one_out[1], "lat", 1), turn(two_out[1], "lat", 1)
        (merged,) = call(merge_kernel, [((16, 80, C), BF16)], (one_out[0], lat_one, two_out[0], lat_two))
        parts = spread(merged, ("dp", "lon"))
        chunk, sums_four = call(
            owned_kernel, [((8, 72, C), F32), ((devices, 2, C), F32)], (parts, bias_one)
        )
        got_four = spread(sums_four, ALL)
        chunks = spread(chunk, ("lat", "lon"))
        kinds = [((1, 1), F32)] + [(conv_weight.shape, F32)] * 3 + [(conv_weight.shape, BF16)]
        norm, *news = call(
            lambda *refs: update_kernel(count, *refs),
            kinds + [(vectors.shape, F32)] * 3,
            (
                chunks,
                got_four,
                got_one,
                got_two,
                got_three,
                conv_weight,
                conv_first,
                conv_second,
                vectors,
                vec_first,
                vec_second,
            ),
            [pltpu.VMEM(conv_weight.shape, F32)],
        )
        return (outputs, grad_inputs, norm.reshape(()), *news)
    stacked = jnp.stack([one_out[0], two_out[0]]).transpose(0, 2, 1, 3).reshape(2, 9 * C, C)
    conv_total, bias_total = lax.psum((stacked, bias_one[0:1]), ALL)
    vec_total = vector_grads(got_one, got_two, got_three, bias_total, count)
    grad_norm = jnp.sqrt(jnp.sum(conv_total * conv_total) + jnp.sum(vec_total * vec_total))
    clip = jnp.minimum(1.0, CLIP / (grad_norm + 1e-06))
    index = lax.axis_index("dp")
    conv_own = lax.dynamic_slice_in_dim(conv_total, index * conv_weight.shape[1], conv_weight.shape[1], 1)
    vec_own = lax.dynamic_slice_in_dim(vec_total, index * vectors.shape[1], vectors.shape[1], 1)
    conv_news = adam(conv_weight, conv_first, conv_second, conv_own * clip, RATE_CONV, DECAY_CONV)
    vec_news = adam(vectors, vec_first, vec_second, vec_own * clip, RATE_VEC, 0.0)
    return (outputs, grad_inputs, grad_norm, *conv_news, conv_news[0].astype(BF16), *vec_news)


def solution(mesh):
    grid = P("dp", "lat", "lon", None)
    rows = P(None, "dp", None)
    columns = P(None, "dp")
    in_specs = (grid, P("dp"), grid, rows, rows, rows, columns, columns, columns)
    out_specs = (grid, grid, P(), rows, rows, rows, rows, columns, columns, columns)
    return jax.shard_map(body, mesh=mesh, in_specs=in_specs, out_specs=out_specs, check_vma=False)
```

time: 872 us -> 133 us (0.15); the launches traced: 862 us -> 133 us
  blocking collectives: 505 us -> 55.8 us
  starting transfers between devices: 91.7 us -> 20.5 us
  waiting for transfers between devices: 87.7 us -> 16.7 us
  local copies, waits for them, and re-layouts: 68.9 us -> 9.13 us
  other arithmetic: 44.9 us -> 0 us
  matrix products: 43.8 us -> 0 us
  Pallas kernels: 0 us -> 29.9 us
  between operations: 20.2 us -> 0.89 us
    psum x12 -> x0, blocking collectives: 477 us -> none  [the longest x6 237 us: batch_norm(): lax.psum((jnp.sum(active, axis=(0, 1, 2)), jnp.sum(active * active, axis=...]
    psum x1 -> x0, waiting for transfers between devices: 79.7 us -> none  [body(): lax.psum((grad_conv, grad_bias), ('dp', 'lat', 'lon'))]
    ppermute x48 -> x13, starting transfers between devices: 91.7 us -> 17.1 us  [turn(): lax.ppermute(block, axis, [(i, (i + by) % size) for i in range(size)])]
    all_to_all x0 -> x5, blocking collectives: none -> 55.8 us  [spread(): return lax.all_to_all(block, axes, 0, 0, tiled=True)]
    pallas_call x0 -> x16, Pallas kernels: none -> 29.9 us  [call(): pl.pallas_call(kernel, out_shape=tuple((jax.ShapeDtypeStruct(shape, kind)...]
    all_gather x2 -> x0, blocking collectives: 27.9 us -> none  [the longest x1 15.8 us: body(): lax.all_gather(local_low[0], 'dp', axis=1, tiled=True)]
    conv_general_dilated x12 -> x0, matrix products: 23 us -> none  [convolve(): lax.conv_general_dilated(padded, kernel, (1, 1), 'VALID', dimension_numbe...]
    dot_general x54 -> x0, matrix products: 20.7 us -> none  [weight_grad(): lax.dot_general(window, grad_low, (((0, 1, 2), (0, 1, 2)), ((), ())), pre...]
  transfers between devices with their start and end apart: 49 -> 14, of which waited for: 6 -> 6; matrix products, arithmetic and copies ran while one was open for 9% -> 0% of each run, Pallas kernels for 0% -> 8%
where the time goes in v1:
time: 133 us
  blocking collectives  55.8 us (42%)
  Pallas kernels  29.9 us (22%)
  starting transfers between devices  20.5 us (15%)
  waiting for transfers between devices  16.7 us (13%)
  local copies, waits for them, and re-layouts  9.13 us (7%)
    all_to_all x5, blocking collectives, spread(): return lax.all_to_all(block, axes, 0, 0, tiled=True)  55.8 us
    pallas_call x16, Pallas kernels, call(): pl.pallas_call(kernel, out_shape=tuple((jax.ShapeDtypeStruct(shape, kind)...  29.9 us
    ppermute x13, starting transfers between devices, turn(): lax.ppermute(block, axis, [(i, (i + by) % size) for i in range(size)])  17.1 us
    ppermute x13, waiting for transfers between devices, turn(): lax.ppermute(block, axis, [(i, (i + by) % size) for i in range(size)])  16.7 us
    unnamed x38, local copies, waits for them, and re-layouts  9.13 us
    all_to_all x1, starting transfers between devices, spread(): return lax.all_to_all(block, axes, 0, 0, tiled=True)  3.42 us
  transfers between devices with their start and end apart: 14, of which 6 were waited for; matrix products, arithmetic and copies ran while one was open for 0% of the time, Pallas kernels for 8%

profile of v1, /device:TPU:0, one launch (start us, length us, event | category | flops | bytes accessed | tf_op | source)
XLA Modules:
  0.0 132.9 jit_solution(15607222061330769537)
XLA Ops:
  0.6 0.0 copy-start
  0.7 1.1 copy-done
  1.8 1.1 copy-done.6
  2.9 1.0 copy-done.10
  3.9 0.7 copy-done.14
  4.6 0.1 shard_map.168
  4.7 0.5 collective-permute-start
  5.2 4.7 %collective-permute-start.10 = (bf16[288,128]{1,0:T(8,128)(2,1)S(1)}, bf16[288,128]{1,0:T(8,128)(2,1)S(1)}, u32[]{:S(2)}, u32[]{:S(2)}) collective-permute-start(bf16[288,128]{1,0:T(8,128)(2,1)S(1)} %get-tuple-element.66.rest_0_), channel_id=1, source_target_pairs={{0,24},{8,0},{16,8},{24,16},{1,25},{9,1},{17,9},{25,17},{2,26},{10... | collective-permute-start | bytes 221192 | tf_op jit(solution)/shard_map/ppermute | solution.py:624
  9.8 0.0 collective-permute-start.3
  9.8 0.0 collective-permute-start.8
  9.8 4.4 %collective-permute-start.4 = (bf16[304,128]{1,0:T(8,128)(2,1)S(1)}, bf16[304,128]{1,0:T(8,128)(2,1)S(1)}, u32[]{:S(2)}, u32[]{:S(2)}) collective-permute-start(bf16[304,128]{1,0:T(8,128)(2,1)S(1)} %get-tuple-element.58.rest_0_), channel_id=1, source_target_pairs={{0,16},{8,24},{16,0},{24,8},{1,17},{9,25},{17,1},{25,9},{2,18},{10... | collective-permute-start | bytes 233480 | tf_op jit(solution)/shard_map/ppermute | solution.py:624
  14.2 0.0 collective-permute-done.lat_in
  14.2 0.5 shard_map.169
  14.7 1.5 %collective-permute-start.1 = (bf16[20,3,16,128]{3,2,1,0:T(8,128)(2,1)S(1)}, bf16[20,3,16,128]{3,2,1,0:T(8,128)(2,1)S(1)}, u32[]{:S(2)}, u32[]{:S(2)}) collective-permute-start(bf16[20,3,16,128]{3,2,1,0:T(8,128)(2,1)S(1)} %get-tuple-element.56), channel_id=1, source_target_pairs={{0,1},{1,2},{2,3},{3,0},{4,5},{5,6},{6,7},{7,4},{8,9},{9,10},{10,1... | collective-permute-start | bytes 737288 | tf_op jit(solution)/shard_map/ppermute | solution.py:624
  16.3 0.0 collective-permute-done.10.rest_3_
  16.3 1.4 %collective-permute-start.2 = (bf16[20,3,16,128]{3,2,1,0:T(8,128)(2,1)S(1)}, bf16[20,3,16,128]{3,2,1,0:T(8,128)(2,1)S(1)}, u32[]{:S(2)}, u32[]{:S(2)}) collective-permute-start(bf16[20,3,16,128]{3,2,1,0:T(8,128)(2,1)S(1)} %get-tuple-element.57), channel_id=1, source_target_pairs={{0,3},{1,0},{2,1},{3,2},{4,7},{5,4},{6,5},{7,6},{8,11},{9,8},{10,9... | collective-permute-start | bytes 737288 | tf_op jit(solution)/shard_map/ppermute | solution.py:624
  17.7 0.8 collective-permute-done.8.rest_1_
  18.5 1.5 %collective-permute-start.6 = (bf16[18,3,16,128]{3,2,1,0:T(8,128)(2,1)S(1)}, bf16[18,3,16,128]{3,2,1,0:T(8,128)(2,1)S(1)}, u32[]{:S(2)}, u32[]{:S(2)}) collective-permute-start(bf16[18,3,16,128]{3,2,1,0:T(8,128)(2,1)S(1)} %get-tuple-element.63), channel_id=1, source_target_pairs={{0,1},{1,2},{2,3},{3,0},{4,5},{5,6},{6,7},{7,4},{8,9},{9,10},{10,1... | collective-permute-start | bytes 663560 | tf_op jit(solution)/shard_map/ppermute | solution.py:624
  20.0 0.0 collective-permute-done.3.rest_1_
  20.0 1.4 %collective-permute-start.7 = (bf16[18,3,16,128]{3,2,1,0:T(8,128)(2,1)S(1)}, bf16[18,3,16,128]{3,2,1,0:T(8,128)(2,1)S(1)}, u32[]{:S(2)}, u32[]{:S(2)}) collective-permute-start(bf16[18,3,16,128]{3,2,1,0:T(8,128)(2,1)S(1)} %get-tuple-element.64), channel_id=1, source_target_pairs={{0,3},{1,0},{2,1},{3,2},{4,7},{5,4},{6,5},{7,6},{8,11},{9,8},{10,9... | collective-permute-start | bytes 663560 | tf_op jit(solution)/shard_map/ppermute | solution.py:624
  21.4 0.0 collective-permute-done.4.rest_2_
  21.4 1.1 collective-permute-start.5
  22.5 3.3 %collective-permute-done.5.rest_3_ = bf16[304,128]{1,0:T(8,128)(2,1)S(1)} collective-permute-done((bf16[304,128]{1,0:T(8,128)(2,1)S(1)}, bf16[304,128]{1,0:T(8,128)(2,1)S(1)}, u32[]{:S(2)}, u32[]{:S(2)}) %collective-permute-start.5) | collective-permute-done | bytes 77856 | tf_op jit(solution)/shard_map/ppermute | solution.py:624
  25.8 0.0 collective-permute-start.9
  25.8 0.1 shard_map.171
  26.0 5.9 %collective-permute-done.9.rest_2_ = bf16[288,128]{1,0:T(8,128)(2,1)S(1)} collective-permute-done((bf16[288,128]{1,0:T(8,128)(2,1)S(1)}, bf16[288,128]{1,0:T(8,128)(2,1)S(1)}, u32[]{:S(2)}, u32[]{:S(2)}) %collective-permute-start.9) | collective-permute-done | bytes 73760 | tf_op jit(solution)/shard_map/ppermute | solution.py:624
  31.9 0.4 shard_map.174
  32.2 2.4 %collective-permute-done.6.from_left = bf16[18,3,16,128]{3,2,1,0:T(8,128)(2,1)S(1)} collective-permute-done((bf16[18,3,16,128]{3,2,1,0:T(8,128)(2,1)S(1)}, bf16[18,3,16,128]{3,2,1,0:T(8,128)(2,1)S(1)}, u32[]{:S(2)}, u32[]{:S(2)}) %collective-permute-start.6) | collective-permute-done | bytes 221216 | tf_op jit(solution)/shard_map/ppermute | solution.py:624
  34.6 3.1 %collective-permute-done.7.from_right = bf16[18,3,16,128]{3,2,1,0:T(8,128)(2,1)S(1)} collective-permute-done((bf16[18,3,16,128]{3,2,1,0:T(8,128)(2,1)S(1)}, bf16[18,3,16,128]{3,2,1,0:T(8,128)(2,1)S(1)}, u32[]{:S(2)}, u32[]{:S(2)}) %collective-permute-start.7) | collective-permute-done | bytes 221216 | tf_op jit(solution)/shard_map/ppermute | solution.py:624
  37.7 0.0 copy-done.18
  37.7 1.0 shard_map.173
  38.7 0.0 collective-permute-done.1.from_left
  38.7 0.0 collective-permute-done.2.from_right
  38.7 1.0 shard_map.170.x_all.refs_4_
  39.8 3.2 %shard_map.172 = (f32[20,304,128]{2,1,0:T(8,128)S(1)}, f32[32,8,128]{2,1,0:T(8,128)S(1)}) custom-call(bf16[11,2,304,384]{3,2,1,0:T(8,128)(2,1)S(1)} %shard_map.170.x_all.refs_4_, bf16[1536,256]{1,0:T(8,128)(2,1)S(1)} %get-tuple-element.59.block.block_one, f32[16,128]{1,0:T(8,128)S(1)} %get-tuple-element.60.vec.refs_5_.refs_3_), custom_call_target="tpu_custom_call" | custom-call | flops 2390753280 | bytes 5931008 | tf_op jit(solution)/shard_map/pallas_call | solution.py:38
  42.9 10.1 %all_to_all.30.refs_1_.refs_2_ = f32[32,8,128]{2,1,0:T(8,128)S(1)} all-to-all(f32[32,8,128]{2,1,0:T(8,128)S(1)} %get-tuple-element.68), channel_id=1, replica_groups=mesh['dp'=4,'lat'=2,'lon'=4] {'dp','lat','lon'}, dimensions={0} | all-to-all | bytes 262144 | tf_op jit(solution)/shard_map/all_to_all | solution.py:619
  53.0 4.6 %shard_map.175 = (bf16[10,2,304,384]{3,2,1,0:T(8,128)(2,1)S(1)}, f32[18,304,128]{2,1,0:T(8,128)S(1)}, f32[32,3,4,128]{3,2,1,0:T(4,128)S(1)}) custom-call(f32[20,304,128]{2,1,0:T(8,128)S(1)} %get-tuple-element.61.refs_0_.refs_3_, f32[32,8,128]{2,1,0:T(8,128)S(1)} %all_to_all.30.refs_1_.refs_2_, f32[18,304,128]{2,1,0:T(8,128)S(1)} %get-tuple-element.81.refs_2_.refs_1_.dn, ...), custom_call_target="tpu_custom_call" | custom-call | flops 2151677952 | bytes 6844416 | tf_op jit(solution)/shard_map/pallas_call | solution.py:38
  57.6 11.2 %all_to_all.31.refs_2_.refs_3_ = f32[32,3,4,128]{3,2,1,0:T(4,128)S(1)} all-to-all(f32[32,3,4,128]{3,2,1,0:T(4,128)S(1)} %get-tuple-element.73), channel_id=1, replica_groups=mesh['dp'=4,'lat'=2,'lon'=4] {'dp','lat','lon'}, dimensions={0} | all-to-all | bytes 393216 | tf_op jit(solution)/shard_map/all_to_all | solution.py:619
  68.8 5.4 %shard_map.176 = (bf16[16,192,128]{2,1,0:T(8,128)(2,1)S(1)}, f32[18,304,128]{2,1,0:T(8,128)S(1)}, f32[32,8,128]{2,1,0:T(8,128)S(1)}) custom-call(f32[18,304,128]{2,1,0:T(8,128)S(1)} %get-tuple-element.77.refs_0_.refs_1_, f32[18,304,128]{2,1,0:T(8,128)S(1)} %get-tuple-element.81.refs_2_.refs_1_.dn, f32[32,3,4,128]{3,2,1,0:T(4,128)S(1)} %all_to_all.31.refs_2_.refs_3_, ...), custom_call_target="tpu_custom_call" | custom-call | flops 2151677952 | bytes 9707520 | tf_op jit(solution)/shard_map/pallas_call | solution.py:38
  74.2 10.2 %all_to_all.32.refs_3_.refs_4_ = f32[32,8,128]{2,1,0:T(8,128)S(1)} all-to-all(f32[32,8,128]{2,1,0:T(8,128)S(1)} %get-tuple-element.75), channel_id=1, replica_groups=mesh['dp'=4,'lat'=2,'lon'=4] {'dp','lat','lon'}, dimensions={0} | all-to-all | bytes 262144 | tf_op jit(solution)/shard_map/all_to_all | solution.py:619
  84.4 2.7 %shard_map.180 = (f32[16,36,128]{2,1,0:T(8,128)S(1)}, f32[16,36,128]{2,1,0:T(8,128)S(1)}) custom-call(bf16[10,2,304,384]{3,2,1,0:T(8,128)(2,1)S(1)} %get-tuple-element.85.refs_0_, bf16[16,192,128]{2,1,0:T(8,128)(2,1)S(1)} %get-tuple-element.86.refs_1_), custom_call_target="tpu_custom_call" | custom-call | flops 1912602624 | bytes 5455872 | tf_op jit(solution)/shard_map/pallas_call | solution.py:38
  87.1 0.1 collective-permute-start.12
  87.2 4.7 %shard_map.178 = (bf16[9,2,192,384]{3,2,1,0:T(8,128)(2,1)S(1)}, f32[8,128]{1,0:T(8,128)S(1)}, f32[16,36,128]{2,1,0:T(8,128)S(1)}, f32[16,36,128]{2,1,0:T(8,128)S(1)}) custom-call(f32[20,304,128]{2,1,0:T(8,128)S(1)} %get-tuple-element.61.refs_0_.refs_3_, f32[18,304,128]{2,1,0:T(8,128)S(1)} %get-tuple-element.78.refs_1_, ...), custom_call_target="tpu_custom_call" | custom-call | flops 2151677952 | bytes 11321344 | tf_op jit(solution)/shard_map/pallas_call | solution.py:38
  91.9 1.6 %copy-done.8 = bf16[9,2,192,384]{3,2,1,0:T(8,128)(2,1)} copy-done((bf16[9,2,192,384]{3,2,1,0:T(8,128)(2,1)}, bf16[9,2,192,384]{3,2,1,0:T(8,128)(2,1)S(1)}, u32[]{:S(2)}) %copy-start.8) | copy-done | bytes 2654232
  93.5 0.5 collective-permute-start.11
  94.0 0.0 collective-permute-done.12.got_two
  94.0 1.3 collective-permute-done.11.got_one
  95.2 0.1 shard_map.181
  95.3 14.6 %all_to_all.33.parts = bf16[16,80,128]{2,1,0:T(8,128)(2,1)S(1)} all-to-all(bf16[16,80,128]{2,1,0:T(8,128)(2,1)S(1)} %shard_map.181), channel_id=1, replica_groups=mesh['dp'=4,'lat'=2,'lon'=4] {'dp','lon'}, dimensions={0} | all-to-all | bytes 655360 | tf_op jit(solution)/shard_map/all_to_all | solution.py:619
  109.9 0.8 shard_map.182
  110.7 9.6 %all_to_all.34.refs_1_ = f32[32,2,128]{2,1,0:T(2,128)S(1)} all-to-all(f32[32,2,128]{2,1,0:T(2,128)S(1)} %get-tuple-element.91), channel_id=1, replica_groups=mesh['dp'=4,'lat'=2,'lon'=4] {'dp','lat','lon'}, dimensions={0} | all-to-all | bytes 65536 | tf_op jit(solution)/shard_map/all_to_all | solution.py:619
  120.3 3.4 %all-to-all-start.4 = ((f32[8,72,128]{2,1,0:T(8,128)}), f32[8,72,128]{2,1,0:T(8,128)S(1)}, u32[]{:S(2)}, u32[]{:S(2)}) async-start(f32[8,72,128]{2,1,0:T(8,128)} %get-tuple-element.90), calls=%async_computation.4 | async-start | bytes 589824 | tf_op jit(solution)/shard_map/all_to_all | solution.py:619
  123.8 1.8 %copy-done.5 = f32[18,304,128]{2,1,0:T(8,128)S(1)} copy-done((f32[18,304,128]{2,1,0:T(8,128)S(1)}, f32[18,304,128]{2,1,0:T(8,128)}, u32[]{:S(2)}) %copy-start.5) | copy-done | bytes 2801688
  125.5 1.7 %shard_map.177 = bf16[12,16,16,128]{3,2,1,0:T(8,128)(2,1)} custom-call(bf16[12,16,16,128]{3,2,1,0:T(8,128)(2,1)S(1)} %copy-done.1, f32[18,304,128]{2,1,0:T(8,128)S(1)} %copy-done.5, f32[32,3,4,128]{3,2,1,0:T(4,128)S(1)} %all_to_all.31.refs_2_.refs_3_, f32[16,128]{1,0:T(8,128)S(1)} %get-tuple-element.60.vec.refs_5_.refs_3_), custom_call_target="tpu_custom_call" | custom-call | flops 100000000 | bytes 3792896 | tf_op jit(solution)/shard_map/pallas_call | solution.py:38
  127.3 0.1 copy-done.3
  127.3 1.7 %copy-done.9 = bf16[9,2,192,384]{3,2,1,0:T(8,128)(2,1)S(1)} copy-done((bf16[9,2,192,384]{3,2,1,0:T(8,128)(2,1)S(1)}, bf16[9,2,192,384]{3,2,1,0:T(8,128)(2,1)}, u32[]{:S(2)}) %copy-start.9) | copy-done | bytes 2654232
  129.1 0.0 copy-start.16
  129.1 0.0 copy-start.17
  129.1 2.3 %shard_map.179 = bf16[12,16,16,128]{3,2,1,0:T(8,128)(2,1)} custom-call(bf16[9,2,192,384]{3,2,1,0:T(8,128)(2,1)S(1)} %copy-done.9, f32[18,304,128]{2,1,0:T(8,128)S(1)} %copy-done.3, bf16[1536,256]{1,0:T(8,128)(2,1)S(1)} %get-tuple-element.82.block), custom_call_target="tpu_custom_call" | custom-call | flops 1434451968 | bytes 6242304 | tf_op jit(solution)/shard_map/pallas_call | solution.py:38
  131.4 0.0 all-to-all-done.4.refs_0_
  131.4 0.0 copy-done.13
  131.4 0.0 copy-done.15
  131.4 0.0 copy-done.16
  131.5 1.4 %shard_map.183 = (f32[1,1]{1,0:T(1,128)}, f32[2,288,128]{2,1,0:T(8,128)}, f32[2,288,128]{2,1,0:T(8,128)}, f32[2,288,128]{2,1,0:T(8,128)}, bf16[2,288,128]{2,1,0:...) custom-call(f32[8,72,128]{2,1,0:T(8,128)S(1)} %all-to-all-done.4.refs_0_, ...), custom_call_target="tpu_custom_call" | custom-call | bytes 1673472 | tf_op jit(solution)/shard_map/pallas_call | solution.py:38
  (23 shorter events, 0.0 us)
Async XLA Ops:
  0.6 1.1 copy-start
  1.8 1.1 copy-start.6
  2.9 1.0 copy-start.10
  3.9 0.7 copy-start.14
  4.6 33.1 %copy-start.7 = (bf16[12,16,16,128]{3,2,1,0:T(8,128)(2,1)S(1)}, bf16[12,16,16,128]{3,2,1,0:T(8,128)(2,1)}, u32[]{:S(2)}) copy-start(bf16[12,16,16,128]{3,2,1,0:T(8,128)(2,1)} %cot.5) | copy-start | bytes 2359300
  4.6 33.1 %copy-start.18 = (s32[12]{0:T(128)S(1)}, s32[12]{0:T(128)}, u32[]{:S(2)}) copy-start(s32[12]{0:T(128)} %lead.1) | copy-start | bytes 148
  4.7 34.0 %copy-start.1 = (bf16[12,16,16,128]{3,2,1,0:T(8,128)(2,1)S(1)}, bf16[12,16,16,128]{3,2,1,0:T(8,128)(2,1)}, u32[]{:S(2)}) copy-start(bf16[12,16,16,128]{3,2,1,0:T(8,128)(2,1)} %refs_0_.1) | copy-start | bytes 2359300
  4.7 9.5 %collective-permute-start = (bf16[6,12,16,128]{3,2,1,0:T(8,128)(2,1)S(1)}, bf16[6,12,16,128]{3,2,1,0:T(8,128)(2,1)S(1)}, u32[]{:S(2)}, u32[]{:S(2)}) collective-permute-start(bf16[6,12,16,128]{3,2,1,0:T(8,128)(2,1)S(1)} %get-tuple-element.55), channel_id=1, source_target_pairs={{0,4},{4,0},{1,5},{5,1},{2,6},{6,2},{3,7},{7,3},{8,12},{12,8},{9,1... | collective-permute-start | bytes 884744 | tf_op jit(solution)/shard_map/ppermute | solution.py:624
  5.2 11.1 %collective-permute-start.10 = (bf16[288,128]{1,0:T(8,128)(2,1)S(1)}, bf16[288,128]{1,0:T(8,128)(2,1)S(1)}, u32[]{:S(2)}, u32[]{:S(2)}) collective-permute-start(bf16[288,128]{1,0:T(8,128)(2,1)S(1)} %get-tuple-element.66.rest_0_), channel_id=1, source_target_pairs={{0,24},{8,0},{16,8},{24,16},{1,25},{9,1},{17,9},{25,17},{2,26},{10... | collective-permute-start | bytes 221192 | tf_op jit(solution)/shard_map/ppermute | solution.py:624
  9.8 10.2 %collective-permute-start.3 = (bf16[304,128]{1,0:T(8,128)(2,1)S(1)}, bf16[304,128]{1,0:T(8,128)(2,1)S(1)}, u32[]{:S(2)}, u32[]{:S(2)}) collective-permute-start(bf16[304,128]{1,0:T(8,128)(2,1)S(1)} %get-tuple-element.58.rest_0_), channel_id=1, source_target_pairs={{0,8},{8,16},{16,24},{24,0},{1,9},{9,17},{17,25},{25,1},{2,10},{10... | collective-permute-start | bytes 233480 | tf_op jit(solution)/shard_map/ppermute | solution.py:624
  9.8 8.7 %collective-permute-start.8 = (bf16[288,128]{1,0:T(8,128)(2,1)S(1)}, bf16[288,128]{1,0:T(8,128)(2,1)S(1)}, u32[]{:S(2)}, u32[]{:S(2)}) collective-permute-start(bf16[288,128]{1,0:T(8,128)(2,1)S(1)} %get-tuple-element.66.rest_0_), channel_id=1, source_target_pairs={{0,8},{8,16},{16,24},{24,0},{1,9},{9,17},{17,25},{25,1},{2,10},{10... | collective-permute-start | bytes 221192 | tf_op jit(solution)/shard_map/ppermute | solution.py:624
  9.8 11.6 %collective-permute-start.4 = (bf16[304,128]{1,0:T(8,128)(2,1)S(1)}, bf16[304,128]{1,0:T(8,128)(2,1)S(1)}, u32[]{:S(2)}, u32[]{:S(2)}) collective-permute-start(bf16[304,128]{1,0:T(8,128)(2,1)S(1)} %get-tuple-element.58.rest_0_), channel_id=1, source_target_pairs={{0,16},{8,24},{16,0},{24,8},{1,17},{9,25},{17,1},{25,9},{2,18},{10... | collective-permute-start | bytes 233480 | tf_op jit(solution)/shard_map/ppermute | solution.py:624
  14.7 24.0 %collective-permute-start.1 = (bf16[20,3,16,128]{3,2,1,0:T(8,128)(2,1)S(1)}, bf16[20,3,16,128]{3,2,1,0:T(8,128)(2,1)S(1)}, u32[]{:S(2)}, u32[]{:S(2)}) collective-permute-start(bf16[20,3,16,128]{3,2,1,0:T(8,128)(2,1)S(1)} %get-tuple-element.56), channel_id=1, source_target_pairs={{0,1},{1,2},{2,3},{3,0},{4,5},{5,6},{6,7},{7,4},{8,9},{9,10},{10,1... | collective-permute-start | bytes 737288 | tf_op jit(solution)/shard_map/ppermute | solution.py:624
  16.3 22.4 %collective-permute-start.2 = (bf16[20,3,16,128]{3,2,1,0:T(8,128)(2,1)S(1)}, bf16[20,3,16,128]{3,2,1,0:T(8,128)(2,1)S(1)}, u32[]{:S(2)}, u32[]{:S(2)}) collective-permute-start(bf16[20,3,16,128]{3,2,1,0:T(8,128)(2,1)S(1)} %get-tuple-element.57), channel_id=1, source_target_pairs={{0,3},{1,0},{2,1},{3,2},{4,7},{5,4},{6,5},{7,6},{8,11},{9,8},{10,9... | collective-permute-start | bytes 737288 | tf_op jit(solution)/shard_map/ppermute | solution.py:624
  18.5 16.1 %collective-permute-start.6 = (bf16[18,3,16,128]{3,2,1,0:T(8,128)(2,1)S(1)}, bf16[18,3,16,128]{3,2,1,0:T(8,128)(2,1)S(1)}, u32[]{:S(2)}, u32[]{:S(2)}) collective-permute-start(bf16[18,3,16,128]{3,2,1,0:T(8,128)(2,1)S(1)} %get-tuple-element.63), channel_id=1, source_target_pairs={{0,1},{1,2},{2,3},{3,0},{4,5},{5,6},{6,7},{7,4},{8,9},{9,10},{10,1... | collective-permute-start | bytes 663560 | tf_op jit(solution)/shard_map/ppermute | solution.py:624
  20.0 17.7 %collective-permute-start.7 = (bf16[18,3,16,128]{3,2,1,0:T(8,128)(2,1)S(1)}, bf16[18,3,16,128]{3,2,1,0:T(8,128)(2,1)S(1)}, u32[]{:S(2)}, u32[]{:S(2)}) collective-permute-start(bf16[18,3,16,128]{3,2,1,0:T(8,128)(2,1)S(1)} %get-tuple-element.64), channel_id=1, source_target_pairs={{0,3},{1,0},{2,1},{3,2},{4,7},{5,4},{6,5},{7,6},{8,11},{9,8},{10,9... | collective-permute-start | bytes 663560 | tf_op jit(solution)/shard_map/ppermute | solution.py:624
  21.4 4.4 %collective-permute-start.5 = (bf16[304,128]{1,0:T(8,128)(2,1)S(1)}, bf16[304,128]{1,0:T(8,128)(2,1)S(1)}, u32[]{:S(2)}, u32[]{:S(2)}) collective-permute-start(bf16[304,128]{1,0:T(8,128)(2,1)S(1)} %get-tuple-element.58.rest_0_), channel_id=1, source_target_pairs={{0,24},{8,0},{16,8},{24,16},{1,25},{9,1},{17,9},{25,17},{2,26},{10... | collective-permute-start | bytes 233480 | tf_op jit(solution)/shard_map/ppermute | solution.py:624
  25.8 6.0 %collective-permute-start.9 = (bf16[288,128]{1,0:T(8,128)(2,1)S(1)}, bf16[288,128]{1,0:T(8,128)(2,1)S(1)}, u32[]{:S(2)}, u32[]{:S(2)}) collective-permute-start(bf16[288,128]{1,0:T(8,128)(2,1)S(1)} %get-tuple-element.66.rest_0_), channel_id=1, source_target_pairs={{0,16},{8,24},{16,0},{24,8},{1,17},{9,25},{17,1},{25,9},{2,18},{10... | collective-permute-start | bytes 221192 | tf_op jit(solution)/shard_map/ppermute | solution.py:624
  38.7 30.1 %copy-start.2 = (f32[18,304,128]{2,1,0:T(8,128)}, f32[18,304,128]{2,1,0:T(8,128)S(1)}, u32[]{:S(2)}) copy-start(f32[18,304,128]{2,1,0:T(8,128)S(1)} %get-tuple-element.81.refs_2_.refs_1_.dn) | copy-start | bytes 8404996
  57.6 16.6 %copy-start.4 = (f32[18,304,128]{2,1,0:T(8,128)}, f32[18,304,128]{2,1,0:T(8,128)S(1)}, u32[]{:S(2)}) copy-start(f32[18,304,128]{2,1,0:T(8,128)S(1)} %get-tuple-element.77.refs_0_.refs_1_) | copy-start | bytes 8404996
  87.1 6.9 %collective-permute-start.12 = (f32[16,36,128]{2,1,0:T(8,128)S(1)}, f32[16,36,128]{2,1,0:T(8,128)S(1)}, u32[]{:S(2)}, u32[]{:S(2)}) collective-permute-start(f32[16,36,128]{2,1,0:T(8,128)S(1)} %get-tuple-element.88), channel_id=1, source_target_pairs={{0,4},{4,0},{1,5},{5,1},{2,6},{6,2},{3,7},{7,3},{8,12},{12,8},{9,1... | collective-permute-start | bytes 884744 | tf_op jit(solution)/shard_map/ppermute | solution.py:624
  91.9 1.6 %copy-start.8 = (bf16[9,2,192,384]{3,2,1,0:T(8,128)(2,1)}, bf16[9,2,192,384]{3,2,1,0:T(8,128)(2,1)S(1)}, u32[]{:S(2)}) copy-start(bf16[9,2,192,384]{3,2,1,0:T(8,128)(2,1)S(1)} %get-tuple-element.80.g_inner) | copy-start | bytes 7962628
  93.5 1.7 %collective-permute-start.11 = (f32[16,36,128]{2,1,0:T(8,128)S(1)}, f32[16,36,128]{2,1,0:T(8,128)S(1)}, u32[]{:S(2)}, u32[]{:S(2)}) collective-permute-start(f32[16,36,128]{2,1,0:T(8,128)S(1)} %get-tuple-element.84), channel_id=1, source_target_pairs={{0,4},{4,0},{1,5},{5,1},{2,6},{6,2},{3,7},{7,3},{8,12},{12,8},{9,1... | collective-permute-start | bytes 884744 | tf_op jit(solution)/shard_map/ppermute | solution.py:624
  120.3 11.1 %all-to-all-start.4 = ((f32[8,72,128]{2,1,0:T(8,128)}), f32[8,72,128]{2,1,0:T(8,128)S(1)}, u32[]{:S(2)}, u32[]{:S(2)}) async-start(f32[8,72,128]{2,1,0:T(8,128)} %get-tuple-element.90), calls=%async_computation.4 | async-start | bytes 589824 | tf_op jit(solution)/shard_map/all_to_all | solution.py:619
  123.8 1.8 %copy-start.5 = (f32[18,304,128]{2,1,0:T(8,128)S(1)}, f32[18,304,128]{2,1,0:T(8,128)}, u32[]{:S(2)}) copy-start(f32[18,304,128]{2,1,0:T(8,128)} %copy-done.4) | copy-start | bytes 8404996
  125.5 1.8 %copy-start.3 = (f32[18,304,128]{2,1,0:T(8,128)S(1)}, f32[18,304,128]{2,1,0:T(8,128)}, u32[]{:S(2)}) copy-start(f32[18,304,128]{2,1,0:T(8,128)} %copy-done.2) | copy-start | bytes 8404996
  127.3 1.7 %copy-start.9 = (bf16[9,2,192,384]{3,2,1,0:T(8,128)(2,1)S(1)}, bf16[9,2,192,384]{3,2,1,0:T(8,128)(2,1)}, u32[]{:S(2)}) copy-start(bf16[9,2,192,384]{3,2,1,0:T(8,128)(2,1)} %copy-done.8) | copy-start | bytes 7962628
  129.1 2.3 %copy-start.11 = (f32[2,288,128]{2,1,0:T(8,128)S(1)}, f32[2,288,128]{2,1,0:T(8,128)}, u32[]{:S(2)}) copy-start(f32[2,288,128]{2,1,0:T(8,128)} %refs_5_.1) | copy-start | bytes 884740
  129.1 2.3 %copy-start.12 = (f32[2,288,128]{2,1,0:T(8,128)S(1)}, f32[2,288,128]{2,1,0:T(8,128)}, u32[]{:S(2)}) copy-start(f32[2,288,128]{2,1,0:T(8,128)} %refs_6_.1) | copy-start | bytes 884740
  129.1 2.3 %copy-start.13 = (f32[2,288,128]{2,1,0:T(8,128)S(1)}, f32[2,288,128]{2,1,0:T(8,128)}, u32[]{:S(2)}) copy-start(f32[2,288,128]{2,1,0:T(8,128)} %refs_7_.1) | copy-start | bytes 884740
  129.1 2.3 %copy-start.15 = (f32[6,32]{1,0:T(8,128)S(1)}, f32[6,32]{1,0:T(8,128)}, u32[]{:S(2)}) copy-start(f32[6,32]{1,0:T(8,128)} %refs_8_.1) | copy-start | bytes 2308
  129.1 2.3 %copy-start.16 = (f32[6,32]{1,0:T(8,128)S(1)}, f32[6,32]{1,0:T(8,128)}, u32[]{:S(2)}) copy-start(f32[6,32]{1,0:T(8,128)} %refs_9_.1) | copy-start | bytes 2308
  129.1 2.3 %copy-start.17 = (f32[6,32]{1,0:T(8,128)S(1)}, f32[6,32]{1,0:T(8,128)}, u32[]{:S(2)}) copy-start(f32[6,32]{1,0:T(8,128)} %refs_10_.1) | copy-start | bytes 2308

commit v2 on v1

v2 whole, which is shorter than its diff:
```python
import math

import jax
import jax.numpy as jnp
from jax import lax
from jax.experimental import pallas as pl
from jax.experimental.pallas import tpu as pltpu
from jax.sharding import PartitionSpec as P

MB = 3
STEP = 5
EPS = 1e-05
CLIP = 1.0
BETA_ONE = 0.5
BETA_TWO = 0.5
RATE_CONV = 0.03
RATE_VEC = 0.3
DECAY_CONV = 0.01
ADAM_EPS = 1e-08
ALL = ("dp", "lat", "lon")
F32 = jnp.float32
BF16 = jnp.bfloat16
GELU_A = math.sqrt(2.0 / math.pi)
GELU_B = GELU_A * 0.044715

S, R, C = 12, 16, 128
TI = S * R
NH = S + 1
TH = 8 * (NH + NH % 2)
T = TI + TH
W3 = 3 * C
PER = S // MB
FLAT = 24 + 24 * S
VM = pl.BlockSpec(memory_space=pltpu.VMEM)
SM = pl.BlockSpec(memory_space=pltpu.SMEM)
FAR = pl.BlockSpec(memory_space=pltpu.HBM)


def call(kernel, outs, args, scratch=(), flops=0, limit=16, scalars=0, far=0, far_out=(), aliases=None):
    args = [
        pltpu.with_memory_space_constraint(arg, pltpu.HBM) if scalars <= n < scalars + far else arg
        for n, arg in enumerate(args)
    ]
    spaces = [SM] * scalars + [FAR] * far + [VM] * (len(args) - scalars - far)
    return pl.pallas_call(
        kernel,
        out_shape=tuple(
            pltpu.HBM(shape, kind) if n in far_out else jax.ShapeDtypeStruct(shape, kind)
            for n, (shape, kind) in enumerate(outs)
        ),
        in_specs=spaces,
        out_specs=tuple(FAR if n in far_out else VM for n in range(len(outs))),
        scratch_shapes=list(scratch),
        input_output_aliases=aliases or {},
        compiler_params=pltpu.CompilerParams(vmem_limit_bytes=limit << 20),
        cost_estimate=pl.CostEstimate(
            flops=flops,
            transcendentals=0,
            bytes_accessed=sum(math.prod(a.shape) * a.dtype.itemsize for a in args),
        ),
    )(*args)


def own_row(row):
    return jnp.where(lax.axis_index("lat") == 0, row, R - 1 - row)


def own_tap(tap):
    return jnp.where(lax.axis_index("lat") == 0, tap, 2 - tap)


def act(v):
    return 0.5 * v * (1.0 + jnp.tanh(v * (GELU_A + GELU_B * (v * v))))


def act_both(v):
    sq = v * v
    tan = jnp.tanh(v * (GELU_A + GELU_B * sq))
    half = 0.5 * (1.0 + tan)
    value = v * half
    slope = half + value * (1.0 - tan) * (GELU_A + (3.0 * GELU_B) * sq)
    return value, slope


def fold(v):
    return jnp.sum(v.reshape(v.shape[0] // 8, 8, C), axis=0)


def down(v):
    return jnp.sum(v, axis=0, keepdims=True)


def batch_sums(values):
    return [fold(values[PER * R * m : PER * R * (m + 1)]) for m in range(MB)]


def build(flat, out, place, tile, side):
    for n in range(S):
        value = tile(n)
        flat[16 + 24 * n : 32 + 24 * n, :] = value
        out[place + (slice(16 * n, 16 * n + 16), slice(C, 2 * C))] = value.astype(BF16)
    whole = out.shape[-2] == T
    for p in range(TH // 16):
        pair = [side(h) if h < NH else jnp.zeros((8, C), F32) for h in (2 * p, 2 * p + 1)]
        for h, value in zip((2 * p, 2 * p + 1), pair):
            if h < NH:
                flat[8 + 24 * h : 16 + 24 * h, :] = value
        if whole:
            at = TI + 16 * p
            out[place + (slice(at, at + 16), slice(C, 2 * C))] = jnp.concatenate(pair, axis=0).astype(BF16)
    emit_sides(flat, out, place)


def emit_sides(flat, out, place):
    for kx in (0, 2):
        columns = slice(C * kx, C * kx + C)
        for n in range(S):
            at = 15 + 24 * n + kx
            out[place + (slice(16 * n, 16 * n + 16), columns)] = flat[at : at + 16, :].astype(BF16)
        if out.shape[-2] != T:
            continue
        for p in range(TH // 16):
            at = 7 + 48 * p + kx
            first = flat[at : at + 8, :]
            second = flat[at + 24 : at + 32, :] if 2 * p + 1 < NH else jnp.zeros((8, C), F32)
            out[place + (slice(TI + 16 * p, TI + 16 * p + 16), columns)] = jnp.concatenate(
                [first, second], axis=0
            ).astype(BF16)


def place_of(i, odd):
    return (i + odd, 1 - odd)


def sided(rows):
    mixed = {}
    for h in range(NH):
        low, high = max(h - 1, 0) // PER, min(h, S - 1) // PER
        if low != high:
            mixed[h] = jnp.concatenate(
                [jnp.broadcast_to(rows[low], (4, C)), jnp.broadcast_to(rows[high], (4, C))], axis=0
            )
    return (
        lambda n: rows[n // PER],
        lambda h: mixed[h] if h in mixed else rows[min(h, S - 1) // PER],
    )


def put_all(ref, rows):
    block = jnp.concatenate(rows, axis=0)
    ref[...] = jnp.broadcast_to(block[None], ref.shape)


def taken(ref, count):
    return [ref[i : i + 1, :] for i in range(count)]


def vec_rows(ref):
    return [ref[i : i + 1, :] for i in range(6)]


def norm_of(sums, count):
    means = [sums[m] * (1.0 / count) for m in range(MB)]
    inverses = [lax.rsqrt(sums[MB + m] * (1.0 / count) - means[m] * means[m] + EPS) for m in range(MB)]
    return means, inverses


def piece_of(pieces, k, which, rows):
    if k == 0:
        return pieces[0][which, rows, :]
    mine, other = pieces[2 * k - 1], pieces[2 * k]
    return jnp.where(lax.axis_index("lat") == which, mine[rows, :], other[rows, :])


def fill_forward(block, pieces, which):
    count = (len(pieces) + 1) // 2
    size = C // count
    zero = jnp.zeros((C, C), BF16)
    for kx in range(3):
        block[C * kx : C * kx + C, C:] = zero
        block[C * (9 + kx) : C * (10 + kx), :C] = zero
        for ky in range(3):
            source = pl.multiple_of((3 * own_tap(ky) + kx) * size, size)
            for k in range(count):
                owner = lax.rem(lax.axis_index("dp") + (count - k), count) if count > 1 else 0
                part = piece_of(pieces, k, which, pl.ds(source, size))
                for a in range(2):
                    top = pl.multiple_of((3 * (ky + a) + kx) * C + owner * size, size)
                    block[pl.ds(top, size), a * C : a * C + C] = part


def fill_backward(block, forward):
    zero = jnp.zeros((C, C), BF16)
    for kx in range(3):
        block[C * kx : C * kx + C, C:] = zero
        block[C * (9 + kx) : C * (10 + kx), :C] = zero
        for ky in range(3):
            source = (3 * (2 - ky) + 2 - kx) * C
            part = forward[source : source + C, :C].T
            for a in range(2):
                top = (3 * (ky + a) + kx) * C
                block[top : top + C, a * C : a * C + C] = part


def conv_rows(ref, low, high, weight, rows=T):
    pairs = [
        jnp.concatenate([ref[i, 0, :rows], ref[i, 1, :rows], ref[i + 1, 0, :rows], ref[i + 1, 1, :rows]], axis=1)
        for i in range(low, high)
    ]
    got = jnp.dot(jnp.concatenate(pairs, axis=0), weight, preferred_element_type=F32)
    return [
        got[n * rows : n * rows + rows, a * C : a * C + C] for n in range(high - low) for a in range(2)
    ]


def added(total, new):
    return new if total is None else [old + more for old, more in zip(total, new)]


def pack_taps(weight, out):
    size = weight.shape[0] // 9
    for t in range(9):
        out[size * t : size * t + size, :] = weight[pl.ds(t, size, stride=9), :].astype(BF16)


def prep_kernel(x, cot, weight, vectors, packed, lat_out, x_near, cot_near, held, held_vec, sems):
    last = lax.axis_index("lat") == 0
    copies = [
        pltpu.make_async_copy(weight, held, sems.at[0]),
        pltpu.make_async_copy(vectors, held_vec, sems.at[1]),
        pltpu.make_async_copy(x.at[:, pl.ds(jnp.where(last, R - 4, 0), 4)], lat_out.at[:, 0:4], sems.at[2]),
        pltpu.make_async_copy(cot.at[:, pl.ds(jnp.where(last, R - 2, 0), 2)], lat_out.at[:, 4:6], sems.at[3]),
        pltpu.make_async_copy(x, x_near, sems.at[4]),
        pltpu.make_async_copy(cot, cot_near, sems.at[5]),
    ]
    for copy in copies:
        copy.start()
    for copy in copies[:2]:
        copy.wait()
    size = 9 * (weight.shape[1] // 9)
    width = vectors.shape[1]
    pick = lax.broadcasted_iota(jnp.int32, (width, C), 1) - lax.axis_index("dp") * width
    pick = jnp.where(pick == lax.broadcasted_iota(jnp.int32, (width, C), 0), 1.0, 0.0).astype(BF16)
    placed = jnp.dot(held_vec[...].astype(BF16), pick, preferred_element_type=F32)
    for k in range(2):
        pack_taps(held.at[k], packed.at[k])
        packed[k, size:, :] = jnp.concatenate([placed, jnp.zeros((10, C), F32)], axis=0).astype(BF16)
    for copy in copies[2:]:
        copy.wait()


def x_beyond(lat_in, n, k):
    return lat_in[n, jnp.where(lax.axis_index("lat") == 0, k, 3 - k)]


def cot_beyond(lat_in, n, k):
    return lat_in[n, jnp.where(lax.axis_index("lat") == 0, 4 + k, 5 - k)]


def cut_far(tile, far_r, far_l, at, columns, rows):
    for m in range(MB):
        tiles = [tile(q, n).astype(F32) for q in range(rows) for n in range(PER * m, PER * m + PER)]
        far_r[at, m] = jnp.concatenate([v[R - columns :] for v in tiles], axis=0).astype(BF16)
        far_l[at, m] = jnp.concatenate([v[:columns] for v in tiles], axis=0).astype(BF16)


def edge_kernel(x, far_r, far_l):
    @pl.loop(0, R // 2)
    def _(i):
        for q in range(2):
            cut_far(lambda _, n: x[n, own_row(2 * i + q)], far_r, far_l, 2 * i + q, 4, 1)


def beyond_kernel(lat_in, packed, right_in, left_in, mine, far_r, far_l):
    for k in range(4):
        cut_far(lambda _, n: x_beyond(lat_in, n, k), far_r, far_l, R + k, 4, 1)
    mine[...] = packed[lax.axis_index("lat")]


def later_kernel(after, cot, lat_in, far_r, far_l):
    @pl.loop(0, R // 2)
    def _(i):
        cut_far(lambda q, n: cot[n, own_row(2 * i + q)], far_r, far_l, i, 2, 2)

    cut_far(lambda q, n: cot_beyond(lat_in, n, q), far_r, far_l, R // 2, 2, 2)


def shift_kernel(x, lat_in, from_left, from_right, out, *flats):
    for edge in (0, R + 5):
        out[edge // 2, edge % 2] = jnp.zeros((TI, W3), BF16)

    def one(flat, tile, at, place):
        for m in range(MB):
            left, right = from_left[at, m].astype(F32), from_right[at, m].astype(F32)
            for n in range(PER):
                s = PER * m + n
                flat[15 + 24 * s : 16 + 24 * s, :] = left[4 * n + 3 : 4 * n + 4]
                flat[32 + 24 * s : 33 + 24 * s, :] = right[4 * n : 4 * n + 1]
        for n in range(S):
            value = tile(n)
            flat[16 + 24 * n : 32 + 24 * n, :] = value.astype(F32)
            out[place + (slice(16 * n, 16 * n + 16), slice(C, 2 * C))] = value
        emit_sides(flat, out, place)

    @pl.loop(0, R // 2)
    def _(i):
        for odd in range(2):
            source = own_row(2 * i + odd)
            one(flats[odd], lambda n: x[n, source], 2 * i + odd, place_of(i, odd))

    for k in range(4):
        one(flats[k % 2], lambda n: x_beyond(lat_in, n, k), R + k, place_of((R + k) // 2, k % 2))


def halo_kernel(after, x, lat_in, from_left, from_right, block, vec, pre, halo, *flats):
    for flat in flats:
        flat[...] = jnp.zeros(flat.shape, F32)
    for edge in (0, R + 5):
        halo[edge // 2, edge % 2] = jnp.zeros((TH, W3), BF16)

    def one(flat, tile, row, place):
        for m in range(MB):
            left, right = from_left[row, m].astype(F32), from_right[row, m].astype(F32)
            for n in range(PER):
                s = PER * m + n
                value = tile(s).astype(F32)
                flat[12 + 24 * s : 16 + 24 * s, :] = left[4 * n : 4 * n + 4]
                flat[16 + 24 * s : 24 + 24 * s, :] = value[:8]
                flat[24 + 24 * s : 32 + 24 * s, :] = value[8:]
                flat[32 + 24 * s : 36 + 24 * s, :] = right[4 * n : 4 * n + 4]
        for kx in range(3):
            for p in range(TH // 16):
                at = 7 + 48 * p + kx
                second = flat[at + 24 : at + 32, :] if 2 * p + 1 < NH else jnp.zeros((8, C), F32)
                halo[place + (slice(16 * p, 16 * p + 16), slice(C * kx, C * kx + C))] = jnp.concatenate(
                    [flat[at : at + 8, :], second], axis=0
                ).astype(BF16)

    @pl.loop(0, R // 2)
    def _(i):
        for odd in range(2):
            source = own_row(2 * i + odd)
            one(flats[odd], lambda n: x[n, source], 2 * i + odd, place_of(i, odd))

    for k in range(4):
        one(flats[k % 2], lambda n: x_beyond(lat_in, n, k), R + k, place_of((R + k) // 2, k % 2))
    for row, v in enumerate(conv_rows(halo, 0, R // 2 + 2, block[...], TH)):
        pre[row] = v + vec[0:1, :]


def lead_scales(lead):
    return [0.5 * jnp.sqrt(jnp.full((1, C), lead[n], jnp.int32).astype(F32)) for n in range(S)]


def lead_kernel(lead, cot, dn, sums):
    scale = lead_scales(lead)

    def body(i, total):
        for odd in range(2):
            row = 2 * i + odd
            source = own_row(row)
            values = [cot[n, source].astype(F32) * scale[n] for n in range(S)]
            for n in range(S):
                dn[row, 16 * n : 16 * n + 16, :] = values[n]
            new = [sum(fold(values[n]) for n in range(PER * m, PER * m + PER)) for m in range(MB)]
            total = added(total, new)
        return total

    total = lax.fori_loop(0, R // 2, body, [jnp.zeros((8, C), F32)] * MB)
    sums[...] = jnp.concatenate([down(v) for v in total] + [jnp.zeros((8 - MB, C), F32)], axis=0)


def lead_side_kernel(lead, after, lat_in, from_left, from_right, lat, side, *flats):
    scale = lead_scales(lead)
    for flat in flats:
        flat[...] = jnp.zeros(flat.shape, F32)
    for k in range(2):
        for n in range(S):
            lat[k, 16 * n : 16 * n + 16, :] = cot_beyond(lat_in, n, k).astype(F32) * scale[n]

    @pl.loop(0, R // 2 + 1)
    def _(i):
        for m in range(MB):
            left = from_left[i, m].astype(F32)
            right = from_right[i, m].astype(F32)
            for odd in range(2):
                for n in range(PER):
                    s, at = PER * m + n, 8 * odd + 2 * n
                    flats[odd][14 + 24 * s : 16 + 24 * s, :] = left[at : at + 2] * scale[s]
                    flats[odd][32 + 24 * s : 34 + 24 * s, :] = right[at : at + 2] * scale[s]
        for odd in range(2):
            row = 2 * i + odd
            flat = flats[odd]
            for h in range(NH):
                side[row, 8 * h : 8 * h + 8, :] = flat[8 + 24 * h : 16 + 24 * h, :]
            side[row, 8 * NH :, :] = jnp.zeros((TH - 8 * NH, C), F32)


def block_kernel(*rest):
    pieces, (block, vec) = rest[:-2], rest[-2:]
    fill_forward(block, pieces, 0)
    last = pieces[0].shape[1]
    vec[...] = sum(
        piece_of(pieces, k, 0, slice(last - 16, last)).astype(F32) for k in range((len(pieces) + 1) // 2)
    )


def weight_kernel(after, block_one, *rest):
    pieces, (block_two, two_back, one_far, one_back, sem) = rest[:-5], rest[-5:]
    fill_backward(one_back, block_one)
    copy = pltpu.make_async_copy(one_back, one_far, sem)
    copy.start()
    fill_forward(block_two, pieces, 1)
    fill_backward(two_back, block_two)
    copy.wait()


def first_kernel(x_all, block, vec, pre, sums):
    bias = vec[0:1, :]
    total = None
    for low, high in ((0, 4), (4, 8), (8, 10)):
        for n, v in enumerate(conv_rows(x_all, low, high, block[...], TI)):
            row = 2 * low + n
            pre[row] = v + bias
            if row < R:
                value = act(v + bias)
                total = added(total, batch_sums(value) + batch_sums(value * value))
    put_all(sums, [down(v) for v in total] + [jnp.zeros((2, C), F32)])


def second_kernel(count, pre, pre_side, sums_in, dn, dn_sums, block, vec_in, n_all, pre_two, sums, kept, *flats):
    vec = vec_rows(vec_in)
    kept[...] = jnp.sum(sums_in[...], axis=0)
    means, inverses = norm_of(taken(kept, 2 * MB), count)
    gains = [inverses[m] * vec[1] for m in range(MB)]
    gain, gain_side = sided(gains)
    shift, shift_side = sided([vec[2] - means[m] * gains[m] for m in range(MB)])
    for flat in flats:
        flat[...] = jnp.zeros(flat.shape, F32)
    n_all[0, 0] = jnp.zeros((T, W3), BF16)

    def one(i, odd):
        row = 2 * i + odd
        build(
            flats[odd],
            n_all,
            place_of(i, odd),
            lambda n: act(pre[row, 16 * n : 16 * n + 16, :]) * gain(n) + shift(n),
            lambda h: act(pre_side[row, 8 * h : 8 * h + 8, :]) * gain_side(h) + shift_side(h),
        )

    @pl.loop(0, R // 2 + 1)
    def _(i):
        for odd in range(2):
            one(i, odd)

    one(R // 2 + 1, 0)
    total = None
    for low, high in ((0, 5), (5, 9)):
        for n, v in enumerate(conv_rows(n_all, low, high, block[...])):
            row = 2 * low + n
            pre_two[row] = v + vec[3]
            if row < R:
                value = act(v[:TI] + vec[3])
                new = batch_sums(value) + batch_sums(value * value) + batch_sums(value * dn[row])
                total = added(total, new)
    block_out = jnp.concatenate([down(v) for v in total] + [dn_sums[0:MB, :]], axis=0)
    for g in range(3):
        part = block_out[4 * g : 4 * g + 4]
        for n in range(sums.shape[0]):
            sums[n, g] = part


def second_stats(sums_in, count):
    rows = taken(sums_in, 4 * MB)
    means, inverses = norm_of(rows[: 2 * MB], count)
    dots, plain = rows[2 * MB : 3 * MB], rows[3 * MB :]
    dgain = [inverses[m] * (dots[m] - means[m] * plain[m]) for m in range(MB)]
    return means, inverses, dgain, plain


def back_terms(means, inverses, gain, dgain, dshift, count):
    lin = [inverses[m] * gain for m in range(MB)]
    slope = [-lin[m] * inverses[m] * (dgain[m] * (1.0 / count)) for m in range(MB)]
    const = [-lin[m] * (dshift[m] * (1.0 / count)) - slope[m] * means[m] for m in range(MB)]
    return [sided(rows) for rows in (lin, const, slope)]


def build_back(flat, out, place, terms, pre_tile, tile, pre_side, side):
    def at(pre, incoming, which, index):
        value, deriv = act_both(pre(index))
        lin, const, slope = [term[which](index) for term in terms]
        return deriv * (lin * incoming(index) + const + slope * value)

    build(flat, out, place, lambda n: at(pre_tile, tile, 0, n), lambda h: at(pre_side, side, 1, h))


def back_two_kernel(
    count, pre_two, dn, dn_lat, dn_side, sums_in, pre, block, vec, grad, mid, sums, kept, g_all, *flats
):
    total = jnp.sum(sums_in[...], axis=0)
    kept[...] = jnp.concatenate([total[g, i : i + 1] for g in range(MB) for i in range(4)], axis=0)
    means, inverses, dgain, dshift = second_stats(kept, count)
    terms = back_terms(means, inverses, vec[4:5, :], dgain, dshift, count)
    for flat in flats:
        flat[...] = jnp.zeros(flat.shape, F32)
    for edge in (0, R + 3):
        g_all[edge // 2, edge % 2] = jnp.zeros((T, W3), BF16)

    def make(odd, place, row, inner, inner_row):
        build_back(
            flats[odd],
            g_all,
            place,
            terms,
            lambda n: pre_two[row, 16 * n : 16 * n + 16, :],
            lambda n: inner[inner_row, 16 * n : 16 * n + 16, :],
            lambda h: pre_two[row, TI + 8 * h : TI + 8 * h + 8, :],
            lambda h: dn_side[row, 8 * h : 8 * h + 8, :],
        )

    def body(i, total):
        for odd in range(2):
            place = place_of(i, odd)
            make(odd, place, 2 * i + odd, dn, 2 * i + odd)
            own = g_all[place + (slice(0, TI), slice(C, 2 * C))]
            grad[2 * i + odd] = own
            total = total + fold(own.astype(F32))
        return total

    bias = lax.fori_loop(0, R // 2, body, jnp.zeros((8, C), F32))
    for odd in range(2):
        make(odd, place_of(R // 2, odd), R + odd, dn_lat, odd)
    total = None
    for low, high in ((0, 5), (5, 9)):
        for n, v in enumerate(conv_rows(g_all, low, high, block[...])):
            row = 2 * low + n
            mid[row] = v
            if row < R:
                own = v[:TI]
                total = added(total, batch_sums(own) + batch_sums(own * act(pre[row])))
    put_all(sums, [down(v) for v in total] + [down(bias), jnp.zeros((1, C), F32)])


def wgrad_add(acc, inner, grad, low, high):
    left = jnp.concatenate([grad(row) for row in range(low, high)], axis=0)
    right = jnp.concatenate(
        [
            jnp.concatenate([inner[(row + ky) // 2, (row + ky) % 2, :TI] for ky in range(3)], axis=1)
            for row in range(low, high)
        ],
        axis=0,
    )
    part = lax.dot_general(left, right, (((0,), (0,)), ((), ())), preferred_element_type=F32)
    for ky in range(3):
        own = part[:, W3 * ky : W3 * ky + W3]
        acc[ky] = own if low == 0 else acc[ky] + own


def split_out(acc, which, keep, send):
    first = lax.axis_index("lat") == 0
    for ky in range(3):
        for kx in range(3):
            at = pl.ds(pl.multiple_of(144 * which + 16 * (3 * own_tap(ky) + kx), 16), 16)
            taps = acc[ky, :, C * kx : C * kx + C].T
            for d in range(4):
                low, high = taps[32 * d : 32 * d + 16], taps[32 * d + 16 : 32 * d + 32]
                keep[d, at, :] = jnp.where(first, low, high)
                send[d, at, :] = jnp.where(first, high, low).astype(BF16)


def plain_out(acc, which, out):
    for ky in range(3):
        for kx in range(3):
            out[which, 3 * own_tap(ky) + kx] = acc[ky, :, C * kx : C * kx + C].T


def output_kernel(count, after, x, pre_two, sums_in, vec_in, out):
    vec = vec_rows(vec_in)
    means, inverses, _, _ = second_stats(sums_in, count)
    gains = [inverses[m] * vec[4] for m in range(MB)]
    shifts = [vec[5] - means[m] * gains[m] for m in range(MB)]

    @pl.loop(0, R)
    def _(row):
        source = own_row(row)
        for s in range(S):
            value = act(pre_two[row, 16 * s : 16 * s + 16, :])
            out[s, source] = (x[s, source].astype(F32) + value * gains[s // PER] + shifts[s // PER]).astype(BF16)


def first_back_stats(first_in, sums_in, count):
    means, inverses = norm_of(taken(first_in, 2 * MB), count)
    rows = taken(sums_in, 2 * MB + 1)
    dshift = rows[:MB]
    dgain = [inverses[m] * (rows[MB + m] - means[m] * dshift[m]) for m in range(MB)]
    return means, inverses, dgain, dshift, rows[2 * MB]


def back_one_kernel(split, count, pre, pre_side, mid, first_in, sums_in, x_all, n_all, grad_two, vec, g_inner, bias, kept, *rest):
    outs, (acc_one, acc_two), flats = rest[:-4], rest[-4:-2], rest[-2:]
    kept[...] = jnp.sum(sums_in[...], axis=0)
    means, inverses, dgain, dshift, _ = first_back_stats(first_in, kept, count)
    terms = back_terms(means, inverses, vec[1:2, :], dgain, dshift, count)
    for flat in flats:
        flat[...] = jnp.zeros(flat.shape, F32)
    g_inner[0, 0] = jnp.zeros((TI, W3), BF16)

    def make(row):
        build_back(
            flats[row % 2],
            g_inner,
            ((row + 1) // 2, (row + 1) % 2),
            terms,
            lambda n: pre[row, 16 * n : 16 * n + 16, :],
            lambda n: mid[row, 16 * n : 16 * n + 16, :],
            lambda h: pre_side[row, 8 * h : 8 * h + 8, :],
            lambda h: mid[row, TI + 8 * h : TI + 8 * h + 8, :],
        )

    def made(row):
        return g_inner[(row + 1) // 2, (row + 1) % 2, :, C : 2 * C]

    total = jnp.zeros((8, C), F32)
    for n in range(4):
        for row in range(4 * n, 4 * n + 4):
            make(row)
            total = total + fold(made(row).astype(F32))
        wgrad_add(acc_two, n_all, lambda row: grad_two[row], 4 * n, 4 * n + 4)
        if n > 0:
            wgrad_add(acc_one, x_all, made, 4 * n - 4, 4 * n)
    make(R)
    wgrad_add(acc_one, x_all, made, R - 4, R)
    bias[...] = jnp.concatenate([down(total), jnp.zeros((7, C), F32)], axis=0)
    (split_out if split else plain_out)(acc_two, 1, *outs)
    (split_out if split else plain_out)(acc_one, 0, *outs)


def input_grad_kernel(lead, after, g_inner, cot, block, out):
    scale = lead_scales(lead)
    for row, v in enumerate(conv_rows(g_inner, 0, R // 2, block[...], TI)):
        source = own_row(row)
        for n in range(S):
            incoming = cot[n, source].astype(F32) * scale[n]
            out[n, source] = (v[16 * n : 16 * n + 16] + incoming).astype(BF16)


def merge_kernel(keep, got, out):
    for d in range(4):
        total = keep[d] + got[d].astype(F32)
        for n in range(4):
            parts = [total[144 * k + 36 * n : 144 * k + 36 * n + 36] for k in range(2)]
            out[4 * d + n] = jnp.concatenate(parts + [jnp.zeros((8, C), F32)], axis=0).astype(BF16)


def owned_kernel(outputs, grad_inputs, parts, bias, chunk, sums):
    total = parts[0].astype(F32)
    for n in range(1, parts.shape[0]):
        total = total + parts[n].astype(F32)
    own = total[:72]
    chunk[...] = total.astype(BF16)
    put_all(sums, [down(fold(own * own)), bias[0:1, :]])


def pair_kernel(own, other, out):
    first = lax.axis_index("lat") == 0
    mine, its = own[...].astype(F32), other[...].astype(F32)
    low, high = jnp.where(first, mine[:72], its[:72]), jnp.where(first, its[:72], mine[:72])
    out[...] = jnp.concatenate([low, high], axis=0).astype(BF16)


def fetch_kernel(*refs):
    far, near, sems = refs[:6], refs[7:13], refs[13]
    copies = [pltpu.make_async_copy(far[n], near[n], sems.at[n]) for n in range(6)]
    for copy in copies:
        copy.start()
    for copy in copies:
        copy.wait()


def adam(weight, first, second, grad, rate, decay):
    first_new = BETA_ONE * first + (1.0 - BETA_ONE) * grad
    second_new = BETA_TWO * second + (1.0 - BETA_TWO) * grad * grad
    first_hat = first_new * (1.0 / (1.0 - BETA_ONE**STEP))
    second_hat = second_new * (1.0 / (1.0 - BETA_TWO**STEP))
    weight_new = weight - rate * (first_hat / (jnp.sqrt(second_hat) + ADAM_EPS) + decay * weight)
    return weight_new, first_new, second_new


def vector_grads(first_in, second_in, third_in, bias_one, count):
    _, _, dgain_two, dshift_two = second_stats(second_in, count)
    _, _, dgain_one, dshift_one, bias_two = first_back_stats(first_in, third_in, count)
    rows = [bias_one, sum(dgain_one), sum(dshift_one), bias_two, sum(dgain_two), sum(dshift_two)]
    return jnp.concatenate(rows, axis=0)


def update_kernel(count, *refs):
    weight, first, second, vectors, vec_first, vec_second = refs[:6]
    chunks, (sums_in, first_in, second_in, third_in), refs = refs[6:10], refs[10:14], refs[14:]
    norm_out, weight_new, first_new, second_new, weight_low, vectors_new, vec_first_new, vec_second_new = refs[:8]
    slab, grad = refs[8:]
    total = jnp.sum(sums_in[...], axis=0)
    vec_grad = vector_grads(first_in, second_in, third_in, total[1:2], count)
    square = jnp.sum(total[0:1], axis=1, keepdims=True) + jnp.sum(
        down(vec_grad * vec_grad), axis=1, keepdims=True
    )
    norm = jnp.sqrt(square)
    norm_out[...] = norm
    clip = jnp.minimum(1.0, CLIP / (norm + 1e-06))
    for n, chunk in enumerate(chunks):
        at = pl.ds(36 * lax.rem(lax.axis_index("lon") + n, 4), 36)
        part = chunk[...].astype(F32)
        for lat in range(2):
            for k in range(2):
                slab[k, lat, at, :] = part[72 * lat + 36 * k : 72 * lat + 36 * k + 36]
    for k in range(2):
        for lat in range(2):
            for t in range(9):
                grad[k, pl.ds(144 * lat + t, 16, stride=9), :] = slab[k, lat, 16 * t : 16 * t + 16, :]
        new = adam(weight[k], first[k], second[k], grad[k] * clip, RATE_CONV, DECAY_CONV)
        weight_new[k], first_new[k], second_new[k] = new
        weight_low[k] = new[0].astype(BF16)
    width = vectors.shape[1]
    turned = pltpu.roll(
        jnp.concatenate([vec_grad, jnp.zeros((2, C), F32)], axis=0),
        lax.rem(C - lax.axis_index("dp") * width, C),
        axis=1,
    )
    new = adam(vectors[...], vec_first[...], vec_second[...], turned[:6, :width] * clip, RATE_VEC, 0.0)
    vectors_new[...], vec_first_new[...], vec_second_new[...] = new


def spread(block, axes):
    return lax.all_to_all(block, axes, 0, 0, tiled=True)


def turn(block, axis, by):
    size = lax.axis_size(axis)
    return lax.ppermute(block, axis, [(i, (i + by) % size) for i in range(size)])


def body(inputs, lead_time, cotangent, conv_weight, conv_first, conv_second, vectors, vec_first, vec_second):
    devices = lax.axis_size("dp") * lax.axis_size("lat") * lax.axis_size("lon")
    groups = lax.axis_size("dp")
    split = groups == 4 and lax.axis_size("lon") == 4
    count = float(PER * R * R * devices)
    size = conv_weight.shape[1] // 9
    flats = [pltpu.VMEM((FLAT, C), F32)] * 2
    conv_flops = 2 * T * 12 * C * 2 * C

    packed, lat_out, x_near, cot_near = call(
        prep_kernel,
        [
            ((2, 9 * size + 16, C), BF16),
            ((S, 6, R, C), BF16),
            (inputs.shape, BF16),
            (inputs.shape, BF16),
        ],
        (inputs, cotangent, conv_weight, vectors),
        [
            pltpu.VMEM(conv_weight.shape, F32),
            pltpu.VMEM(vectors.shape, F32),
            pltpu.SemaphoreType.DMA((6,)),
        ],
        far=4,
    )
    lat_in = turn(lat_out, "lat", 1)
    edge_kinds = [((R + 4, MB, 16, C), BF16)] * 2
    edges = call(edge_kernel, edge_kinds, (x_near,))
    mine, far_r, far_l = call(
        beyond_kernel,
        [((9 * size + 16, C), BF16)] + edge_kinds,
        (lat_in, packed, *edges),
        aliases={2: 1, 3: 2},
    )
    far_left, far_right = turn(far_r, "lon", 1), turn(far_l, "lon", -1)
    if split:
        pieces = [packed]
        for k in range(1, groups):
            fetched = turn(mine, "dp", k)
            pieces += [fetched, turn(fetched, "lat", 1)]
    else:
        whole = lax.all_gather(packed, "dp")
        taps = whole[:, :, : 9 * size].reshape(groups, 2, 9, size, C).transpose(1, 2, 0, 3, 4)
        tail = jnp.sum(whole[:, :, 9 * size :], axis=0)
        pieces = [jnp.concatenate([taps.reshape(2, 9 * C, C), tail], axis=1)]
    dn, dn_sums = call(
        lead_kernel, [((R, TI, C), F32), ((8, C), F32)], (lead_time, cot_near), flops=10**8, scalars=1
    )
    (x_all,) = call(
        shift_kernel, [((11, 2, TI, W3), BF16)], (x_near, lat_in, far_left, far_right), flats, flops=10**8
    )
    block_one, vec = call(block_kernel, [((12 * C, 2 * C), BF16), ((16, C), F32)], pieces, flops=10**8)
    pre_one, sums_one = call(
        first_kernel,
        [((R + 4, TI, C), F32), ((devices, 8, C), F32)],
        (x_all, block_one, vec),
        flops=conv_flops * 6,
    )
    sums_one, dn = lax.optimization_barrier((sums_one, dn))
    got_one = spread(sums_one, ALL)
    block_two, two_back, one_back = call(
        weight_kernel,
        [((12 * C, 2 * C), BF16)] * 3,
        (got_one, block_one, *pieces),
        [pltpu.VMEM((12 * C, 2 * C), BF16), pltpu.SemaphoreType.DMA(())],
        flops=10**8,
        far_out=(2,),
    )
    (pre_side,) = call(
        halo_kernel,
        [((R + 4, TH, C), F32)],
        (got_one, x_near, lat_in, far_left, far_right, block_one, vec),
        [pltpu.VMEM((11, 2, TH, W3), BF16)] + flats,
        flops=conv_flops * 4,
    )
    cot_r, cot_l = call(
        later_kernel, [((R // 2 + 1, MB, 16, C), BF16)] * 2, (got_one, cot_near, lat_in)
    )
    cot_left, cot_right = turn(cot_r, "lon", 1), turn(cot_l, "lon", -1)
    n_all, pre_two, sums_two, stat_one = call(
        lambda *refs: second_kernel(count, *refs),
        [((10, 2, T, W3), BF16), ((R + 2, T, C), F32), ((devices, 3, 4, C), F32), ((8, C), F32)],
        (pre_one, pre_side, got_one, dn, dn_sums, block_two, vec),
        flats,
        flops=conv_flops * 9,
    )
    dn_lat, dn_side = call(
        lead_side_kernel,
        [((2, TI, C), F32), ((R + 2, TH, C), F32)],
        (lead_time, sums_two, lat_in, cot_left, cot_right),
        flats,
        flops=10**8,
        scalars=1,
    )
    sums_two, dn_lat, dn_side = lax.optimization_barrier((sums_two, dn_lat, dn_side))
    got_two = spread(sums_two, ALL)
    grad_two, mid, sums_three, stat_two = call(
        lambda *refs: back_two_kernel(count, *refs),
        [((R, TI, C), BF16), ((R + 2, T, C), F32), ((devices, 8, C), F32), ((4 * MB, C), F32)],
        (pre_two, dn, dn_lat, dn_side, got_two, pre_one, two_back, vec),
        [pltpu.VMEM((10, 2, T, W3), BF16)] + flats,
        flops=conv_flops * 9,
    )
    got_three = spread(sums_three, ALL)
    grad_kinds = [((4, 288, C), F32), ((4, 288, C), BF16)] if split else [((2, 9, C, C), F32)]
    g_inner, bias_one, stat_three, *grads = call(
        lambda *refs: back_one_kernel(split, count, *refs),
        [((9, 2, TI, W3), BF16), ((8, C), F32), ((8, C), F32)] + grad_kinds,
        (pre_one, pre_side, mid, stat_one, got_three, x_all, n_all, grad_two, vec),
        [pltpu.VMEM((3, C, W3), F32)] * 2 + flats,
        flops=conv_flops * 9,
    )

    def finish(after):
        (outputs,) = call(
            lambda *refs: output_kernel(count, *refs),
            [((S, R, R, C), BF16)],
            (after, inputs, pre_two, stat_two, vec),
            flops=10**8,
        )
        (grad_inputs,) = call(
            input_grad_kernel,
            [((S, R, R, C), BF16)],
            (lead_time, after, g_inner, cotangent, one_back),
            flops=conv_flops * 6,
            scalars=1,
        )
        return outputs, grad_inputs

    if split:
        (merged,) = call(merge_kernel, [((16, 80, C), BF16)], (grads[0], turn(grads[1], "lat", 1)))
        parts = spread(merged, ("dp", "lon"))
        outputs, grad_inputs = finish(merged)
        chunk, sums_four = call(
            owned_kernel,
            [((80, C), BF16), ((devices, 2, C), F32)],
            (outputs, grad_inputs, parts, bias_one),
            far=2,
        )
        got_four = spread(sums_four, ALL)
        (pair,) = call(pair_kernel, [((144, C), BF16)], (chunk, turn(chunk, "lat", 1)), flops=10**10)
        chunks = [pair] + [turn(pair, "lon", -k) for k in range(1, 4)]
        kinds = [((1, 1), F32)] + [(conv_weight.shape, F32)] * 3 + [(conv_weight.shape, BF16)]
        moments = (conv_weight, conv_first, conv_second, vectors, vec_first, vec_second)
        moments = call(
            fetch_kernel,
            [(moment.shape, F32) for moment in moments],
            (*moments, pair),
            [pltpu.SemaphoreType.DMA((6,))],
            flops=10**10,
            far=6,
        )
        norm, *news = call(
            lambda *refs: update_kernel(count, *refs),
            kinds + [(vectors.shape, F32)] * 3,
            (*moments, *chunks, got_four, stat_one, stat_two, stat_three),
            [pltpu.VMEM((2, 2, 144, C), F32), pltpu.VMEM(conv_weight.shape, F32)],
        )
        return (outputs, grad_inputs, norm.reshape(()), *news)
    outputs, grad_inputs = finish(bias_one)
    stacked = grads[0].transpose(0, 2, 1, 3).reshape(2, 9 * C, C)
    conv_total, bias_total = lax.psum((stacked, bias_one[0:1]), ALL)
    vec_total = vector_grads(stat_one, stat_two, stat_three, bias_total, count)
    grad_norm = jnp.sqrt(jnp.sum(conv_total * conv_total) + jnp.sum(vec_total * vec_total))
    clip = jnp.minimum(1.0, CLIP / (grad_norm + 1e-06))
    index = lax.axis_index("dp")
    conv_own = lax.dynamic_slice_in_dim(conv_total, index * conv_weight.shape[1], conv_weight.shape[1], 1)
    vec_own = lax.dynamic_slice_in_dim(vec_total, index * vectors.shape[1], vectors.shape[1], 1)
    conv_news = adam(conv_weight, conv_first, conv_second, conv_own * clip, RATE_CONV, DECAY_CONV)
    vec_news = adam(vectors, vec_first, vec_second, vec_own * clip, RATE_VEC, 0.0)
    return (outputs, grad_inputs, grad_norm, *conv_news, conv_news[0].astype(BF16), *vec_news)


def solution(mesh):
    grid = P("dp", "lat", "lon", None)
    rows = P(None, "dp", None)
    columns = P(None, "dp")
    in_specs = (grid, P("dp"), grid, rows, rows, rows, columns, columns, columns)
    out_specs = (grid, grid, P(), rows, rows, rows, rows, columns, columns, columns)
    return jax.shard_map(body, mesh=mesh, in_specs=in_specs, out_specs=out_specs, check_vma=False)
```

time: 133 us -> 110 us (0.83)
  blocking collectives: 55.8 us -> 33.7 us
  local copies, waits for them, and re-layouts: 9.13 us -> 2.62 us
  Pallas kernels: 29.9 us -> 33.9 us
  starting transfers between devices: 20.5 us -> 23.8 us
  waiting for transfers between devices: 16.7 us -> 14.4 us
    all_to_all x5 -> x3, blocking collectives: 55.8 us -> 33.7 us  [spread(): return lax.all_to_all(block, axes, 0, 0, tiled=True)]
    ppermute x13 -> x16, waiting for transfers between devices: 16.7 us -> 9.82 us  [turn(): lax.ppermute(block, axis, [(i, (i + by) % size) for i in range(size)])]
    unnamed x38 -> x12, local copies, waits for them, and re-layouts: 9.13 us -> 2.62 us
    all_to_all x1 -> x2, waiting for transfers between devices: 0.01 us -> 4.6 us  [spread(): return lax.all_to_all(block, axes, 0, 0, tiled=True)]
    pallas_call x16 -> x21, Pallas kernels: 29.9 us -> 33.9 us  [call(): pl.pallas_call(kernel, out_shape=tuple((pltpu.HBM(shape, kind) if n in fa...]
    all_to_all x1 -> x2, starting transfers between devices: 3.42 us -> 6.11 us  [spread(): return lax.all_to_all(block, axes, 0, 0, tiled=True)]
    ppermute x13 -> x16, starting transfers between devices: 17.1 us -> 17.7 us  [turn(): lax.ppermute(block, axis, [(i, (i + by) % size) for i in range(size)])]
  transfers between devices with their start and end apart: 14 -> 18, of which waited for: 6 -> 6; matrix products, arithmetic and copies ran while one was open for 0% -> 0% of each run, Pallas kernels for 8% -> 14%
where the time goes in v2:
time: 110 us; the launch traced here: 109 us
  Pallas kernels  33.9 us (31%)
  blocking collectives  33.7 us (31%)
  starting transfers between devices  23.8 us (22%)
  waiting for transfers between devices  14.4 us (13%)
  local copies, waits for them, and re-layouts  2.62 us (2%)
    pallas_call x21, Pallas kernels, call(): pl.pallas_call(kernel, out_shape=tuple((pltpu.HBM(shape, kind) if n in fa...  33.9 us
    all_to_all x3, blocking collectives, spread(): return lax.all_to_all(block, axes, 0, 0, tiled=True)  33.7 us
    ppermute x16, starting transfers between devices, turn(): lax.ppermute(block, axis, [(i, (i + by) % size) for i in range(size)])  17.7 us
    ppermute x16, waiting for transfers between devices, turn(): lax.ppermute(block, axis, [(i, (i + by) % size) for i in range(size)])  9.82 us
    all_to_all x2, starting transfers between devices, spread(): return lax.all_to_all(block, axes, 0, 0, tiled=True)  6.11 us
    all_to_all x2, waiting for transfers between devices, spread(): return lax.all_to_all(block, axes, 0, 0, tiled=True)  4.6 us
    unnamed x12, local copies, waits for them, and re-layouts  2.62 us
  transfers between devices with their start and end apart: 18, of which 6 were waited for; matrix products, arithmetic and copies ran while one was open for 0% of the time, Pallas kernels for 14%

profile of v2, /device:TPU:0, one launch (start us, length us, event | category | flops | bytes accessed | tf_op | source)
XLA Modules:
  0.0 109.3 jit_solution(10925166176891356022)
XLA Ops:
  0.6 0.0 copy-start.5
  0.7 1.7 %shard_map.168 = (bf16[2,304,128]{2,1,0:T(8,128)(2,1)S(1)}, bf16[12,6,16,128]{3,2,1,0:T(8,128)(2,1)S(1)}, bf16[12,16,16,128]{3,2,1,0:T(8,128)(2,1)S(1)}, bf16[12,16,16,128]{3,2,1,0:T(8,128)(2,1)S(1)}) custom-call(bf16[12,16,16,128]{3,2,1,0:T(8,128)(2,1)} %refs_1_.2, bf16[12,16,16,128]{3,2,1,0:T(8,128)(2,1)} %cot.3, f32[2,288,128]{2,1,0:T(8,128)} %refs_0_.1, ...), custom_call_target="tpu_custom_call" | custom-call | bytes 1868544 | tf_op jit(solution)/shard_map/pallas_call | solution.py:45
  2.3 0.5 collective-permute-start
  2.9 0.2 shard_map.169
  3.1 1.0 collective-permute-done.lat_in
  4.1 2.9 %collective-permute-start.1 = (bf16[20,3,16,128]{3,2,1,0:T(8,128)(2,1)S(1)}, bf16[20,3,16,128]{3,2,1,0:T(8,128)(2,1)S(1)}, u32[]{:S(2)}, u32[]{:S(2)}) collective-permute-start(bf16[20,3,16,128]{3,2,1,0:T(8,128)(2,1)S(1)} %get-tuple-element.71), channel_id=1, source_target_pairs={{0,1},{1,2},{2,3},{3,0},{4,5},{5,6},{6,7},{7,4},{8,9},{9,10},{10,1... | collective-permute-start | bytes 737288 | tf_op jit(solution)/shard_map/ppermute | solution.py:739
  7.0 1.0 collective-permute-start.2
  8.0 4.0 %collective-permute-start.7 = (bf16[304,128]{1,0:T(8,128)(2,1)S(1)}, bf16[304,128]{1,0:T(8,128)(2,1)S(1)}, u32[]{:S(2)}, u32[]{:S(2)}) collective-permute-start(bf16[304,128]{1,0:T(8,128)(2,1)S(1)} %get-tuple-element.73), channel_id=1, source_target_pairs={{0,24},{8,0},{16,8},{24,16},{1,25},{9,1},{17,9},{25,17},{2,26},{10... | collective-permute-start | bytes 233480 | tf_op jit(solution)/shard_map/ppermute | solution.py:739
  12.1 0.0 collective-permute-start.5
  12.1 1.0 collective-permute-start.3
  13.1 1.8 %collective-permute-done.7.rest_5_ = bf16[304,128]{1,0:T(8,128)(2,1)S(1)} collective-permute-done((bf16[304,128]{1,0:T(8,128)(2,1)S(1)}, bf16[304,128]{1,0:T(8,128)(2,1)S(1)}, u32[]{:S(2)}, u32[]{:S(2)}) %collective-permute-start.7) | collective-permute-done | bytes 77856 | tf_op jit(solution)/shard_map/ppermute | solution.py:739
  14.9 0.0 collective-permute-start.8
  14.9 4.2 %collective-permute-done.5.rest_3_ = bf16[304,128]{1,0:T(8,128)(2,1)S(1)} collective-permute-done((bf16[304,128]{1,0:T(8,128)(2,1)S(1)}, bf16[304,128]{1,0:T(8,128)(2,1)S(1)}, u32[]{:S(2)}, u32[]{:S(2)}) %collective-permute-start.5) | collective-permute-done | bytes 77856 | tf_op jit(solution)/shard_map/ppermute | solution.py:739
  19.0 0.0 collective-permute-start.6
  19.0 0.0 collective-permute-done.3.rest_1_
  19.0 0.5 collective-permute-start.4
  19.5 0.0 copy-done.5
  19.5 0.9 shard_map.174
  20.4 0.0 collective-permute-done.8.rest_6_
  20.4 0.0 collective-permute-done.6.rest_4_
  20.4 0.0 collective-permute-done.4.rest_2_
  20.4 0.1 shard_map.172
  20.6 0.0 collective-permute-done.1.from_left
  20.6 0.0 collective-permute-done.2.from_right
  20.6 0.8 shard_map.171.x_all.refs_5_
  21.4 1.9 %shard_map.173 = (f32[20,192,128]{2,1,0:T(8,128)S(1)}, f32[32,8,128]{2,1,0:T(8,128)S(1)}) custom-call(bf16[11,2,192,384]{3,2,1,0:T(8,128)(2,1)S(1)} %shard_map.171.x_all.refs_5_, bf16[1536,256]{1,0:T(8,128)(2,1)S(1)} %get-tuple-element.74.block.block_one, f32[16,128]{1,0:T(8,128)S(1)} %get-tuple-element.75.vec.refs_6_.refs_7_.refs_8_.refs_4_), custom_call_target="tpu_custom_call" | custom-call | flops 1434451968 | bytes 4038656 | tf_op jit(solution)/shard_map/pallas_call | solution.py:45
  23.3 12.2 %all_to_all.25.after.refs_2_ = f32[32,8,128]{2,1,0:T(8,128)S(1)} all-to-all(f32[32,8,128]{2,1,0:T(8,128)S(1)} %get-tuple-element.80), channel_id=1, replica_groups=mesh['dp'=4,'lat'=2,'lon'=4] {'dp','lat','lon'}, dimensions={0} | all-to-all | bytes 262144 | tf_op jit(solution)/shard_map/all_to_all | solution.py:734
  35.5 0.3 shard_map.178
  35.8 0.4 collective-permute-start.9
  36.2 2.6 %collective-permute-start.10 = (bf16[9,3,16,128]{3,2,1,0:T(8,128)(2,1)S(1)}, bf16[9,3,16,128]{3,2,1,0:T(8,128)(2,1)S(1)}, u32[]{:S(2)}, u32[]{:S(2)}) collective-permute-start(bf16[9,3,16,128]{3,2,1,0:T(8,128)(2,1)S(1)} %get-tuple-element.87), channel_id=1, source_target_pairs={{0,3},{1,0},{2,1},{3,2},{4,7},{5,4},{6,5},{7,6},{8,11},{9,8},{10,9... | collective-permute-start | bytes 331784 | tf_op jit(solution)/shard_map/ppermute | solution.py:739
  38.8 1.6 %shard_map.175.refs_1_ = f32[20,112,128]{2,1,0:T(8,128)S(1)} custom-call(f32[32,8,128]{2,1,0:T(8,128)S(1)} %all_to_all.25.after.refs_2_, bf16[12,16,16,128]{3,2,1,0:T(8,128)(2,1)S(1)} %get-tuple-element.66.x, bf16[12,6,16,128]{3,2,1,0:T(8,128)(2,1)S(1)} %collective-permute-done.lat_in, bf16[20,3,16,128]{3,2,1,0:T(8,128)(2,1)S(1)} %collective-permute-done.1.from_left, ...), custom_call_target="tpu_custom_call" | custom-call | flops 956301312 | bytes 2498560 | tf_op jit(solution)/shard_map/pallas_call | solution.py:45
  40.4 1.2 %shard_map.176 = (bf16[1536,256]{1,0:T(8,128)(2,1)S(1)}, bf16[1536,256]{1,0:T(8,128)(2,1)S(1)}, bf16[1536,256]{1,0:T(8,128)(2,1)}) custom-call(f32[32,8,128]{2,1,0:T(8,128)S(1)} %all_to_all.25.after.refs_2_, bf16[1536,256]{1,0:T(8,128)(2,1)S(1)} %get-tuple-element.74.block.block_one, bf16[2,304,128]{2,1,0:T(8,128)(2,1)S(1)} %get-tuple-element.68.packed.rest_0_, ...), custom_call_target="tpu_custom_call" | custom-call | flops 100000000 | bytes 1540096 | tf_op jit(solution)/shard_map/pallas_call | solution.py:45
  41.5 4.6 %shard_map.177 = (bf16[10,2,304,384]{3,2,1,0:T(8,128)(2,1)S(1)}, f32[18,304,128]{2,1,0:T(8,128)S(1)}, f32[32,3,4,128]{3,2,1,0:T(4,128)S(1)}, f32[8,128]{1,0:T(8,128)S(1)}) custom-call(f32[20,192,128]{2,1,0:T(8,128)S(1)} %get-tuple-element.76.refs_0_.refs_5_, f32[20,112,128]{2,1,0:T(8,128)S(1)} %shard_map.175.refs_1_, ...), custom_call_target="tpu_custom_call" | custom-call | flops 2151677952 | bytes 5615616 | tf_op jit(solution)/shard_map/pallas_call | solution.py:45
  46.1 0.0 collective-permute-done.9.from_left
  46.1 0.0 collective-permute-done.10.from_right
  46.1 0.9 shard_map.179
  47.0 11.2 %all_to_all.26.refs_4_ = f32[32,3,4,128]{3,2,1,0:T(4,128)S(1)} all-to-all(f32[32,3,4,128]{3,2,1,0:T(4,128)S(1)} %get-tuple-element.92.after), channel_id=1, replica_groups=mesh['dp'=4,'lat'=2,'lon'=4] {'dp','lat','lon'}, dimensions={0} | all-to-all | bytes 393216 | tf_op jit(solution)/shard_map/all_to_all | solution.py:734
  58.2 5.2 %shard_map.180 = (bf16[16,192,128]{2,1,0:T(8,128)(2,1)S(1)}, f32[18,304,128]{2,1,0:T(8,128)S(1)}, f32[32,8,128]{2,1,0:T(8,128)S(1)}, f32[12,128]{1,0:T(8,128)S(1)}) custom-call(f32[18,304,128]{2,1,0:T(8,128)S(1)} %get-tuple-element.84.refs_0_.refs_2_, f32[16,192,128]{2,1,0:T(8,128)S(1)} %get-tuple-element.81.refs_3_.refs_1_, ...), custom_call_target="tpu_custom_call" | custom-call | flops 2151677952 | bytes 8560640 | tf_op jit(solution)/shard_map/pallas_call | solution.py:45
  63.4 10.2 %all_to_all.27.refs_4_ = f32[32,8,128]{2,1,0:T(8,128)S(1)} all-to-all(f32[32,8,128]{2,1,0:T(8,128)S(1)} %get-tuple-element.96), channel_id=1, replica_groups=mesh['dp'=4,'lat'=2,'lon'=4] {'dp','lat','lon'}, dimensions={0} | all-to-all | bytes 262144 | tf_op jit(solution)/shard_map/all_to_all | solution.py:734
  73.7 4.4 %shard_map.181 = (bf16[9,2,192,384]{3,2,1,0:T(8,128)(2,1)S(1)}, f32[8,128]{1,0:T(8,128)S(1)}, f32[8,128]{1,0:T(8,128)S(1)}, f32[4,288,128]{2,1,0:T(8,128)S(1)}, bf16[4,288,128]{2,1,0:T(8,128)(2,1)S(1)}) custom-call(f32[20,192,128]{2,1,0:T(8,128)S(1)} %get-tuple-element.76.refs_0_.refs_5_, f32[20,112,128]{2,1,0:T(8,128)S(1)} %shard_map.175.refs_1_, ...), custom_call_target="tpu_custom_call" | custom-call | flops 2151677952 | bytes 14757888 | tf_op jit(solution)/shard_map/pallas_call | solution.py:45
  78.1 0.0 copy-start.2
  78.1 1.5 %copy-done.2 = bf16[9,2,192,384]{3,2,1,0:T(8,128)(2,1)} copy-done((bf16[9,2,192,384]{3,2,1,0:T(8,128)(2,1)}, bf16[9,2,192,384]{3,2,1,0:T(8,128)(2,1)S(1)}, u32[]{:S(2)}) %copy-start.2) | copy-done | bytes 2654232
  79.6 0.0 collective-permute-start.11
  79.6 1.6 %collective-permute-done.11.got = bf16[4,288,128]{2,1,0:T(8,128)(2,1)S(1)} collective-permute-done((bf16[4,288,128]{2,1,0:T(8,128)(2,1)S(1)}, bf16[4,288,128]{2,1,0:T(8,128)(2,1)S(1)}, u32[]{:S(2)}, u32[]{:S(2)}) %collective-permute-start.11) | collective-permute-done | bytes 294944 | tf_op jit(solution)/shard_map/ppermute | solution.py:739
  81.2 0.8 shard_map.182.refs_0_.after
  82.0 3.5 %all-to-all-start.3 = ((bf16[16,80,128]{2,1,0:T(8,128)(2,1)}), bf16[16,80,128]{2,1,0:T(8,128)(2,1)S(1)}, u32[]{:S(2)}, u32[]{:S(2)}) async-start(bf16[16,80,128]{2,1,0:T(8,128)(2,1)} %shard_map.182.refs_0_.after), calls=%async_computation.3 | async-start | bytes 655360 | tf_op jit(solution)/shard_map/all_to_all | solution.py:734
  85.5 0.0 copy-start
  85.5 1.1 %copy-done = bf16[12,16,16,128]{3,2,1,0:T(8,128)(2,1)S(1)} copy-done((bf16[12,16,16,128]{3,2,1,0:T(8,128)(2,1)S(1)}, bf16[12,16,16,128]{3,2,1,0:T(8,128)(2,1)}, u32[]{:S(2)}) %copy-start) | copy-done | bytes 786456
  86.7 2.8 %shard_map.183.outputs = bf16[12,16,16,128]{3,2,1,0:T(8,128)(2,1)} custom-call(bf16[16,80,128]{2,1,0:T(8,128)(2,1)} %shard_map.182.refs_0_.after, bf16[12,16,16,128]{3,2,1,0:T(8,128)(2,1)S(1)} %copy-done, f32[18,304,128]{2,1,0:T(8,128)S(1)} %get-tuple-element.84.refs_0_.refs_2_, f32[12,128]{1,0:T(8,128)S(1)} %get-tuple-element.101.refs_3_.refs_12_, ...), custom_call_target="tpu_custom_call" | custom-call | flops 100000000 | bytes 3930112 | tf_op jit(solution)/shard_map/pallas_call | solution.py:45
  89.5 3.3 %shard_map.184.grad_inputs = bf16[12,16,16,128]{3,2,1,0:T(8,128)(2,1)} custom-call(s32[12]{0:T(128)S(1)} %copy-done.5, bf16[16,80,128]{2,1,0:T(8,128)(2,1)} %shard_map.182.refs_0_.after, bf16[9,2,192,384]{3,2,1,0:T(8,128)(2,1)S(1)} %copy-done.3, bf16[12,16,16,128]{3,2,1,0:T(8,128)(2,1)S(1)} %copy-done.1, bf16[1536,256]{1,0:T(8,128)(2,1)S(1)} %copy-done.4), custom_call_target="tpu_custom_call" | custom-call | flops 1434451968 | bytes 4554800 | tf_op jit(solution)/shard_map/pallas_call | solution.py:45
  92.8 4.6 %all-to-all-done.3.parts = bf16[16,80,128]{2,1,0:T(8,128)(2,1)S(1)} async-done(((bf16[16,80,128]{2,1,0:T(8,128)(2,1)}), bf16[16,80,128]{2,1,0:T(8,128)(2,1)S(1)}, u32[]{:S(2)}, u32[]{:S(2)}) %all-to-all-start.3) | async-done | bytes 327712 | tf_op jit(solution)/shard_map/all_to_all | solution.py:734
  97.4 0.7 shard_map.185
  98.0 0.0 collective-permute-start.12
  98.0 2.6 %all-to-all-start.4 = ((f32[32,2,128]{2,1,0:T(2,128)}), f32[32,2,128]{2,1,0:T(2,128)S(1)}, u32[]{:S(2)}, u32[]{:S(2)}) async-start(f32[32,2,128]{2,1,0:T(2,128)} %get-tuple-element.112), calls=%async_computation.4 | async-start | bytes 65536 | tf_op jit(solution)/shard_map/all_to_all | solution.py:734
  100.6 0.0 collective-permute-done.12.other
  100.7 1.8 %collective-permute-start.15 = (bf16[144,128]{1,0:T(8,128)(2,1)S(1)}, bf16[144,128]{1,0:T(8,128)(2,1)S(1)}, u32[]{:S(2)}, u32[]{:S(2)}) collective-permute-start(bf16[144,128]{1,0:T(8,128)(2,1)S(1)} %shard_map.186.refs_6_), channel_id=1, source_target_pairs={{0,1},{1,2},{2,3},{3,0},{4,5},{5,6},{6,7},{7,4},{8,9},{9,10},{10,1... | collective-permute-start | bytes 110600 | tf_op jit(solution)/shard_map/ppermute | solution.py:739
  102.5 1.5 %collective-permute-start.14 = (bf16[144,128]{1,0:T(8,128)(2,1)S(1)}, bf16[144,128]{1,0:T(8,128)(2,1)S(1)}, u32[]{:S(2)}, u32[]{:S(2)}) collective-permute-start(bf16[144,128]{1,0:T(8,128)(2,1)S(1)} %shard_map.186.refs_6_), channel_id=1, source_target_pairs={{0,2},{1,3},{2,0},{3,1},{4,6},{5,7},{6,4},{7,5},{8,10},{9,11},{10,... | collective-permute-start | bytes 110600 | tf_op jit(solution)/shard_map/ppermute | solution.py:739
  103.9 1.5 %collective-permute-start.13 = (bf16[144,128]{1,0:T(8,128)(2,1)S(1)}, bf16[144,128]{1,0:T(8,128)(2,1)S(1)}, u32[]{:S(2)}, u32[]{:S(2)}) collective-permute-start(bf16[144,128]{1,0:T(8,128)(2,1)S(1)} %shard_map.186.refs_6_), channel_id=1, source_target_pairs={{0,3},{1,0},{2,1},{3,2},{4,7},{5,4},{6,5},{7,6},{8,11},{9,8},{10,9... | collective-permute-start | bytes 110600 | tf_op jit(solution)/shard_map/ppermute | solution.py:739
  105.4 1.2 %shard_map.187 = (f32[2,288,128]{2,1,0:T(8,128)S(1)}, f32[2,288,128]{2,1,0:T(8,128)S(1)}, f32[2,288,128]{2,1,0:T(8,128)S(1)}, f32[6,32]{1,0:T(8,128)S(1)}, f32[6,32]{1,0:T(8,128)S(1)}, /*index=5*/f32[6,32]{1,0:T(8,128)S(1)}) custom-call(f32[2,288,128]{2,1,0:T(8,128)} %refs_0_.1, f32[2,288,128]{2,1,0:T(8,128)} %refs_1_.3, f32[2,288,128]{2,1,0:T(8,128)} %refs_2_.1, ...), custom_call_target="tpu_custom_call" | custom-call | flops 10000000000 | bytes 923904 | tf_op jit(solution)/shard_map/pallas_call | solution.py:45
  106.6 0.0 collective-permute-done.15.refs_9_
  106.6 0.0 collective-permute-done.14.refs_8_
  106.6 1.3 %collective-permute-done.13.refs_7_ = bf16[144,128]{1,0:T(8,128)(2,1)S(1)} collective-permute-done((bf16[144,128]{1,0:T(8,128)(2,1)S(1)}, bf16[144,128]{1,0:T(8,128)(2,1)S(1)}, u32[]{:S(2)}, u32[]{:S(2)}) %collective-permute-start.13) | collective-permute-done | bytes 36896 | tf_op jit(solution)/shard_map/ppermute | solution.py:739
  107.9 0.0 all-to-all-done.4.refs_10_
  107.9 1.4 %shard_map.188 = (f32[1,1]{1,0:T(1,128)}, f32[2,288,128]{2,1,0:T(8,128)}, f32[2,288,128]{2,1,0:T(8,128)}, f32[2,288,128]{2,1,0:T(8,128)}, bf16[2,288,128]{2,1,0:...) custom-call(f32[2,288,128]{2,1,0:T(8,128)S(1)} %get-tuple-element.106.refs_0_, ...), custom_call_target="tpu_custom_call" | custom-call | bytes 1081600 | tf_op jit(solution)/shard_map/pallas_call | solution.py:45
  (8 shorter events, 0.1 us)
Async XLA Ops:
  0.6 18.9 %copy-start.5 = (s32[12]{0:T(128)S(1)}, s32[12]{0:T(128)}, u32[]{:S(2)}) copy-start(s32[12]{0:T(128)} %lead.5) | copy-start | bytes 148
  2.3 1.7 %collective-permute-start = (bf16[12,6,16,128]{3,2,1,0:T(8,128)(2,1)S(1)}, bf16[12,6,16,128]{3,2,1,0:T(8,128)(2,1)S(1)}, u32[]{:S(2)}, u32[]{:S(2)}) collective-permute-start(bf16[12,6,16,128]{3,2,1,0:T(8,128)(2,1)S(1)} %get-tuple-element.67), channel_id=1, source_target_pairs={{0,4},{4,0},{1,5},{5,1},{2,6},{6,2},{3,7},{7,3},{8,12},{12,8},{9,1... | collective-permute-start | bytes 884744 | tf_op jit(solution)/shard_map/ppermute | solution.py:739
  4.1 16.5 %collective-permute-start.1 = (bf16[20,3,16,128]{3,2,1,0:T(8,128)(2,1)S(1)}, bf16[20,3,16,128]{3,2,1,0:T(8,128)(2,1)S(1)}, u32[]{:S(2)}, u32[]{:S(2)}) collective-permute-start(bf16[20,3,16,128]{3,2,1,0:T(8,128)(2,1)S(1)} %get-tuple-element.71), channel_id=1, source_target_pairs={{0,1},{1,2},{2,3},{3,0},{4,5},{5,6},{6,7},{7,4},{8,9},{9,10},{10,1... | collective-permute-start | bytes 737288 | tf_op jit(solution)/shard_map/ppermute | solution.py:739
  7.0 13.6 %collective-permute-start.2 = (bf16[20,3,16,128]{3,2,1,0:T(8,128)(2,1)S(1)}, bf16[20,3,16,128]{3,2,1,0:T(8,128)(2,1)S(1)}, u32[]{:S(2)}, u32[]{:S(2)}) collective-permute-start(bf16[20,3,16,128]{3,2,1,0:T(8,128)(2,1)S(1)} %get-tuple-element.72), channel_id=1, source_target_pairs={{0,3},{1,0},{2,1},{3,2},{4,7},{5,4},{6,5},{7,6},{8,11},{9,8},{10,9... | collective-permute-start | bytes 737288 | tf_op jit(solution)/shard_map/ppermute | solution.py:739
  8.0 6.8 %collective-permute-start.7 = (bf16[304,128]{1,0:T(8,128)(2,1)S(1)}, bf16[304,128]{1,0:T(8,128)(2,1)S(1)}, u32[]{:S(2)}, u32[]{:S(2)}) collective-permute-start(bf16[304,128]{1,0:T(8,128)(2,1)S(1)} %get-tuple-element.73), channel_id=1, source_target_pairs={{0,24},{8,0},{16,8},{24,16},{1,25},{9,1},{17,9},{25,17},{2,26},{10... | collective-permute-start | bytes 233480 | tf_op jit(solution)/shard_map/ppermute | solution.py:739
  12.1 7.0 %collective-permute-start.5 = (bf16[304,128]{1,0:T(8,128)(2,1)S(1)}, bf16[304,128]{1,0:T(8,128)(2,1)S(1)}, u32[]{:S(2)}, u32[]{:S(2)}) collective-permute-start(bf16[304,128]{1,0:T(8,128)(2,1)S(1)} %get-tuple-element.73), channel_id=1, source_target_pairs={{0,16},{8,24},{16,0},{24,8},{1,17},{9,25},{17,1},{25,9},{2,18},{10... | collective-permute-start | bytes 233480 | tf_op jit(solution)/shard_map/ppermute | solution.py:739
  12.1 7.0 %collective-permute-start.3 = (bf16[304,128]{1,0:T(8,128)(2,1)S(1)}, bf16[304,128]{1,0:T(8,128)(2,1)S(1)}, u32[]{:S(2)}, u32[]{:S(2)}) collective-permute-start(bf16[304,128]{1,0:T(8,128)(2,1)S(1)} %get-tuple-element.73), channel_id=1, source_target_pairs={{0,8},{8,16},{16,24},{24,0},{1,9},{9,17},{17,25},{25,1},{2,10},{10... | collective-permute-start | bytes 233480 | tf_op jit(solution)/shard_map/ppermute | solution.py:739
  14.9 5.5 %collective-permute-start.8 = (bf16[304,128]{1,0:T(8,128)(2,1)S(1)}, bf16[304,128]{1,0:T(8,128)(2,1)S(1)}, u32[]{:S(2)}, u32[]{:S(2)}) collective-permute-start(bf16[304,128]{1,0:T(8,128)(2,1)S(1)} %collective-permute-done.7.rest_5_), channel_id=1, source_target_pairs={{0,4},{4,0},{1,5},{5,1},{2,6},{6,2},{3,7},{7,3},{8,12},{12,8},{9,1... | collective-permute-start | bytes 233480 | tf_op jit(solution)/shard_map/ppermute | solution.py:739
  19.0 1.4 %collective-permute-start.6 = (bf16[304,128]{1,0:T(8,128)(2,1)S(1)}, bf16[304,128]{1,0:T(8,128)(2,1)S(1)}, u32[]{:S(2)}, u32[]{:S(2)}) collective-permute-start(bf16[304,128]{1,0:T(8,128)(2,1)S(1)} %collective-permute-done.5.rest_3_), channel_id=1, source_target_pairs={{0,4},{4,0},{1,5},{5,1},{2,6},{6,2},{3,7},{7,3},{8,12},{12,8},{9,1... | collective-permute-start | bytes 233480 | tf_op jit(solution)/shard_map/ppermute | solution.py:739
  19.0 1.4 %collective-permute-start.4 = (bf16[304,128]{1,0:T(8,128)(2,1)S(1)}, bf16[304,128]{1,0:T(8,128)(2,1)S(1)}, u32[]{:S(2)}, u32[]{:S(2)}) collective-permute-start(bf16[304,128]{1,0:T(8,128)(2,1)S(1)} %collective-permute-done.3.rest_1_), channel_id=1, source_target_pairs={{0,4},{4,0},{1,5},{5,1},{2,6},{6,2},{3,7},{7,3},{8,12},{12,8},{9,1... | collective-permute-start | bytes 233480 | tf_op jit(solution)/shard_map/ppermute | solution.py:739
  35.8 10.3 %collective-permute-start.9 = (bf16[9,3,16,128]{3,2,1,0:T(8,128)(2,1)S(1)}, bf16[9,3,16,128]{3,2,1,0:T(8,128)(2,1)S(1)}, u32[]{:S(2)}, u32[]{:S(2)}) collective-permute-start(bf16[9,3,16,128]{3,2,1,0:T(8,128)(2,1)S(1)} %get-tuple-element.86), channel_id=1, source_target_pairs={{0,1},{1,2},{2,3},{3,0},{4,5},{5,6},{6,7},{7,4},{8,9},{9,10},{10,1... | collective-permute-start | bytes 331784 | tf_op jit(solution)/shard_map/ppermute | solution.py:739
  36.2 9.9 %collective-permute-start.10 = (bf16[9,3,16,128]{3,2,1,0:T(8,128)(2,1)S(1)}, bf16[9,3,16,128]{3,2,1,0:T(8,128)(2,1)S(1)}, u32[]{:S(2)}, u32[]{:S(2)}) collective-permute-start(bf16[9,3,16,128]{3,2,1,0:T(8,128)(2,1)S(1)} %get-tuple-element.87), channel_id=1, source_target_pairs={{0,3},{1,0},{2,1},{3,2},{4,7},{5,4},{6,5},{7,6},{8,11},{9,8},{10,9... | collective-permute-start | bytes 331784 | tf_op jit(solution)/shard_map/ppermute | solution.py:739
  78.1 1.5 %copy-start.2 = (bf16[9,2,192,384]{3,2,1,0:T(8,128)(2,1)}, bf16[9,2,192,384]{3,2,1,0:T(8,128)(2,1)S(1)}, u32[]{:S(2)}) copy-start(bf16[9,2,192,384]{3,2,1,0:T(8,128)(2,1)S(1)} %get-tuple-element.102.g_inner) | copy-start | bytes 7962628
  79.6 1.6 %collective-permute-start.11 = (bf16[4,288,128]{2,1,0:T(8,128)(2,1)S(1)}, bf16[4,288,128]{2,1,0:T(8,128)(2,1)S(1)}, u32[]{:S(2)}, u32[]{:S(2)}) collective-permute-start(bf16[4,288,128]{2,1,0:T(8,128)(2,1)S(1)} %get-tuple-element.100), channel_id=1, source_target_pairs={{0,4},{4,0},{1,5},{5,1},{2,6},{6,2},{3,7},{7,3},{8,12},{12,8},{9,1... | collective-permute-start | bytes 884744 | tf_op jit(solution)/shard_map/ppermute | solution.py:739
  82.0 15.4 %all-to-all-start.3 = ((bf16[16,80,128]{2,1,0:T(8,128)(2,1)}), bf16[16,80,128]{2,1,0:T(8,128)(2,1)S(1)}, u32[]{:S(2)}, u32[]{:S(2)}) async-start(bf16[16,80,128]{2,1,0:T(8,128)(2,1)} %shard_map.182.refs_0_.after), calls=%async_computation.3 | async-start | bytes 655360 | tf_op jit(solution)/shard_map/all_to_all | solution.py:734
  85.5 1.1 %copy-start = (bf16[12,16,16,128]{3,2,1,0:T(8,128)(2,1)S(1)}, bf16[12,16,16,128]{3,2,1,0:T(8,128)(2,1)}, u32[]{:S(2)}) copy-start(bf16[12,16,16,128]{3,2,1,0:T(8,128)(2,1)} %refs_1_.2) | copy-start | bytes 2359300
  86.7 2.8 %copy-start.1 = (bf16[12,16,16,128]{3,2,1,0:T(8,128)(2,1)S(1)}, bf16[12,16,16,128]{3,2,1,0:T(8,128)(2,1)}, u32[]{:S(2)}) copy-start(bf16[12,16,16,128]{3,2,1,0:T(8,128)(2,1)} %cot.3) | copy-start | bytes 2359300
  86.7 2.8 %copy-start.3 = (bf16[9,2,192,384]{3,2,1,0:T(8,128)(2,1)S(1)}, bf16[9,2,192,384]{3,2,1,0:T(8,128)(2,1)}, u32[]{:S(2)}) copy-start(bf16[9,2,192,384]{3,2,1,0:T(8,128)(2,1)} %copy-done.2) | copy-start | bytes 7962628
  86.7 2.8 %copy-start.4 = (bf16[1536,256]{1,0:T(8,128)(2,1)S(1)}, bf16[1536,256]{1,0:T(8,128)(2,1)}, u32[]{:S(2)}) copy-start(bf16[1536,256]{1,0:T(8,128)(2,1)} %get-tuple-element.103.block) | copy-start | bytes 2359300
  98.0 2.6 %collective-permute-start.12 = (bf16[80,128]{1,0:T(8,128)(2,1)S(1)}, bf16[80,128]{1,0:T(8,128)(2,1)S(1)}, u32[]{:S(2)}, u32[]{:S(2)}) collective-permute-start(bf16[80,128]{1,0:T(8,128)(2,1)S(1)} %get-tuple-element.105.own), channel_id=1, source_target_pairs={{0,4},{4,0},{1,5},{5,1},{2,6},{6,2},{3,7},{7,3},{8,12},{12,8},{9,1... | collective-permute-start | bytes 61448 | tf_op jit(solution)/shard_map/ppermute | solution.py:739
  98.0 9.9 %all-to-all-start.4 = ((f32[32,2,128]{2,1,0:T(2,128)}), f32[32,2,128]{2,1,0:T(2,128)S(1)}, u32[]{:S(2)}, u32[]{:S(2)}) async-start(f32[32,2,128]{2,1,0:T(2,128)} %get-tuple-element.112), calls=%async_computation.4 | async-start | bytes 65536 | tf_op jit(solution)/shard_map/all_to_all | solution.py:734
  100.7 5.9 %collective-permute-start.15 = (bf16[144,128]{1,0:T(8,128)(2,1)S(1)}, bf16[144,128]{1,0:T(8,128)(2,1)S(1)}, u32[]{:S(2)}, u32[]{:S(2)}) collective-permute-start(bf16[144,128]{1,0:T(8,128)(2,1)S(1)} %shard_map.186.refs_6_), channel_id=1, source_target_pairs={{0,1},{1,2},{2,3},{3,0},{4,5},{5,6},{6,7},{7,4},{8,9},{9,10},{10,1... | collective-permute-start | bytes 110600 | tf_op jit(solution)/shard_map/ppermute | solution.py:739
  102.5 4.1 %collective-permute-start.14 = (bf16[144,128]{1,0:T(8,128)(2,1)S(1)}, bf16[144,128]{1,0:T(8,128)(2,1)S(1)}, u32[]{:S(2)}, u32[]{:S(2)}) collective-permute-start(bf16[144,128]{1,0:T(8,128)(2,1)S(1)} %shard_map.186.refs_6_), channel_id=1, source_target_pairs={{0,2},{1,3},{2,0},{3,1},{4,6},{5,7},{6,4},{7,5},{8,10},{9,11},{10,... | collective-permute-start | bytes 110600 | tf_op jit(solution)/shard_map/ppermute | solution.py:739
  103.9 4.0 %collective-permute-start.13 = (bf16[144,128]{1,0:T(8,128)(2,1)S(1)}, bf16[144,128]{1,0:T(8,128)(2,1)S(1)}, u32[]{:S(2)}, u32[]{:S(2)}) collective-permute-start(bf16[144,128]{1,0:T(8,128)(2,1)S(1)} %shard_map.186.refs_6_), channel_id=1, source_target_pairs={{0,3},{1,0},{2,1},{3,2},{4,7},{5,4},{6,5},{7,6},{8,11},{9,8},{10,9... | collective-permute-start | bytes 110600 | tf_op jit(solution)/shard_map/ppermute | solution.py:739

commit v3 on v2

--- a/solution.py
+++ b/solution.py
@@ -151,6 +151,18 @@
     ref[...] = jnp.broadcast_to(block[None], ref.shape)
 
 
+def put_pairs(ref, rows):
+    for g in range(ref.shape[1]):
+        part = jnp.concatenate(rows[2 * g : 2 * g + 2], axis=0)
+        for n in range(ref.shape[0]):
+            ref[n, g] = part
+
+
+def got_pairs(ref):
+    total = jnp.sum(ref[...], axis=0)
+    return [total[g, i : i + 1] for g in range(total.shape[0]) for i in range(2)]
+
+
 def taken(ref, count):
     return [ref[i : i + 1, :] for i in range(count)]
 
@@ -211,6 +223,24 @@
     return [
         got[n * rows : n * rows + rows, a * C : a * C + C] for n in range(high - low) for a in range(2)
     ]
+
+
+def staggered(make, conv, rows, groups):
+    total, done = None, 0
+    stops = [min(2 * high + 1, rows) for _, high in groups]
+    for n, (low, high) in enumerate(groups):
+        for row in range(done, stops[n]):
+            make(row)
+        done = max(done, stops[n])
+        total = conv(low, high, total)
+        for row in range(done, stops[min(n + 1, len(groups) - 1)]):
+            make(row)
+        done = stops[min(n + 1, len(groups) - 1)]
+    return total
+
+
+def in_pairs(high):
+    return [(low, min(low + 2, high)) for low in range(0, high, 2)]
 
 
 def added(total, new):
@@ -285,13 +315,21 @@
     cut_far(lambda q, n: cot_beyond(lat_in, n, q), far_r, far_l, R // 2, 2, 2)
 
 
-def shift_kernel(x, lat_in, from_left, from_right, out, *flats):
+def own_tile(x, lat_in, row):
+    if row < R:
+        return lambda n: x[n, own_row(row)]
+    return lambda n: x_beyond(lat_in, n, row - R)
+
+
+def first_kernel(x, lat_in, from_left, from_right, block, vec, out, pre, sums, *flats):
     for edge in (0, R + 5):
         out[edge // 2, edge % 2] = jnp.zeros((TI, W3), BF16)
-
-    def one(flat, tile, at, place):
+    bias = vec[0:1, :]
+
+    def make(row):
+        flat, place, tile = flats[row % 2], place_of(row // 2, row % 2), own_tile(x, lat_in, row)
         for m in range(MB):
-            left, right = from_left[at, m].astype(F32), from_right[at, m].astype(F32)
+            left, right = from_left[row, m].astype(F32), from_right[row, m].astype(F32)
             for n in range(PER):
                 s = PER * m + n
                 flat[15 + 24 * s : 16 + 24 * s, :] = left[4 * n + 3 : 4 * n + 4]
@@ -302,14 +340,17 @@
             out[place + (slice(16 * n, 16 * n + 16), slice(C, 2 * C))] = value
         emit_sides(flat, out, place)
 
-    @pl.loop(0, R // 2)
-    def _(i):
-        for odd in range(2):
-            source = own_row(2 * i + odd)
-            one(flats[odd], lambda n: x[n, source], 2 * i + odd, place_of(i, odd))
-
-    for k in range(4):
-        one(flats[k % 2], lambda n: x_beyond(lat_in, n, k), R + k, place_of((R + k) // 2, k % 2))
+    def conv(low, high, total):
+        for n, v in enumerate(conv_rows(out, low, high, block[...], TI)):
+            row = 2 * low + n
+            pre[row] = v + bias
+            if row < R:
+                value = act(v + bias)
+                total = added(total, batch_sums(value) + batch_sums(value * value))
+        return total
+
+    total = staggered(make, conv, R + 4, in_pairs(R // 2 + 2))
+    put_pairs(sums, [down(v) for v in total])
 
 
 def halo_kernel(after, x, lat_in, from_left, from_right, block, vec, pre, halo, *flats):
@@ -318,7 +359,8 @@
     for edge in (0, R + 5):
         halo[edge // 2, edge % 2] = jnp.zeros((TH, W3), BF16)
 
-    def one(flat, tile, row, place):
+    def make(row):
+        flat, place, tile = flats[row % 2], place_of(row // 2, row % 2), own_tile(x, lat_in, row)
         for m in range(MB):
             left, right = from_left[row, m].astype(F32), from_right[row, m].astype(F32)
             for n in range(PER):
@@ -336,16 +378,12 @@
                     [flat[at : at + 8, :], second], axis=0
                 ).astype(BF16)
 
-    @pl.loop(0, R // 2)
-    def _(i):
-        for odd in range(2):
-            source = own_row(2 * i + odd)
-            one(flats[odd], lambda n: x[n, source], 2 * i + odd, place_of(i, odd))
-
-    for k in range(4):
-        one(flats[k % 2], lambda n: x_beyond(lat_in, n, k), R + k, place_of((R + k) // 2, k % 2))
-    for row, v in enumerate(conv_rows(halo, 0, R // 2 + 2, block[...], TH)):
-        pre[row] = v + vec[0:1, :]
+    def conv(low, high, total):
+        for n, v in enumerate(conv_rows(halo, low, high, block[...], TH)):
+            pre[2 * low + n] = v + vec[0:1, :]
+        return total
+
+    staggered(make, conv, R + 4, ((0, 3), (3, 6), (6, 10)))
 
 
 def lead_scales(lead):
@@ -406,31 +444,15 @@
 
 
 def weight_kernel(after, block_one, *rest):
-    pieces, (block_two, two_back, one_far, one_back, sem) = rest[:-5], rest[-5:]
-    fill_backward(one_back, block_one)
-    copy = pltpu.make_async_copy(one_back, one_far, sem)
-    copy.start()
+    pieces, (block_two, two_back, one_back) = rest[:-3], rest[-3:]
     fill_forward(block_two, pieces, 1)
     fill_backward(two_back, block_two)
-    copy.wait()
-
-
-def first_kernel(x_all, block, vec, pre, sums):
-    bias = vec[0:1, :]
-    total = None
-    for low, high in ((0, 4), (4, 8), (8, 10)):
-        for n, v in enumerate(conv_rows(x_all, low, high, block[...], TI)):
-            row = 2 * low + n
-            pre[row] = v + bias
-            if row < R:
-                value = act(v + bias)
-                total = added(total, batch_sums(value) + batch_sums(value * value))
-    put_all(sums, [down(v) for v in total] + [jnp.zeros((2, C), F32)])
+    fill_backward(one_back, block_one)
 
 
 def second_kernel(count, pre, pre_side, sums_in, dn, dn_sums, block, vec_in, n_all, pre_two, sums, kept, *flats):
     vec = vec_rows(vec_in)
-    kept[...] = jnp.sum(sums_in[...], axis=0)
+    kept[...] = jnp.concatenate(got_pairs(sums_in) + [jnp.zeros((2, C), F32)], axis=0)
     means, inverses = norm_of(taken(kept, 2 * MB), count)
     gains = [inverses[m] * vec[1] for m in range(MB)]
     gain, gain_side = sided(gains)
@@ -449,14 +471,7 @@
             lambda h: act(pre_side[row, 8 * h : 8 * h + 8, :]) * gain_side(h) + shift_side(h),
         )
 
-    @pl.loop(0, R // 2 + 1)
-    def _(i):
-        for odd in range(2):
-            one(i, odd)
-
-    one(R // 2 + 1, 0)
-    total = None
-    for low, high in ((0, 5), (5, 9)):
+    def conv(low, high, total):
         for n, v in enumerate(conv_rows(n_all, low, high, block[...])):
             row = 2 * low + n
             pre_two[row] = v + vec[3]
@@ -464,6 +479,9 @@
                 value = act(v[:TI] + vec[3])
                 new = batch_sums(value) + batch_sums(value * value) + batch_sums(value * dn[row])
                 total = added(total, new)
+        return total
+
+    total = staggered(lambda row: one(row // 2, row % 2), conv, R + 3, in_pairs(R // 2 + 1))
     block_out = jnp.concatenate([down(v) for v in total] + [dn_sums[0:MB, :]], axis=0)
     for g in range(3):
         part = block_out[4 * g : 4 * g + 4]
@@ -496,7 +514,7 @@
 
 
 def back_two_kernel(
-    count, pre_two, dn, dn_lat, dn_side, sums_in, pre, block, vec, grad, mid, sums, kept, g_all, *flats
+    count, pre_two, dn, dn_lat, dn_side, sums_in, pre, block, vec, grad, mid, sums, kept, bias_two, g_all, *flats
 ):
     total = jnp.sum(sums_in[...], axis=0)
     kept[...] = jnp.concatenate([total[g, i : i + 1] for g in range(MB) for i in range(4)], axis=0)
@@ -519,27 +537,31 @@
             lambda h: dn_side[row, 8 * h : 8 * h + 8, :],
         )
 
-    def body(i, total):
-        for odd in range(2):
-            place = place_of(i, odd)
-            make(odd, place, 2 * i + odd, dn, 2 * i + odd)
+    biases = []
+
+    def row_of(row):
+        place = place_of(row // 2, row % 2)
+        if row < R:
+            make(row % 2, place, row, dn, row)
             own = g_all[place + (slice(0, TI), slice(C, 2 * C))]
-            grad[2 * i + odd] = own
-            total = total + fold(own.astype(F32))
-        return total
-
-    bias = lax.fori_loop(0, R // 2, body, jnp.zeros((8, C), F32))
-    for odd in range(2):
-        make(odd, place_of(R // 2, odd), R + odd, dn_lat, odd)
-    total = None
-    for low, high in ((0, 5), (5, 9)):
+            grad[row] = own
+            biases.append(fold(own.astype(F32)))
+        else:
+            make(row % 2, place, row, dn_lat, row - R)
+
+    def conv(low, high, total):
         for n, v in enumerate(conv_rows(g_all, low, high, block[...])):
             row = 2 * low + n
             mid[row] = v
             if row < R:
                 own = v[:TI]
                 total = added(total, batch_sums(own) + batch_sums(own * act(pre[row])))
-    put_all(sums, [down(v) for v in total] + [down(bias), jnp.zeros((1, C), F32)])
+        return total
+
+    total = staggered(row_of, conv, R + 2, in_pairs(R // 2 + 1))
+    bias = sum(biases)
+    put_pairs(sums, [down(v) for v in total])
+    bias_two[...] = jnp.concatenate([down(bias), jnp.zeros((7, C), F32)], axis=0)
 
 
 def wgrad_add(acc, inner, grad, low, high):
@@ -591,16 +613,16 @@
 
 def first_back_stats(first_in, sums_in, count):
     means, inverses = norm_of(taken(first_in, 2 * MB), count)
-    rows = taken(sums_in, 2 * MB + 1)
+    rows = taken(sums_in, 2 * MB)
     dshift = rows[:MB]
     dgain = [inverses[m] * (rows[MB + m] - means[m] * dshift[m]) for m in range(MB)]
-    return means, inverses, dgain, dshift, rows[2 * MB]
-
-
-def back_one_kernel(split, count, pre, pre_side, mid, first_in, sums_in, x_all, n_all, grad_two, vec, g_inner, bias, kept, *rest):
+    return means, inverses, dgain, dshift
+
+
+def back_one_kernel(split, count, pre, pre_side, mid, first_in, sums_in, x_all, n_all, grad_two, bias_two, vec, g_inner, bias, kept, *rest):
     outs, (acc_one, acc_two), flats = rest[:-4], rest[-4:-2], rest[-2:]
-    kept[...] = jnp.sum(sums_in[...], axis=0)
-    means, inverses, dgain, dshift, _ = first_back_stats(first_in, kept, count)
+    kept[...] = jnp.concatenate(got_pairs(sums_in) + [jnp.zeros((2, C), F32)], axis=0)
+    means, inverses, dgain, dshift = first_back_stats(first_in, kept, count)
     terms = back_terms(means, inverses, vec[1:2, :], dgain, dshift, count)
     for flat in flats:
         flat[...] = jnp.zeros(flat.shape, F32)
@@ -622,18 +644,22 @@
         return g_inner[(row + 1) // 2, (row + 1) % 2, :, C : 2 * C]
 
     total = jnp.zeros((8, C), F32)
-    for n in range(4):
-        for row in range(4 * n, 4 * n + 4):
-            make(row)
+    for row in range(R + 1):
+        make(row)
+        if row < R:
             total = total + fold(made(row).astype(F32))
-        wgrad_add(acc_two, n_all, lambda row: grad_two[row], 4 * n, 4 * n + 4)
-        if n > 0:
-            wgrad_add(acc_one, x_all, made, 4 * n - 4, 4 * n)
-    make(R)
-    wgrad_add(acc_one, x_all, made, R - 4, R)
+    for low in range(0, R, 4):
+        wgrad_add(acc_two, n_all, lambda row: grad_two[row], low, low + 4)
+        wgrad_add(acc_one, x_all, made, low, low + 4)
     bias[...] = jnp.concatenate([down(total), jnp.zeros((7, C), F32)], axis=0)
     (split_out if split else plain_out)(acc_two, 1, *outs)
     (split_out if split else plain_out)(acc_one, 0, *outs)
+    if split:
+        keep, send = outs
+        parts = jnp.concatenate(two_of(down(total)) + two_of(bias_two[0:1, :]) + [jnp.zeros((12, C), F32)], axis=0)
+        for d in range(4):
+            keep[d, 288:, :] = parts
+            send[d, 288:, :] = parts.astype(BF16)
 
 
 def input_grad_kernel(lead, after, g_inner, cot, block, out):
@@ -645,28 +671,40 @@
             out[n, source] = (v[16 * n : 16 * n + 16] + incoming).astype(BF16)
 
 
-def merge_kernel(keep, got, out):
-    for d in range(4):
+def two_of(v):
+    high = v.astype(BF16).astype(F32)
+    return [high, (v - high).astype(BF16).astype(F32)]
+
+
+def bias_rows(total):
+    return total[288:289] + total[289:290], total[290:291] + total[291:292]
+
+
+def message(total):
+    one, two = bias_rows(total)
+    tail = two_of(one) + two_of(two) + [jnp.zeros((12, C), F32)]
+    return jnp.concatenate([total[:288]] + tail, axis=0).astype(BF16)
+
+
+def merge_kernel(keep, got, *outs):
+    for k, out in enumerate(outs):
+        d = lax.rem(lax.axis_index("dp") + k, 4)
         total = keep[d] + got[d].astype(F32)
-        for n in range(4):
-            parts = [total[144 * k + 36 * n : 144 * k + 36 * n + 36] for k in range(2)]
-            out[4 * d + n] = jnp.concatenate(parts + [jnp.zeros((8, C), F32)], axis=0).astype(BF16)
-
-
-def owned_kernel(outputs, grad_inputs, parts, bias, chunk, sums):
-    total = parts[0].astype(F32)
-    for n in range(1, parts.shape[0]):
-        total = total + parts[n].astype(F32)
-    own = total[:72]
-    chunk[...] = total.astype(BF16)
-    put_all(sums, [down(fold(own * own)), bias[0:1, :]])
-
-
-def pair_kernel(own, other, out):
-    first = lax.axis_index("lat") == 0
-    mine, its = own[...].astype(F32), other[...].astype(F32)
-    low, high = jnp.where(first, mine[:72], its[:72]), jnp.where(first, its[:72], mine[:72])
-    out[...] = jnp.concatenate([low, high], axis=0).astype(BF16)
+        out[...] = message(total)
+
+
+def column_kernel(*refs):
+    total = sum(ref[...].astype(F32) for ref in refs[:-1])
+    refs[-1][...] = message(total)
+
+
+def plane_kernel(outputs, grad_inputs, *refs):
+    parts, (own, sums, slots) = refs[:4], refs[4:]
+    for n, part in enumerate(parts):
+        slots[lax.rem(lax.axis_index("lon") + (4 - n), 4)] = part[...].astype(F32)
+    total = sum(slots[n] for n in range(4))
+    own[...] = total[:288]
+    put_all(sums, [down(fold(total[:288] * total[:288])), *bias_rows(total), jnp.zeros((1, C), F32)])
 
 
 def fetch_kernel(*refs):
@@ -687,36 +725,33 @@
     return weight_new, first_new, second_new
 
 
-def vector_grads(first_in, second_in, third_in, bias_one, count):
+def vector_grads(first_in, second_in, third_in, bias_one, bias_two, count):
     _, _, dgain_two, dshift_two = second_stats(second_in, count)
-    _, _, dgain_one, dshift_one, bias_two = first_back_stats(first_in, third_in, count)
+    _, _, dgain_one, dshift_one = first_back_stats(first_in, third_in, count)
     rows = [bias_one, sum(dgain_one), sum(dshift_one), bias_two, sum(dgain_two), sum(dshift_two)]
     return jnp.concatenate(rows, axis=0)
 
 
 def update_kernel(count, *refs):
     weight, first, second, vectors, vec_first, vec_second = refs[:6]
-    chunks, (sums_in, first_in, second_in, third_in), refs = refs[6:10], refs[10:14], refs[14:]
+    (mine, its), (sums_in, first_in, second_in, third_in), refs = refs[6:8], refs[8:12], refs[12:]
     norm_out, weight_new, first_new, second_new, weight_low, vectors_new, vec_first_new, vec_second_new = refs[:8]
-    slab, grad = refs[8:]
+    grad = refs[8]
     total = jnp.sum(sums_in[...], axis=0)
-    vec_grad = vector_grads(first_in, second_in, third_in, total[1:2], count)
+    half = sums_in[0]
+    vec_grad = vector_grads(first_in, second_in, third_in, half[1:2], half[2:3], count)
     square = jnp.sum(total[0:1], axis=1, keepdims=True) + jnp.sum(
         down(vec_grad * vec_grad), axis=1, keepdims=True
     )
     norm = jnp.sqrt(square)
     norm_out[...] = norm
     clip = jnp.minimum(1.0, CLIP / (norm + 1e-06))
-    for n, chunk in enumerate(chunks):
-        at = pl.ds(36 * lax.rem(lax.axis_index("lon") + n, 4), 36)
-        part = chunk[...].astype(F32)
-        for lat in range(2):
-            for k in range(2):
-                slab[k, lat, at, :] = part[72 * lat + 36 * k : 72 * lat + 36 * k + 36]
+    core = lax.axis_index("lat")
     for k in range(2):
         for lat in range(2):
             for t in range(9):
-                grad[k, pl.ds(144 * lat + t, 16, stride=9), :] = slab[k, lat, 16 * t : 16 * t + 16, :]
+                at = slice(144 * k + 16 * t, 144 * k + 16 * t + 16)
+                grad[k, pl.ds(144 * lat + t, 16, stride=9), :] = jnp.where(core == lat, mine[at, :], its[at, :])
         new = adam(weight[k], first[k], second[k], grad[k] * clip, RATE_CONV, DECAY_CONV)
         weight_new[k], first_new[k], second_new[k] = new
         weight_low[k] = new[0].astype(BF16)
@@ -774,27 +809,26 @@
         aliases={2: 1, 3: 2},
     )
     far_left, far_right = turn(far_r, "lon", 1), turn(far_l, "lon", -1)
+    dn, dn_sums = call(
+        lead_kernel, [((R, TI, C), F32), ((8, C), F32)], (lead_time, cot_near), flops=10**8, scalars=1
+    )
     if split:
+        fetched = [turn(mine, "dp", k) for k in range(1, groups)]
+        *fetched, dn = lax.optimization_barrier((*fetched, dn))
         pieces = [packed]
-        for k in range(1, groups):
-            fetched = turn(mine, "dp", k)
-            pieces += [fetched, turn(fetched, "lat", 1)]
+        for piece in fetched:
+            pieces += [piece, turn(piece, "lat", 1)]
     else:
         whole = lax.all_gather(packed, "dp")
         taps = whole[:, :, : 9 * size].reshape(groups, 2, 9, size, C).transpose(1, 2, 0, 3, 4)
         tail = jnp.sum(whole[:, :, 9 * size :], axis=0)
         pieces = [jnp.concatenate([taps.reshape(2, 9 * C, C), tail], axis=1)]
-    dn, dn_sums = call(
-        lead_kernel, [((R, TI, C), F32), ((8, C), F32)], (lead_time, cot_near), flops=10**8, scalars=1
-    )
-    (x_all,) = call(
-        shift_kernel, [((11, 2, TI, W3), BF16)], (x_near, lat_in, far_left, far_right), flats, flops=10**8
-    )
     block_one, vec = call(block_kernel, [((12 * C, 2 * C), BF16), ((16, C), F32)], pieces, flops=10**8)
-    pre_one, sums_one = call(
+    x_all, pre_one, sums_one = call(
         first_kernel,
-        [((R + 4, TI, C), F32), ((devices, 8, C), F32)],
-        (x_all, block_one, vec),
+        [((11, 2, TI, W3), BF16), ((R + 4, TI, C), F32), ((devices, MB, 2, C), F32)],
+        (x_near, lat_in, far_left, far_right, block_one, vec),
+        flats,
         flops=conv_flops * 6,
     )
     sums_one, dn = lax.optimization_barrier((sums_one, dn))
@@ -803,9 +837,7 @@
         weight_kernel,
         [((12 * C, 2 * C), BF16)] * 3,
         (got_one, block_one, *pieces),
-        [pltpu.VMEM((12 * C, 2 * C), BF16), pltpu.SemaphoreType.DMA(())],
         flops=10**8,
-        far_out=(2,),
     )
     (pre_side,) = call(
         halo_kernel,
@@ -835,19 +867,19 @@
     )
     sums_two, dn_lat, dn_side = lax.optimization_barrier((sums_two, dn_lat, dn_side))
     got_two = spread(sums_two, ALL)
-    grad_two, mid, sums_three, stat_two = call(
+    grad_two, mid, sums_three, stat_two, bias_two = call(
         lambda *refs: back_two_kernel(count, *refs),
-        [((R, TI, C), BF16), ((R + 2, T, C), F32), ((devices, 8, C), F32), ((4 * MB, C), F32)],
+        [((R, TI, C), BF16), ((R + 2, T, C), F32), ((devices, MB, 2, C), F32), ((4 * MB, C), F32), ((8, C), F32)],
         (pre_two, dn, dn_lat, dn_side, got_two, pre_one, two_back, vec),
         [pltpu.VMEM((10, 2, T, W3), BF16)] + flats,
         flops=conv_flops * 9,
     )
     got_three = spread(sums_three, ALL)
-    grad_kinds = [((4, 288, C), F32), ((4, 288, C), BF16)] if split else [((2, 9, C, C), F32)]
+    grad_kinds = [((4, 304, C), F32), ((4, 304, C), BF16)] if split else [((2, 9, C, C), F32)]
     g_inner, bias_one, stat_three, *grads = call(
         lambda *refs: back_one_kernel(split, count, *refs),
         [((9, 2, TI, W3), BF16), ((8, C), F32), ((8, C), F32)] + grad_kinds,
-        (pre_one, pre_side, mid, stat_one, got_three, x_all, n_all, grad_two, vec),
+        (pre_one, pre_side, mid, stat_one, got_three, x_all, n_all, grad_two, bias_two, vec),
         [pltpu.VMEM((3, C, W3), F32)] * 2 + flats,
         flops=conv_flops * 9,
     )
@@ -869,24 +901,26 @@
         return outputs, grad_inputs
 
     if split:
-        (merged,) = call(merge_kernel, [((16, 80, C), BF16)], (grads[0], turn(grads[1], "lat", 1)))
-        parts = spread(merged, ("dp", "lon"))
-        outputs, grad_inputs = finish(merged)
-        chunk, sums_four = call(
-            owned_kernel,
-            [((80, C), BF16), ((devices, 2, C), F32)],
-            (outputs, grad_inputs, parts, bias_one),
+        merged = call(merge_kernel, [((304, C), BF16)] * 4, (grads[0], turn(grads[1], "lat", 1)))
+        column = [merged[0]] + [turn(merged[k], "dp", k) for k in range(1, 4)]
+        outputs, grad_inputs = finish(merged[0])
+        (added_up,) = call(column_kernel, [((304, C), BF16)], column)
+        row = [added_up] + [turn(added_up, "lon", k) for k in range(1, 4)]
+        own, sums_four = call(
+            plane_kernel,
+            [((288, C), F32), ((2 * groups, 4, C), F32)],
+            (outputs, grad_inputs, *row),
+            [pltpu.VMEM((4, 304, C), F32)],
             far=2,
         )
-        got_four = spread(sums_four, ALL)
-        (pair,) = call(pair_kernel, [((144, C), BF16)], (chunk, turn(chunk, "lat", 1)), flops=10**10)
-        chunks = [pair] + [turn(pair, "lon", -k) for k in range(1, 4)]
+        got_four = spread(sums_four, ("dp", "lat"))
+        its = turn(own, "lat", 1)
         kinds = [((1, 1), F32)] + [(conv_weight.shape, F32)] * 3 + [(conv_weight.shape, BF16)]
         moments = (conv_weight, conv_first, conv_second, vectors, vec_first, vec_second)
         moments = call(
             fetch_kernel,
             [(moment.shape, F32) for moment in moments],
-            (*moments, pair),
+            (*moments, own),
             [pltpu.SemaphoreType.DMA((6,))],
             flops=10**10,
             far=6,
@@ -894,14 +928,14 @@
         norm, *news = call(
             lambda *refs: update_kernel(count, *refs),
             kinds + [(vectors.shape, F32)] * 3,
-            (*moments, *chunks, got_four, stat_one, stat_two, stat_three),
-            [pltpu.VMEM((2, 2, 144, C), F32), pltpu.VMEM(conv_weight.shape, F32)],
+            (*moments, own, its, got_four, stat_one, stat_two, stat_three),
+            [pltpu.VMEM(conv_weight.shape, F32)],
         )
         return (outputs, grad_inputs, norm.reshape(()), *news)
     outputs, grad_inputs = finish(bias_one)
     stacked = grads[0].transpose(0, 2, 1, 3).reshape(2, 9 * C, C)
-    conv_total, bias_total = lax.psum((stacked, bias_one[0:1]), ALL)
-    vec_total = vector_grads(stat_one, stat_two, stat_three, bias_total, count)
+    conv_total, total_one, total_two = lax.psum((stacked, bias_one[0:1], bias_two[0:1]), ALL)
+    vec_total = vector_grads(stat_one, stat_two, stat_three, total_one, total_two, count)
     grad_norm = jnp.sqrt(jnp.sum(conv_total * conv_total) + jnp.sum(vec_total * vec_total))
     clip = jnp.minimum(1.0, CLIP / (grad_norm + 1e-06))
     index = lax.axis_index("dp")

time: 110 us -> 104 us (0.945)
  Pallas kernels: 33.9 us -> 28.8 us
  waiting for transfers between devices: 14.4 us -> 18.9 us
  local copies, waits for them, and re-layouts: 2.62 us -> 0.01 us
  blocking collectives: 33.7 us -> 32.4 us
    ppermute x16 -> x19, waiting for transfers between devices: 9.82 us -> 15 us  [turn(): lax.ppermute(block, axis, [(i, (i + by) % size) for i in range(size)])]
    pallas_call x21 -> x20, Pallas kernels: 33.9 us -> 28.8 us  [call(): pl.pallas_call(kernel, out_shape=tuple((pltpu.HBM(shape, kind) if n in fa...]
    all_to_all x2 -> x1, starting transfers between devices: 6.11 us -> 3.34 us  [spread(): return lax.all_to_all(block, axes, 0, 0, tiled=True)]
    unnamed x12 -> x6, local copies, waits for them, and re-layouts: 2.62 us -> 0.01 us
    ppermute x16 -> x19, starting transfers between devices: 17.7 us -> 19.7 us  [turn(): lax.ppermute(block, axis, [(i, (i + by) % size) for i in range(size)])]
    all_to_all x3, blocking collectives: 33.7 us -> 32.4 us  [spread(): return lax.all_to_all(block, axes, 0, 0, tiled=True)]
    all_to_all x2 -> x1, waiting for transfers between devices: 4.6 us -> 3.98 us  [spread(): return lax.all_to_all(block, axes, 0, 0, tiled=True)]
  transfers between devices with their start and end apart: 18 -> 20, of which waited for: 6 -> 12; matrix products, arithmetic and copies ran while one was open for 0% -> 0% of each run, Pallas kernels for 14% -> 12%
where the time goes in v3:
time: 104 us
  blocking collectives  32.4 us (31%)
  Pallas kernels  28.8 us (28%)
  starting transfers between devices  23 us (22%)
  waiting for transfers between devices  18.9 us (18%)
    all_to_all x3, blocking collectives, spread(): return lax.all_to_all(block, axes, 0, 0, tiled=True)  32.4 us
    pallas_call x20, Pallas kernels, call(): pl.pallas_call(kernel, out_shape=tuple((pltpu.HBM(shape, kind) if n in fa...  28.8 us
    ppermute x19, starting transfers between devices, turn(): lax.ppermute(block, axis, [(i, (i + by) % size) for i in range(size)])  19.7 us
    ppermute x19, waiting for transfers between devices, turn(): lax.ppermute(block, axis, [(i, (i + by) % size) for i in range(size)])  15 us
    all_to_all x1, waiting for transfers between devices, spread(): return lax.all_to_all(block, axes, 0, 0, tiled=True)  3.98 us
    all_to_all x1, starting transfers between devices, spread(): return lax.all_to_all(block, axes, 0, 0, tiled=True)  3.34 us
  transfers between devices with their start and end apart: 20, of which 12 were waited for; matrix products, arithmetic and copies ran while one was open for 0% of the time, Pallas kernels for 12%

profile of v3, /device:TPU:0, one launch (start us, length us, event | category | flops | bytes accessed | tf_op | source)
XLA Modules:
  0.0 104.0 jit_solution(3109738912682601666)
XLA Ops:
  0.7 1.7 %shard_map.168 = (bf16[2,304,128]{2,1,0:T(8,128)(2,1)S(1)}, bf16[12,6,16,128]{3,2,1,0:T(8,128)(2,1)S(1)}, bf16[12,16,16,128]{3,2,1,0:T(8,128)(2,1)S(1)}, bf16[12,16,16,128]{3,2,1,0:T(8,128)(2,1)S(1)}) custom-call(bf16[12,16,16,128]{3,2,1,0:T(8,128)(2,1)} %refs_1_.2, bf16[12,16,16,128]{3,2,1,0:T(8,128)(2,1)} %cot.3, f32[2,288,128]{2,1,0:T(8,128)} %refs_0_.1, ...), custom_call_target="tpu_custom_call" | custom-call | bytes 1868544 | tf_op jit(solution)/shard_map/pallas_call | solution.py:45
  2.3 0.5 collective-permute-start
  2.9 0.2 shard_map.169
  3.1 1.0 collective-permute-done.lat_in
  4.1 2.9 %collective-permute-start.1 = (bf16[20,3,16,128]{3,2,1,0:T(8,128)(2,1)S(1)}, bf16[20,3,16,128]{3,2,1,0:T(8,128)(2,1)S(1)}, u32[]{:S(2)}, u32[]{:S(2)}) collective-permute-start(bf16[20,3,16,128]{3,2,1,0:T(8,128)(2,1)S(1)} %get-tuple-element.80), channel_id=1, source_target_pairs={{0,1},{1,2},{2,3},{3,0},{4,5},{5,6},{6,7},{7,4},{8,9},{9,10},{10,1... | collective-permute-start | bytes 737288 | tf_op jit(solution)/shard_map/ppermute | solution.py:774
  7.0 1.0 collective-permute-start.2
  8.0 4.0 %collective-permute-start.5 = (bf16[304,128]{1,0:T(8,128)(2,1)S(1)}, bf16[304,128]{1,0:T(8,128)(2,1)S(1)}, u32[]{:S(2)}, u32[]{:S(2)}) collective-permute-start(bf16[304,128]{1,0:T(8,128)(2,1)S(1)} %get-tuple-element.82), channel_id=1, source_target_pairs={{0,24},{8,0},{16,8},{24,16},{1,25},{9,1},{17,9},{25,17},{2,26},{10... | collective-permute-start | bytes 233480 | tf_op jit(solution)/shard_map/ppermute | solution.py:774
  12.1 0.0 collective-permute-start.4
  12.1 1.0 collective-permute-start.3
  13.1 0.0 copy-done.2
  13.1 0.9 shard_map.171
  13.9 0.9 collective-permute-done.5.rest_5_
  14.9 4.2 %collective-permute-done.4.rest_3_ = bf16[304,128]{1,0:T(8,128)(2,1)S(1)} collective-permute-done((bf16[304,128]{1,0:T(8,128)(2,1)S(1)}, bf16[304,128]{1,0:T(8,128)(2,1)S(1)}, u32[]{:S(2)}, u32[]{:S(2)}) %collective-permute-start.4) | collective-permute-done | bytes 77856 | tf_op jit(solution)/shard_map/ppermute | solution.py:774
  19.0 0.0 collective-permute-done.3.rest_1_
  19.0 0.0 collective-permute-start.6
  19.0 0.5 collective-permute-start.7
  19.5 0.0 collective-permute-start.8
  19.5 0.8 collective-permute-done.6.rest_2_
  20.3 0.2 collective-permute-done.7.rest_4_
  20.5 0.4 collective-permute-done.8.rest_6_
  20.8 0.1 shard_map.172
  20.9 0.0 collective-permute-done.1.from_left
  21.0 0.0 collective-permute-done.2.from_right
  21.0 2.5 %shard_map.173 = (bf16[11,2,192,384]{3,2,1,0:T(8,128)(2,1)S(1)}, f32[20,192,128]{2,1,0:T(8,128)S(1)}, f32[32,3,2,128]{3,2,1,0:T(2,128)S(1)}) custom-call(bf16[12,16,16,128]{3,2,1,0:T(8,128)(2,1)S(1)} %get-tuple-element.75.x, bf16[12,6,16,128]{3,2,1,0:T(8,128)(2,1)S(1)} %collective-permute-done.lat_in, ...), custom_call_target="tpu_custom_call" | custom-call | flops 1434451968 | bytes 2367488 | tf_op jit(solution)/shard_map/pallas_call | solution.py:45
  23.5 11.4 %all_to_all.20.after.refs_2_ = f32[32,3,2,128]{3,2,1,0:T(2,128)S(1)} all-to-all(f32[32,3,2,128]{3,2,1,0:T(2,128)S(1)} %get-tuple-element.93), channel_id=1, replica_groups=mesh['dp'=4,'lat'=2,'lon'=4] {'dp','lat','lon'}, dimensions={0} | all-to-all | bytes 196608 | tf_op jit(solution)/shard_map/all_to_all | solution.py:769
  34.9 0.3 shard_map.177
  35.2 0.4 collective-permute-start.9
  35.6 2.5 %collective-permute-start.10 = (bf16[9,3,16,128]{3,2,1,0:T(8,128)(2,1)S(1)}, bf16[9,3,16,128]{3,2,1,0:T(8,128)(2,1)S(1)}, u32[]{:S(2)}, u32[]{:S(2)}) collective-permute-start(bf16[9,3,16,128]{3,2,1,0:T(8,128)(2,1)S(1)} %get-tuple-element.100), channel_id=1, source_target_pairs={{0,3},{1,0},{2,1},{3,2},{4,7},{5,4},{6,5},{7,6},{8,11},{9,8},{10,9... | collective-permute-start | bytes 331784 | tf_op jit(solution)/shard_map/ppermute | solution.py:774
  38.2 1.4 %shard_map.174.refs_1_ = f32[20,112,128]{2,1,0:T(8,128)S(1)} custom-call(f32[32,3,2,128]{3,2,1,0:T(2,128)S(1)} %all_to_all.20.after.refs_2_, bf16[12,16,16,128]{3,2,1,0:T(8,128)(2,1)S(1)} %get-tuple-element.75.x, bf16[12,6,16,128]{3,2,1,0:T(8,128)(2,1)S(1)} %collective-permute-done.lat_in, bf16[20,3,16,128]{3,2,1,0:T(8,128)(2,1)S(1)} %collective-permute-done.1.from_left, ...), custom_call_target="tpu_custom_call" | custom-call | flops 956301312 | bytes 2465792 | tf_op jit(solution)/shard_map/pallas_call | solution.py:45
  39.6 0.4 shard_map.175
  40.0 3.5 %shard_map.176 = (bf16[10,2,304,384]{3,2,1,0:T(8,128)(2,1)S(1)}, f32[18,304,128]{2,1,0:T(8,128)S(1)}, f32[32,3,4,128]{3,2,1,0:T(4,128)S(1)}, f32[8,128]{1,0:T(8,128)S(1)}) custom-call(f32[20,192,128]{2,1,0:T(8,128)S(1)} %get-tuple-element.90.refs_0_.refs_5_, f32[20,112,128]{2,1,0:T(8,128)S(1)} %shard_map.174.refs_1_, ...), custom_call_target="tpu_custom_call" | custom-call | flops 2151677952 | bytes 5582848 | tf_op jit(solution)/shard_map/pallas_call | solution.py:45
  43.5 0.0 collective-permute-done.9.from_left
  43.5 0.0 collective-permute-done.10.from_right
  43.5 0.9 shard_map.178
  44.4 11.2 %all_to_all.21.refs_4_ = f32[32,3,4,128]{3,2,1,0:T(4,128)S(1)} all-to-all(f32[32,3,4,128]{3,2,1,0:T(4,128)S(1)} %get-tuple-element.105.after), channel_id=1, replica_groups=mesh['dp'=4,'lat'=2,'lon'=4] {'dp','lat','lon'}, dimensions={0} | all-to-all | bytes 393216 | tf_op jit(solution)/shard_map/all_to_all | solution.py:769
  55.6 4.1 %shard_map.179 = (bf16[16,192,128]{2,1,0:T(8,128)(2,1)S(1)}, f32[18,304,128]{2,1,0:T(8,128)S(1)}, f32[32,3,2,128]{3,2,1,0:T(2,128)S(1)}, f32[12,128]{1,0:T(8,128)S(1)}, f32[8,128]{1,0:T(8,128)S(1)}) custom-call(f32[18,304,128]{2,1,0:T(8,128)S(1)} %get-tuple-element.97.refs_0_.refs_2_, f32[16,192,128]{2,1,0:T(8,128)S(1)} %get-tuple-element.94.refs_3_.refs_1_, ...), custom_call_target="tpu_custom_call" | custom-call | flops 2151677952 | bytes 8560640 | tf_op jit(solution)/shard_map/pallas_call | solution.py:45
  59.7 9.8 %all_to_all.22.refs_4_ = f32[32,3,2,128]{3,2,1,0:T(2,128)S(1)} all-to-all(f32[32,3,2,128]{3,2,1,0:T(2,128)S(1)} %get-tuple-element.109), channel_id=1, replica_groups=mesh['dp'=4,'lat'=2,'lon'=4] {'dp','lat','lon'}, dimensions={0} | all-to-all | bytes 196608 | tf_op jit(solution)/shard_map/all_to_all | solution.py:769
  69.5 4.8 %shard_map.180 = (bf16[9,2,192,384]{3,2,1,0:T(8,128)(2,1)S(1)}, f32[8,128]{1,0:T(8,128)}, f32[8,128]{1,0:T(8,128)S(1)}, f32[4,304,128]{2,1,0:T(8,128)S(1)}, bf16[4,304,128]{2,1,0:T(8,128)(2,1)S(1)}) custom-call(f32[20,192,128]{2,1,0:T(8,128)S(1)} %get-tuple-element.90.refs_0_.refs_5_, f32[20,112,128]{2,1,0:T(8,128)S(1)} %shard_map.174.refs_1_, ...), custom_call_target="tpu_custom_call" | custom-call | flops 2151677952 | bytes 14729216 | tf_op jit(solution)/shard_map/pallas_call | solution.py:45
  74.3 0.0 collective-permute-start.11
  74.3 1.6 %collective-permute-done.11.got = bf16[4,304,128]{2,1,0:T(8,128)(2,1)S(1)} collective-permute-done((bf16[4,304,128]{2,1,0:T(8,128)(2,1)S(1)}, bf16[4,304,128]{2,1,0:T(8,128)(2,1)S(1)}, u32[]{:S(2)}, u32[]{:S(2)}) %collective-permute-start.11) | collective-permute-done | bytes 311328 | tf_op jit(solution)/shard_map/ppermute | solution.py:774
  75.9 0.1 shard_map.181
  76.0 0.7 collective-permute-start.12
  76.7 1.0 collective-permute-start.13
  77.7 2.2 %collective-permute-start.14 = (bf16[304,128]{1,0:T(8,128)(2,1)S(1)}, bf16[304,128]{1,0:T(8,128)(2,1)S(1)}, u32[]{:S(2)}, u32[]{:S(2)}) collective-permute-start(bf16[304,128]{1,0:T(8,128)(2,1)S(1)} %get-tuple-element.122), channel_id=1, source_target_pairs={{0,24},{8,0},{16,8},{24,16},{1,25},{9,1},{17,9},{25,17},{2,26},{10... | collective-permute-start | bytes 233480 | tf_op jit(solution)/shard_map/ppermute | solution.py:774
  79.9 0.0 copy-done
  79.9 1.7 %shard_map.182.outputs = bf16[12,16,16,128]{3,2,1,0:T(8,128)(2,1)} custom-call(bf16[304,128]{1,0:T(8,128)(2,1)S(1)} %get-tuple-element.116.refs_0_.after, bf16[12,16,16,128]{3,2,1,0:T(8,128)(2,1)S(1)} %copy-done, f32[18,304,128]{2,1,0:T(8,128)S(1)} %get-tuple-element.97.refs_0_.refs_2_, f32[12,128]{1,0:T(8,128)S(1)} %get-tuple-element.117.refs_3_.refs_10_, ...), custom_call_target="tpu_custom_call" | custom-call | flops 100000000 | bytes 3680256 | tf_op jit(solution)/shard_map/pallas_call | solution.py:45
  81.6 1.6 %collective-permute-done.12.refs_1_ = bf16[304,128]{1,0:T(8,128)(2,1)S(1)} collective-permute-done((bf16[304,128]{1,0:T(8,128)(2,1)S(1)}, bf16[304,128]{1,0:T(8,128)(2,1)S(1)}, u32[]{:S(2)}, u32[]{:S(2)}) %collective-permute-start.12) | collective-permute-done | bytes 77856 | tf_op jit(solution)/shard_map/ppermute | solution.py:774
  83.2 2.5 %collective-permute-done.13.refs_2_ = bf16[304,128]{1,0:T(8,128)(2,1)S(1)} collective-permute-done((bf16[304,128]{1,0:T(8,128)(2,1)S(1)}, bf16[304,128]{1,0:T(8,128)(2,1)S(1)}, u32[]{:S(2)}, u32[]{:S(2)}) %collective-permute-start.13) | collective-permute-done | bytes 77856 | tf_op jit(solution)/shard_map/ppermute | solution.py:774
  85.7 0.0 collective-permute-done.14.refs_3_
  85.7 0.1 shard_map.184.refs_0_
  85.8 0.7 collective-permute-start.17
  86.5 1.2 %collective-permute-start.16 = (bf16[304,128]{1,0:T(8,128)(2,1)S(1)}, bf16[304,128]{1,0:T(8,128)(2,1)S(1)}, u32[]{:S(2)}, u32[]{:S(2)}) collective-permute-start(bf16[304,128]{1,0:T(8,128)(2,1)S(1)} %shard_map.184.refs_0_), channel_id=1, source_target_pairs={{0,2},{1,3},{2,0},{3,1},{4,6},{5,7},{6,4},{7,5},{8,10},{9,11},{10,... | collective-permute-start | bytes 233480 | tf_op jit(solution)/shard_map/ppermute | solution.py:774
  87.7 0.5 collective-permute-start.15
  88.2 2.8 %shard_map.183.grad_inputs = bf16[12,16,16,128]{3,2,1,0:T(8,128)(2,1)} custom-call(s32[12]{0:T(128)S(1)} %copy-done.2, bf16[304,128]{1,0:T(8,128)(2,1)S(1)} %get-tuple-element.116.refs_0_.after, bf16[9,2,192,384]{3,2,1,0:T(8,128)(2,1)S(1)} %get-tuple-element.118.g_inner, bf16[12,16,16,128]{3,2,1,0:T(8,128)(2,1)S(1)} %copy-done.1, ...), custom_call_target="tpu_custom_call" | custom-call | flops 1434451968 | bytes 4304944 | tf_op jit(solution)/shard_map/pallas_call | solution.py:45
  91.1 0.0 collective-permute-done.17.refs_3_
  91.1 0.3 collective-permute-done.16.refs_2_
  91.3 1.6 %collective-permute-done.15.refs_1_ = bf16[304,128]{1,0:T(8,128)(2,1)S(1)} collective-permute-done((bf16[304,128]{1,0:T(8,128)(2,1)S(1)}, bf16[304,128]{1,0:T(8,128)(2,1)S(1)}, u32[]{:S(2)}, u32[]{:S(2)}) %collective-permute-start.15) | collective-permute-done | bytes 77856 | tf_op jit(solution)/shard_map/ppermute | solution.py:774
  93.0 0.7 shard_map.185
  93.7 3.3 %all-to-all-start.3 = ((f32[8,4,128]{2,1,0:T(4,128)}), f32[8,4,128]{2,1,0:T(4,128)S(1)}, u32[]{:S(2)}, u32[]{:S(2)}) async-start(f32[8,4,128]{2,1,0:T(4,128)} %get-tuple-element.130), calls=%async_computation.3 | async-start | bytes 32768 | tf_op jit(solution)/shard_map/all_to_all | solution.py:769
  97.0 0.4 collective-permute-start.18
  97.4 1.2 %shard_map.186 = (f32[2,288,128]{2,1,0:T(8,128)S(1)}, f32[2,288,128]{2,1,0:T(8,128)S(1)}, f32[2,288,128]{2,1,0:T(8,128)S(1)}, f32[6,32]{1,0:T(8,128)S(1)}, f32[6,32]{1,0:T(8,128)S(1)}, /*index=5*/f32[6,32]{1,0:T(8,128)S(1)}) custom-call(f32[2,288,128]{2,1,0:T(8,128)} %refs_0_.1, f32[2,288,128]{2,1,0:T(8,128)} %refs_1_.3, f32[2,288,128]{2,1,0:T(8,128)} %refs_2_.1, ...), custom_call_target="tpu_custom_call" | custom-call | flops 10000000000 | bytes 1034496 | tf_op jit(solution)/shard_map/pallas_call | solution.py:45
  98.6 4.0 %all-to-all-done.3.refs_8_ = f32[8,4,128]{2,1,0:T(4,128)S(1)} async-done(((f32[8,4,128]{2,1,0:T(4,128)}), f32[8,4,128]{2,1,0:T(4,128)S(1)}, u32[]{:S(2)}, u32[]{:S(2)}) %all-to-all-start.3) | async-done | bytes 16416 | tf_op jit(solution)/shard_map/all_to_all | solution.py:769
  102.6 0.0 collective-permute-done.18.refs_7_
  102.6 1.4 %shard_map.187 = (f32[1,1]{1,0:T(1,128)}, f32[2,288,128]{2,1,0:T(8,128)}, f32[2,288,128]{2,1,0:T(8,128)}, f32[2,288,128]{2,1,0:T(8,128)}, bf16[2,288,128]{2,1,0:...) custom-call(f32[2,288,128]{2,1,0:T(8,128)S(1)} %get-tuple-element.124.refs_0_, ...), custom_call_target="tpu_custom_call" | custom-call | bytes 1212672 | tf_op jit(solution)/shard_map/pallas_call | solution.py:45
  (5 shorter events, 0.0 us)
Async XLA Ops:
  0.6 12.4 %copy-start.2 = (s32[12]{0:T(128)S(1)}, s32[12]{0:T(128)}, u32[]{:S(2)}) copy-start(s32[12]{0:T(128)} %lead.5) | copy-start | bytes 148
  2.3 1.7 %collective-permute-start = (bf16[12,6,16,128]{3,2,1,0:T(8,128)(2,1)S(1)}, bf16[12,6,16,128]{3,2,1,0:T(8,128)(2,1)S(1)}, u32[]{:S(2)}, u32[]{:S(2)}) collective-permute-start(bf16[12,6,16,128]{3,2,1,0:T(8,128)(2,1)S(1)} %get-tuple-element.76), channel_id=1, source_target_pairs={{0,4},{4,0},{1,5},{5,1},{2,6},{6,2},{3,7},{7,3},{8,12},{12,8},{9,1... | collective-permute-start | bytes 884744 | tf_op jit(solution)/shard_map/ppermute | solution.py:774
  4.1 16.8 %collective-permute-start.1 = (bf16[20,3,16,128]{3,2,1,0:T(8,128)(2,1)S(1)}, bf16[20,3,16,128]{3,2,1,0:T(8,128)(2,1)S(1)}, u32[]{:S(2)}, u32[]{:S(2)}) collective-permute-start(bf16[20,3,16,128]{3,2,1,0:T(8,128)(2,1)S(1)} %get-tuple-element.80), channel_id=1, source_target_pairs={{0,1},{1,2},{2,3},{3,0},{4,5},{5,6},{6,7},{7,4},{8,9},{9,10},{10,1... | collective-permute-start | bytes 737288 | tf_op jit(solution)/shard_map/ppermute | solution.py:774
  7.0 13.9 %collective-permute-start.2 = (bf16[20,3,16,128]{3,2,1,0:T(8,128)(2,1)S(1)}, bf16[20,3,16,128]{3,2,1,0:T(8,128)(2,1)S(1)}, u32[]{:S(2)}, u32[]{:S(2)}) collective-permute-start(bf16[20,3,16,128]{3,2,1,0:T(8,128)(2,1)S(1)} %get-tuple-element.81), channel_id=1, source_target_pairs={{0,3},{1,0},{2,1},{3,2},{4,7},{5,4},{6,5},{7,6},{8,11},{9,8},{10,9... | collective-permute-start | bytes 737288 | tf_op jit(solution)/shard_map/ppermute | solution.py:774
  8.0 6.8 %collective-permute-start.5 = (bf16[304,128]{1,0:T(8,128)(2,1)S(1)}, bf16[304,128]{1,0:T(8,128)(2,1)S(1)}, u32[]{:S(2)}, u32[]{:S(2)}) collective-permute-start(bf16[304,128]{1,0:T(8,128)(2,1)S(1)} %get-tuple-element.82), channel_id=1, source_target_pairs={{0,24},{8,0},{16,8},{24,16},{1,25},{9,1},{17,9},{25,17},{2,26},{10... | collective-permute-start | bytes 233480 | tf_op jit(solution)/shard_map/ppermute | solution.py:774
  12.1 7.0 %collective-permute-start.4 = (bf16[304,128]{1,0:T(8,128)(2,1)S(1)}, bf16[304,128]{1,0:T(8,128)(2,1)S(1)}, u32[]{:S(2)}, u32[]{:S(2)}) collective-permute-start(bf16[304,128]{1,0:T(8,128)(2,1)S(1)} %get-tuple-element.82), channel_id=1, source_target_pairs={{0,16},{8,24},{16,0},{24,8},{1,17},{9,25},{17,1},{25,9},{2,18},{10... | collective-permute-start | bytes 233480 | tf_op jit(solution)/shard_map/ppermute | solution.py:774
  12.1 7.0 %collective-permute-start.3 = (bf16[304,128]{1,0:T(8,128)(2,1)S(1)}, bf16[304,128]{1,0:T(8,128)(2,1)S(1)}, u32[]{:S(2)}, u32[]{:S(2)}) collective-permute-start(bf16[304,128]{1,0:T(8,128)(2,1)S(1)} %get-tuple-element.82), channel_id=1, source_target_pairs={{0,8},{8,16},{16,24},{24,0},{1,9},{9,17},{17,25},{25,1},{2,10},{10... | collective-permute-start | bytes 233480 | tf_op jit(solution)/shard_map/ppermute | solution.py:774
  19.0 1.3 %collective-permute-start.6 = (bf16[304,128]{1,0:T(8,128)(2,1)S(1)}, bf16[304,128]{1,0:T(8,128)(2,1)S(1)}, u32[]{:S(2)}, u32[]{:S(2)}) collective-permute-start(bf16[304,128]{1,0:T(8,128)(2,1)S(1)} %collective-permute-done.3.rest_1_), channel_id=1, source_target_pairs={{0,4},{4,0},{1,5},{5,1},{2,6},{6,2},{3,7},{7,3},{8,12},{12,8},{9,1... | collective-permute-start | bytes 233480 | tf_op jit(solution)/shard_map/ppermute | solution.py:774
  19.0 1.4 %collective-permute-start.7 = (bf16[304,128]{1,0:T(8,128)(2,1)S(1)}, bf16[304,128]{1,0:T(8,128)(2,1)S(1)}, u32[]{:S(2)}, u32[]{:S(2)}) collective-permute-start(bf16[304,128]{1,0:T(8,128)(2,1)S(1)} %collective-permute-done.4.rest_3_), channel_id=1, source_target_pairs={{0,4},{4,0},{1,5},{5,1},{2,6},{6,2},{3,7},{7,3},{8,12},{12,8},{9,1... | collective-permute-start | bytes 233480 | tf_op jit(solution)/shard_map/ppermute | solution.py:774
  19.5 1.3 %collective-permute-start.8 = (bf16[304,128]{1,0:T(8,128)(2,1)S(1)}, bf16[304,128]{1,0:T(8,128)(2,1)S(1)}, u32[]{:S(2)}, u32[]{:S(2)}) collective-permute-start(bf16[304,128]{1,0:T(8,128)(2,1)S(1)} %collective-permute-done.5.rest_5_), channel_id=1, source_target_pairs={{0,4},{4,0},{1,5},{5,1},{2,6},{6,2},{3,7},{7,3},{8,12},{12,8},{9,1... | collective-permute-start | bytes 233480 | tf_op jit(solution)/shard_map/ppermute | solution.py:774
  35.2 8.3 %collective-permute-start.9 = (bf16[9,3,16,128]{3,2,1,0:T(8,128)(2,1)S(1)}, bf16[9,3,16,128]{3,2,1,0:T(8,128)(2,1)S(1)}, u32[]{:S(2)}, u32[]{:S(2)}) collective-permute-start(bf16[9,3,16,128]{3,2,1,0:T(8,128)(2,1)S(1)} %get-tuple-element.99), channel_id=1, source_target_pairs={{0,1},{1,2},{2,3},{3,0},{4,5},{5,6},{6,7},{7,4},{8,9},{9,10},{10,1... | collective-permute-start | bytes 331784 | tf_op jit(solution)/shard_map/ppermute | solution.py:774
  35.6 7.9 %collective-permute-start.10 = (bf16[9,3,16,128]{3,2,1,0:T(8,128)(2,1)S(1)}, bf16[9,3,16,128]{3,2,1,0:T(8,128)(2,1)S(1)}, u32[]{:S(2)}, u32[]{:S(2)}) collective-permute-start(bf16[9,3,16,128]{3,2,1,0:T(8,128)(2,1)S(1)} %get-tuple-element.100), channel_id=1, source_target_pairs={{0,3},{1,0},{2,1},{3,2},{4,7},{5,4},{6,5},{7,6},{8,11},{9,8},{10,9... | collective-permute-start | bytes 331784 | tf_op jit(solution)/shard_map/ppermute | solution.py:774
  69.5 10.4 %copy-start = (bf16[12,16,16,128]{3,2,1,0:T(8,128)(2,1)S(1)}, bf16[12,16,16,128]{3,2,1,0:T(8,128)(2,1)}, u32[]{:S(2)}) copy-start(bf16[12,16,16,128]{3,2,1,0:T(8,128)(2,1)} %refs_1_.2) | copy-start | bytes 2359300
  74.3 1.6 %collective-permute-start.11 = (bf16[4,304,128]{2,1,0:T(8,128)(2,1)S(1)}, bf16[4,304,128]{2,1,0:T(8,128)(2,1)S(1)}, u32[]{:S(2)}, u32[]{:S(2)}) collective-permute-start(bf16[4,304,128]{2,1,0:T(8,128)(2,1)S(1)} %get-tuple-element.115), channel_id=1, source_target_pairs={{0,4},{4,0},{1,5},{5,1},{2,6},{6,2},{3,7},{7,3},{8,12},{12,8},{9,1... | collective-permute-start | bytes 933896 | tf_op jit(solution)/shard_map/ppermute | solution.py:774
  75.9 12.3 %copy-start.1 = (bf16[12,16,16,128]{3,2,1,0:T(8,128)(2,1)S(1)}, bf16[12,16,16,128]{3,2,1,0:T(8,128)(2,1)}, u32[]{:S(2)}) copy-start(bf16[12,16,16,128]{3,2,1,0:T(8,128)(2,1)} %cot.3) | copy-start | bytes 2359300
  76.0 7.1 %collective-permute-start.12 = (bf16[304,128]{1,0:T(8,128)(2,1)S(1)}, bf16[304,128]{1,0:T(8,128)(2,1)S(1)}, u32[]{:S(2)}, u32[]{:S(2)}) collective-permute-start(bf16[304,128]{1,0:T(8,128)(2,1)S(1)} %get-tuple-element.120), channel_id=1, source_target_pairs={{0,8},{8,16},{16,24},{24,0},{1,9},{9,17},{17,25},{25,1},{2,10},{10... | collective-permute-start | bytes 233480 | tf_op jit(solution)/shard_map/ppermute | solution.py:774
  76.7 9.0 %collective-permute-start.13 = (bf16[304,128]{1,0:T(8,128)(2,1)S(1)}, bf16[304,128]{1,0:T(8,128)(2,1)S(1)}, u32[]{:S(2)}, u32[]{:S(2)}) collective-permute-start(bf16[304,128]{1,0:T(8,128)(2,1)S(1)} %get-tuple-element.121), channel_id=1, source_target_pairs={{0,16},{8,24},{16,0},{24,8},{1,17},{9,25},{17,1},{25,9},{2,18},{10... | collective-permute-start | bytes 233480 | tf_op jit(solution)/shard_map/ppermute | solution.py:774
  77.7 8.0 %collective-permute-start.14 = (bf16[304,128]{1,0:T(8,128)(2,1)S(1)}, bf16[304,128]{1,0:T(8,128)(2,1)S(1)}, u32[]{:S(2)}, u32[]{:S(2)}) collective-permute-start(bf16[304,128]{1,0:T(8,128)(2,1)S(1)} %get-tuple-element.122), channel_id=1, source_target_pairs={{0,24},{8,0},{16,8},{24,16},{1,25},{9,1},{17,9},{25,17},{2,26},{10... | collective-permute-start | bytes 233480 | tf_op jit(solution)/shard_map/ppermute | solution.py:774
  85.8 5.3 %collective-permute-start.17 = (bf16[304,128]{1,0:T(8,128)(2,1)S(1)}, bf16[304,128]{1,0:T(8,128)(2,1)S(1)}, u32[]{:S(2)}, u32[]{:S(2)}) collective-permute-start(bf16[304,128]{1,0:T(8,128)(2,1)S(1)} %shard_map.184.refs_0_), channel_id=1, source_target_pairs={{0,3},{1,0},{2,1},{3,2},{4,7},{5,4},{6,5},{7,6},{8,11},{9,8},{10,9... | collective-permute-start | bytes 233480 | tf_op jit(solution)/shard_map/ppermute | solution.py:774
  86.5 4.8 %collective-permute-start.16 = (bf16[304,128]{1,0:T(8,128)(2,1)S(1)}, bf16[304,128]{1,0:T(8,128)(2,1)S(1)}, u32[]{:S(2)}, u32[]{:S(2)}) collective-permute-start(bf16[304,128]{1,0:T(8,128)(2,1)S(1)} %shard_map.184.refs_0_), channel_id=1, source_target_pairs={{0,2},{1,3},{2,0},{3,1},{4,6},{5,7},{6,4},{7,5},{8,10},{9,11},{10,... | collective-permute-start | bytes 233480 | tf_op jit(solution)/shard_map/ppermute | solution.py:774
  87.7 5.3 %collective-permute-start.15 = (bf16[304,128]{1,0:T(8,128)(2,1)S(1)}, bf16[304,128]{1,0:T(8,128)(2,1)S(1)}, u32[]{:S(2)}, u32[]{:S(2)}) collective-permute-start(bf16[304,128]{1,0:T(8,128)(2,1)S(1)} %shard_map.184.refs_0_), channel_id=1, source_target_pairs={{0,1},{1,2},{2,3},{3,0},{4,5},{5,6},{6,7},{7,4},{8,9},{9,10},{10,1... | collective-permute-start | bytes 233480 | tf_op jit(solution)/shard_map/ppermute | solution.py:774
  93.7 8.9 %all-to-all-start.3 = ((f32[8,4,128]{2,1,0:T(4,128)}), f32[8,4,128]{2,1,0:T(4,128)S(1)}, u32[]{:S(2)}, u32[]{:S(2)}) async-start(f32[8,4,128]{2,1,0:T(4,128)} %get-tuple-element.130), calls=%async_computation.3 | async-start | bytes 32768 | tf_op jit(solution)/shard_map/all_to_all | solution.py:769
  97.0 5.6 %collective-permute-start.18 = (f32[288,128]{1,0:T(8,128)S(1)}, f32[288,128]{1,0:T(8,128)S(1)}, u32[]{:S(2)}, u32[]{:S(2)}) collective-permute-start(f32[288,128]{1,0:T(8,128)S(1)} %get-tuple-element.123.refs_6_), channel_id=1, source_target_pairs={{0,4},{4,0},{1,5},{5,1},{2,6},{6,2},{3,7},{7,3},{8,12},{12,8},{9,1... | collective-permute-start | bytes 442376 | tf_op jit(solution)/shard_map/ppermute | solution.py:774

commit v4 on v3

--- a/solution.py
+++ b/solution.py
@@ -253,15 +253,13 @@
         out[size * t : size * t + size, :] = weight[pl.ds(t, size, stride=9), :].astype(BF16)
 
 
-def prep_kernel(x, cot, weight, vectors, packed, lat_out, x_near, cot_near, held, held_vec, sems):
+def prep_kernel(x, cot, weight, vectors, packed, lat_out, held, held_vec, sems):
     last = lax.axis_index("lat") == 0
     copies = [
         pltpu.make_async_copy(weight, held, sems.at[0]),
         pltpu.make_async_copy(vectors, held_vec, sems.at[1]),
         pltpu.make_async_copy(x.at[:, pl.ds(jnp.where(last, R - 4, 0), 4)], lat_out.at[:, 0:4], sems.at[2]),
         pltpu.make_async_copy(cot.at[:, pl.ds(jnp.where(last, R - 2, 0), 2)], lat_out.at[:, 4:6], sems.at[3]),
-        pltpu.make_async_copy(x, x_near, sems.at[4]),
-        pltpu.make_async_copy(cot, cot_near, sems.at[5]),
     ]
     for copy in copies:
         copy.start()
@@ -294,12 +292,19 @@
         far_l[at, m] = jnp.concatenate([v[:columns] for v in tiles], axis=0).astype(BF16)
 
 
-def edge_kernel(x, far_r, far_l):
+def edge_kernel(x_far, cot_far, x, cot, far_r, far_l, sems):
+    copies = [pltpu.make_async_copy(x_far, x, sems.at[0]), pltpu.make_async_copy(cot_far, cot, sems.at[1])]
+    for copy in copies:
+        copy.start()
+    copies[0].wait()
+
     @pl.loop(0, R // 2)
     def _(i):
         for q in range(2):
             cut_far(lambda _, n: x[n, own_row(2 * i + q)], far_r, far_l, 2 * i + q, 4, 1)
 
+    copies[1].wait()
+
 
 def beyond_kernel(lat_in, packed, right_in, left_in, mine, far_r, far_l):
     for k in range(4):
@@ -307,7 +312,7 @@
     mine[...] = packed[lax.axis_index("lat")]
 
 
-def later_kernel(after, cot, lat_in, far_r, far_l):
+def later_kernel(cot, lat_in, far_r, far_l):
     @pl.loop(0, R // 2)
     def _(i):
         cut_far(lambda q, n: cot[n, own_row(2 * i + q)], far_r, far_l, i, 2, 2)
@@ -783,25 +788,29 @@
     flats = [pltpu.VMEM((FLAT, C), F32)] * 2
     conv_flops = 2 * T * 12 * C * 2 * C
 
-    packed, lat_out, x_near, cot_near = call(
+    packed, lat_out = call(
         prep_kernel,
         [
             ((2, 9 * size + 16, C), BF16),
             ((S, 6, R, C), BF16),
-            (inputs.shape, BF16),
-            (inputs.shape, BF16),
         ],
         (inputs, cotangent, conv_weight, vectors),
         [
             pltpu.VMEM(conv_weight.shape, F32),
             pltpu.VMEM(vectors.shape, F32),
-            pltpu.SemaphoreType.DMA((6,)),
+            pltpu.SemaphoreType.DMA((4,)),
         ],
         far=4,
     )
     lat_in = turn(lat_out, "lat", 1)
     edge_kinds = [((R + 4, MB, 16, C), BF16)] * 2
-    edges = call(edge_kernel, edge_kinds, (x_near,))
+    x_near, cot_near, *edges = call(
+        edge_kernel,
+        [(inputs.shape, BF16)] * 2 + edge_kinds,
+        (inputs, cotangent),
+        [pltpu.SemaphoreType.DMA((2,))],
+        far=2,
+    )
     mine, far_r, far_l = call(
         beyond_kernel,
         [((9 * size + 16, C), BF16)] + edge_kinds,
@@ -812,9 +821,10 @@
     dn, dn_sums = call(
         lead_kernel, [((R, TI, C), F32), ((8, C), F32)], (lead_time, cot_near), flops=10**8, scalars=1
     )
+    cot_r, cot_l = call(later_kernel, [((R // 2 + 1, MB, 16, C), BF16)] * 2, (cot_near, lat_in))
     if split:
         fetched = [turn(mine, "dp", k) for k in range(1, groups)]
-        *fetched, dn = lax.optimization_barrier((*fetched, dn))
+        *fetched, dn, cot_r, cot_l = lax.optimization_barrier((*fetched, dn, cot_r, cot_l))
         pieces = [packed]
         for piece in fetched:
             pieces += [piece, turn(piece, "lat", 1)]
@@ -846,9 +856,7 @@
         [pltpu.VMEM((11, 2, TH, W3), BF16)] + flats,
         flops=conv_flops * 4,
     )
-    cot_r, cot_l = call(
-        later_kernel, [((R // 2 + 1, MB, 16, C), BF16)] * 2, (got_one, cot_near, lat_in)
-    )
+    got_one, cot_r, cot_l = lax.optimization_barrier((got_one, cot_r, cot_l))
     cot_left, cot_right = turn(cot_r, "lon", 1), turn(cot_l, "lon", -1)
     n_all, pre_two, sums_two, stat_one = call(
         lambda *refs: second_kernel(count, *refs),

time: 104 us -> 104 us (level)
    ppermute x19, waiting for transfers between devices: 15 us -> 13.9 us  [turn(): lax.ppermute(block, axis, [(i, (i + by) % size) for i in range(size)])]
  transfers between devices with their start and end apart: 20 -> 20, of which waited for: 12 -> 11; matrix products, arithmetic and copies ran while one was open for 0% -> 0% of each run, Pallas kernels for 12% -> 13%
where the time goes in v4:
time: 104 us; the launch traced here: 103 us
  blocking collectives  32.4 us (31%)
  Pallas kernels  29.4 us (28%)
  starting transfers between devices  22.8 us (22%)
  waiting for transfers between devices  17.9 us (17%)
    all_to_all x3, blocking collectives, spread(): return lax.all_to_all(block, axes, 0, 0, tiled=True)  32.4 us
    pallas_call x20, Pallas kernels, call(): pl.pallas_call(kernel, out_shape=tuple((pltpu.HBM(shape, kind) if n in fa...  29.4 us
    ppermute x19, starting transfers between devices, turn(): lax.ppermute(block, axis, [(i, (i + by) % size) for i in range(size)])  19.4 us
    ppermute x19, waiting for transfers between devices, turn(): lax.ppermute(block, axis, [(i, (i + by) % size) for i in range(size)])  13.9 us
    all_to_all x1, waiting for transfers between devices, spread(): return lax.all_to_all(block, axes, 0, 0, tiled=True)  3.98 us
    all_to_all x1, starting transfers between devices, spread(): return lax.all_to_all(block, axes, 0, 0, tiled=True)  3.34 us
  transfers between devices with their start and end apart: 20, of which 11 were waited for; matrix products, arithmetic and copies ran while one was open for 0% of the time, Pallas kernels for 13%

profile of v4, /device:TPU:0, one launch (start us, length us, event | category | flops | bytes accessed | tf_op | source)
XLA Modules:
  0.0 103.3 jit_solution(6477027851561588136)
XLA Ops:
  0.7 1.1 %shard_map.169 = (bf16[2,304,128]{2,1,0:T(8,128)(2,1)S(1)}, bf16[12,6,16,128]{3,2,1,0:T(8,128)(2,1)S(1)}) custom-call(bf16[12,16,16,128]{3,2,1,0:T(8,128)(2,1)} %refs_1_.2, bf16[12,16,16,128]{3,2,1,0:T(8,128)(2,1)} %cot.3, f32[2,288,128]{2,1,0:T(8,128)} %refs_0_.1, f32[6,32]{1,0:T(8,128)} %refs_3_.1), custom_call_target="tpu_custom_call" | custom-call | bytes 1868544 | tf_op jit(solution)/shard_map/pallas_call | solution.py:45
  1.8 0.5 collective-permute-start
  2.3 1.4 %shard_map.168 = (bf16[12,16,16,128]{3,2,1,0:T(8,128)(2,1)S(1)}, bf16[12,16,16,128]{3,2,1,0:T(8,128)(2,1)S(1)}, bf16[20,3,16,128]{3,2,1,0:T(8,128)(2,1)S(1)}, bf16[20,3,16,128]{3,2,1,0:T(8,128)(2,1)S(1)}) custom-call(bf16[12,16,16,128]{3,2,1,0:T(8,128)(2,1)} %refs_1_.2, bf16[12,16,16,128]{3,2,1,0:T(8,128)(2,1)} %cot.3), custom_call_target="tpu_custom_call" | custom-call | bytes 1572864 | tf_op jit(solution)/shard_map/pallas_call | solution.py:45
  3.7 0.0 collective-permute-done.lat_in
  3.8 2.7 %collective-permute-start.1 = (bf16[20,3,16,128]{3,2,1,0:T(8,128)(2,1)S(1)}, bf16[20,3,16,128]{3,2,1,0:T(8,128)(2,1)S(1)}, u32[]{:S(2)}, u32[]{:S(2)}) collective-permute-start(bf16[20,3,16,128]{3,2,1,0:T(8,128)(2,1)S(1)} %get-tuple-element.85), channel_id=1, source_target_pairs={{0,1},{1,2},{2,3},{3,0},{4,5},{5,6},{6,7},{7,4},{8,9},{9,10},{10,1... | collective-permute-start | bytes 737288 | tf_op jit(solution)/shard_map/ppermute | solution.py:779
  6.5 1.0 collective-permute-start.2
  7.5 4.0 %collective-permute-start.5 = (bf16[304,128]{1,0:T(8,128)(2,1)S(1)}, bf16[304,128]{1,0:T(8,128)(2,1)S(1)}, u32[]{:S(2)}, u32[]{:S(2)}) collective-permute-start(bf16[304,128]{1,0:T(8,128)(2,1)S(1)} %get-tuple-element.87), channel_id=1, source_target_pairs={{0,24},{8,0},{16,8},{24,16},{1,25},{9,1},{17,9},{25,17},{2,26},{10... | collective-permute-start | bytes 233480 | tf_op jit(solution)/shard_map/ppermute | solution.py:779
  11.5 0.0 collective-permute-start.4
  11.5 1.0 collective-permute-start.3
  12.5 0.0 copy-done.2
  12.5 0.9 shard_map.171
  13.4 0.3 shard_map.172
  13.7 0.6 collective-permute-done.5.rest_5_
  14.3 4.4 %collective-permute-done.4.rest_3_ = bf16[304,128]{1,0:T(8,128)(2,1)S(1)} collective-permute-done((bf16[304,128]{1,0:T(8,128)(2,1)S(1)}, bf16[304,128]{1,0:T(8,128)(2,1)S(1)}, u32[]{:S(2)}, u32[]{:S(2)}) %collective-permute-start.4) | collective-permute-done | bytes 77856 | tf_op jit(solution)/shard_map/ppermute | solution.py:779
  18.7 0.0 collective-permute-done.3.rest_1_
  18.7 0.0 collective-permute-start.6
  18.7 0.5 collective-permute-start.7
  19.2 0.0 collective-permute-start.8
  19.2 0.8 collective-permute-done.6.rest_2_
  20.0 0.2 collective-permute-done.7.rest_4_
  20.1 0.4 collective-permute-done.8.rest_6_
  20.5 0.1 shard_map.173
  20.6 0.0 collective-permute-done.1.from_left
  20.6 0.0 collective-permute-done.2.from_right
  20.6 2.5 %shard_map.174 = (bf16[11,2,192,384]{3,2,1,0:T(8,128)(2,1)S(1)}, f32[20,192,128]{2,1,0:T(8,128)S(1)}, f32[32,3,2,128]{3,2,1,0:T(2,128)S(1)}) custom-call(bf16[12,16,16,128]{3,2,1,0:T(8,128)(2,1)S(1)} %get-tuple-element.80.x, bf16[12,6,16,128]{3,2,1,0:T(8,128)(2,1)S(1)} %collective-permute-done.lat_in, ...), custom_call_target="tpu_custom_call" | custom-call | flops 1434451968 | bytes 2367488 | tf_op jit(solution)/shard_map/pallas_call | solution.py:45
  23.2 11.4 %all_to_all.20.after.refs_2_ = f32[32,3,2,128]{3,2,1,0:T(2,128)S(1)} all-to-all(f32[32,3,2,128]{3,2,1,0:T(2,128)S(1)} %get-tuple-element.100), channel_id=1, replica_groups=mesh['dp'=4,'lat'=2,'lon'=4] {'dp','lat','lon'}, dimensions={0} | all-to-all | bytes 196608 | tf_op jit(solution)/shard_map/all_to_all | solution.py:774
  34.6 0.4 collective-permute-start.9
  35.0 2.5 %collective-permute-start.10 = (bf16[9,3,16,128]{3,2,1,0:T(8,128)(2,1)S(1)}, bf16[9,3,16,128]{3,2,1,0:T(8,128)(2,1)S(1)}, u32[]{:S(2)}, u32[]{:S(2)}) collective-permute-start(bf16[9,3,16,128]{3,2,1,0:T(8,128)(2,1)S(1)} %get-tuple-element.110), channel_id=1, source_target_pairs={{0,3},{1,0},{2,1},{3,2},{4,7},{5,4},{6,5},{7,6},{8,11},{9,8},{10,9... | collective-permute-start | bytes 331784 | tf_op jit(solution)/shard_map/ppermute | solution.py:779
  37.5 1.4 %shard_map.175.refs_1_ = f32[20,112,128]{2,1,0:T(8,128)S(1)} custom-call(f32[32,3,2,128]{3,2,1,0:T(2,128)S(1)} %all_to_all.20.after.refs_2_, bf16[12,16,16,128]{3,2,1,0:T(8,128)(2,1)S(1)} %get-tuple-element.80.x, bf16[12,6,16,128]{3,2,1,0:T(8,128)(2,1)S(1)} %collective-permute-done.lat_in, bf16[20,3,16,128]{3,2,1,0:T(8,128)(2,1)S(1)} %collective-permute-done.1.from_left, ...), custom_call_target="tpu_custom_call" | custom-call | flops 956301312 | bytes 2465792 | tf_op jit(solution)/shard_map/pallas_call | solution.py:45
  38.9 0.4 shard_map.176
  39.3 3.6 %shard_map.177 = (bf16[10,2,304,384]{3,2,1,0:T(8,128)(2,1)S(1)}, f32[18,304,128]{2,1,0:T(8,128)S(1)}, f32[32,3,4,128]{3,2,1,0:T(4,128)S(1)}, f32[8,128]{1,0:T(8,128)S(1)}) custom-call(f32[20,192,128]{2,1,0:T(8,128)S(1)} %get-tuple-element.97.refs_0_.refs_5_, f32[20,112,128]{2,1,0:T(8,128)S(1)} %shard_map.175.refs_1_, ...), custom_call_target="tpu_custom_call" | custom-call | flops 2151677952 | bytes 5582848 | tf_op jit(solution)/shard_map/pallas_call | solution.py:45
  42.9 0.0 collective-permute-done.9.from_left
  42.9 0.0 collective-permute-done.10.from_right
  42.9 0.9 shard_map.178
  43.8 11.2 %all_to_all.21.refs_4_ = f32[32,3,4,128]{3,2,1,0:T(4,128)S(1)} all-to-all(f32[32,3,4,128]{3,2,1,0:T(4,128)S(1)} %get-tuple-element.115.after), channel_id=1, replica_groups=mesh['dp'=4,'lat'=2,'lon'=4] {'dp','lat','lon'}, dimensions={0} | all-to-all | bytes 393216 | tf_op jit(solution)/shard_map/all_to_all | solution.py:774
  54.9 4.1 %shard_map.179 = (bf16[16,192,128]{2,1,0:T(8,128)(2,1)S(1)}, f32[18,304,128]{2,1,0:T(8,128)S(1)}, f32[32,3,2,128]{3,2,1,0:T(2,128)S(1)}, f32[12,128]{1,0:T(8,128)S(1)}, f32[8,128]{1,0:T(8,128)S(1)}) custom-call(f32[18,304,128]{2,1,0:T(8,128)S(1)} %get-tuple-element.107.refs_0_.refs_2_, f32[16,192,128]{2,1,0:T(8,128)S(1)} %get-tuple-element.104.refs_3_.refs_1_, ...), custom_call_target="tpu_custom_call" | custom-call | flops 2151677952 | bytes 8560640 | tf_op jit(solution)/shard_map/pallas_call | solution.py:45
  59.0 9.8 %all_to_all.22.refs_4_ = f32[32,3,2,128]{3,2,1,0:T(2,128)S(1)} all-to-all(f32[32,3,2,128]{3,2,1,0:T(2,128)S(1)} %get-tuple-element.119), channel_id=1, replica_groups=mesh['dp'=4,'lat'=2,'lon'=4] {'dp','lat','lon'}, dimensions={0} | all-to-all | bytes 196608 | tf_op jit(solution)/shard_map/all_to_all | solution.py:774
  68.8 4.8 %shard_map.180 = (bf16[9,2,192,384]{3,2,1,0:T(8,128)(2,1)S(1)}, f32[8,128]{1,0:T(8,128)}, f32[8,128]{1,0:T(8,128)S(1)}, f32[4,304,128]{2,1,0:T(8,128)S(1)}, bf16[4,304,128]{2,1,0:T(8,128)(2,1)S(1)}) custom-call(f32[20,192,128]{2,1,0:T(8,128)S(1)} %get-tuple-element.97.refs_0_.refs_5_, f32[20,112,128]{2,1,0:T(8,128)S(1)} %shard_map.175.refs_1_, ...), custom_call_target="tpu_custom_call" | custom-call | flops 2151677952 | bytes 14729216 | tf_op jit(solution)/shard_map/pallas_call | solution.py:45
  73.7 0.0 collective-permute-start.11
  73.7 1.6 %collective-permute-done.11.got = bf16[4,304,128]{2,1,0:T(8,128)(2,1)S(1)} collective-permute-done((bf16[4,304,128]{2,1,0:T(8,128)(2,1)S(1)}, bf16[4,304,128]{2,1,0:T(8,128)(2,1)S(1)}, u32[]{:S(2)}, u32[]{:S(2)}) %collective-permute-start.11) | collective-permute-done | bytes 311328 | tf_op jit(solution)/shard_map/ppermute | solution.py:779
  75.3 0.1 shard_map.181
  75.4 0.7 collective-permute-start.12
  76.1 1.0 collective-permute-start.13
  77.1 2.2 %collective-permute-start.14 = (bf16[304,128]{1,0:T(8,128)(2,1)S(1)}, bf16[304,128]{1,0:T(8,128)(2,1)S(1)}, u32[]{:S(2)}, u32[]{:S(2)}) collective-permute-start(bf16[304,128]{1,0:T(8,128)(2,1)S(1)} %get-tuple-element.132), channel_id=1, source_target_pairs={{0,24},{8,0},{16,8},{24,16},{1,25},{9,1},{17,9},{25,17},{2,26},{10... | collective-permute-start | bytes 233480 | tf_op jit(solution)/shard_map/ppermute | solution.py:779
  79.3 0.0 copy-done
  79.3 1.7 %shard_map.182.outputs = bf16[12,16,16,128]{3,2,1,0:T(8,128)(2,1)} custom-call(bf16[304,128]{1,0:T(8,128)(2,1)S(1)} %get-tuple-element.126.refs_0_.after, bf16[12,16,16,128]{3,2,1,0:T(8,128)(2,1)S(1)} %copy-done, f32[18,304,128]{2,1,0:T(8,128)S(1)} %get-tuple-element.107.refs_0_.refs_2_, f32[12,128]{1,0:T(8,128)S(1)} %get-tuple-element.127.refs_3_.refs_10_, ...), custom_call_target="tpu_custom_call" | custom-call | flops 100000000 | bytes 3680256 | tf_op jit(solution)/shard_map/pallas_call | solution.py:45
  80.9 1.6 %collective-permute-done.12.refs_1_ = bf16[304,128]{1,0:T(8,128)(2,1)S(1)} collective-permute-done((bf16[304,128]{1,0:T(8,128)(2,1)S(1)}, bf16[304,128]{1,0:T(8,128)(2,1)S(1)}, u32[]{:S(2)}, u32[]{:S(2)}) %collective-permute-start.12) | collective-permute-done | bytes 77856 | tf_op jit(solution)/shard_map/ppermute | solution.py:779
  82.5 2.5 %collective-permute-done.13.refs_2_ = bf16[304,128]{1,0:T(8,128)(2,1)S(1)} collective-permute-done((bf16[304,128]{1,0:T(8,128)(2,1)S(1)}, bf16[304,128]{1,0:T(8,128)(2,1)S(1)}, u32[]{:S(2)}, u32[]{:S(2)}) %collective-permute-start.13) | collective-permute-done | bytes 77856 | tf_op jit(solution)/shard_map/ppermute | solution.py:779
  85.1 0.0 collective-permute-done.14.refs_3_
  85.1 0.1 shard_map.184.refs_0_
  85.1 0.7 collective-permute-start.17
  85.9 1.2 %collective-permute-start.16 = (bf16[304,128]{1,0:T(8,128)(2,1)S(1)}, bf16[304,128]{1,0:T(8,128)(2,1)S(1)}, u32[]{:S(2)}, u32[]{:S(2)}) collective-permute-start(bf16[304,128]{1,0:T(8,128)(2,1)S(1)} %shard_map.184.refs_0_), channel_id=1, source_target_pairs={{0,2},{1,3},{2,0},{3,1},{4,6},{5,7},{6,4},{7,5},{8,10},{9,11},{10,... | collective-permute-start | bytes 233480 | tf_op jit(solution)/shard_map/ppermute | solution.py:779
  87.0 0.5 collective-permute-start.15
  87.6 2.8 %shard_map.183.grad_inputs = bf16[12,16,16,128]{3,2,1,0:T(8,128)(2,1)} custom-call(s32[12]{0:T(128)S(1)} %copy-done.2, bf16[304,128]{1,0:T(8,128)(2,1)S(1)} %get-tuple-element.126.refs_0_.after, bf16[9,2,192,384]{3,2,1,0:T(8,128)(2,1)S(1)} %get-tuple-element.128.g_inner, bf16[12,16,16,128]{3,2,1,0:T(8,128)(2,1)S(1)} %copy-done.1, ...), custom_call_target="tpu_custom_call" | custom-call | flops 1434451968 | bytes 4304944 | tf_op jit(solution)/shard_map/pallas_call | solution.py:45
  90.4 0.0 collective-permute-done.17.refs_3_
  90.4 0.3 collective-permute-done.16.refs_2_
  90.7 1.6 %collective-permute-done.15.refs_1_ = bf16[304,128]{1,0:T(8,128)(2,1)S(1)} collective-permute-done((bf16[304,128]{1,0:T(8,128)(2,1)S(1)}, bf16[304,128]{1,0:T(8,128)(2,1)S(1)}, u32[]{:S(2)}, u32[]{:S(2)}) %collective-permute-start.15) | collective-permute-done | bytes 77856 | tf_op jit(solution)/shard_map/ppermute | solution.py:779
  92.3 0.7 shard_map.185
  93.1 3.3 %all-to-all-start.3 = ((f32[8,4,128]{2,1,0:T(4,128)}), f32[8,4,128]{2,1,0:T(4,128)S(1)}, u32[]{:S(2)}, u32[]{:S(2)}) async-start(f32[8,4,128]{2,1,0:T(4,128)} %get-tuple-element.140), calls=%async_computation.3 | async-start | bytes 32768 | tf_op jit(solution)/shard_map/all_to_all | solution.py:774
  96.4 0.4 collective-permute-start.18
  96.8 1.2 %shard_map.186 = (f32[2,288,128]{2,1,0:T(8,128)S(1)}, f32[2,288,128]{2,1,0:T(8,128)S(1)}, f32[2,288,128]{2,1,0:T(8,128)S(1)}, f32[6,32]{1,0:T(8,128)S(1)}, f32[6,32]{1,0:T(8,128)S(1)}, /*index=5*/f32[6,32]{1,0:T(8,128)S(1)}) custom-call(f32[2,288,128]{2,1,0:T(8,128)} %refs_0_.1, f32[2,288,128]{2,1,0:T(8,128)} %refs_1_.3, f32[2,288,128]{2,1,0:T(8,128)} %refs_2_.1, ...), custom_call_target="tpu_custom_call" | custom-call | flops 10000000000 | bytes 1034496 | tf_op jit(solution)/shard_map/pallas_call | solution.py:45
  98.0 4.0 %all-to-all-done.3.refs_8_ = f32[8,4,128]{2,1,0:T(4,128)S(1)} async-done(((f32[8,4,128]{2,1,0:T(4,128)}), f32[8,4,128]{2,1,0:T(4,128)S(1)}, u32[]{:S(2)}, u32[]{:S(2)}) %all-to-all-start.3) | async-done | bytes 16416 | tf_op jit(solution)/shard_map/all_to_all | solution.py:774
  102.0 0.0 collective-permute-done.18.refs_7_
  102.0 1.4 %shard_map.187 = (f32[1,1]{1,0:T(1,128)}, f32[2,288,128]{2,1,0:T(8,128)}, f32[2,288,128]{2,1,0:T(8,128)}, f32[2,288,128]{2,1,0:T(8,128)}, bf16[2,288,128]{2,1,0:...) custom-call(f32[2,288,128]{2,1,0:T(8,128)S(1)} %get-tuple-element.134.refs_0_, ...), custom_call_target="tpu_custom_call" | custom-call | bytes 1212672 | tf_op jit(solution)/shard_map/pallas_call | solution.py:45
  (5 shorter events, 0.1 us)
Async XLA Ops:
  0.6 11.9 %copy-start.2 = (s32[12]{0:T(128)S(1)}, s32[12]{0:T(128)}, u32[]{:S(2)}) copy-start(s32[12]{0:T(128)} %lead.5) | copy-start | bytes 148
  1.8 1.9 %collective-permute-start = (bf16[12,6,16,128]{3,2,1,0:T(8,128)(2,1)S(1)}, bf16[12,6,16,128]{3,2,1,0:T(8,128)(2,1)S(1)}, u32[]{:S(2)}, u32[]{:S(2)}) collective-permute-start(bf16[12,6,16,128]{3,2,1,0:T(8,128)(2,1)S(1)} %get-tuple-element.81), channel_id=1, source_target_pairs={{0,4},{4,0},{1,5},{5,1},{2,6},{6,2},{3,7},{7,3},{8,12},{12,8},{9,1... | collective-permute-start | bytes 884744 | tf_op jit(solution)/shard_map/ppermute | solution.py:779
  3.8 16.8 %collective-permute-start.1 = (bf16[20,3,16,128]{3,2,1,0:T(8,128)(2,1)S(1)}, bf16[20,3,16,128]{3,2,1,0:T(8,128)(2,1)S(1)}, u32[]{:S(2)}, u32[]{:S(2)}) collective-permute-start(bf16[20,3,16,128]{3,2,1,0:T(8,128)(2,1)S(1)} %get-tuple-element.85), channel_id=1, source_target_pairs={{0,1},{1,2},{2,3},{3,0},{4,5},{5,6},{6,7},{7,4},{8,9},{9,10},{10,1... | collective-permute-start | bytes 737288 | tf_op jit(solution)/shard_map/ppermute | solution.py:779
  6.5 14.1 %collective-permute-start.2 = (bf16[20,3,16,128]{3,2,1,0:T(8,128)(2,1)S(1)}, bf16[20,3,16,128]{3,2,1,0:T(8,128)(2,1)S(1)}, u32[]{:S(2)}, u32[]{:S(2)}) collective-permute-start(bf16[20,3,16,128]{3,2,1,0:T(8,128)(2,1)S(1)} %get-tuple-element.86), channel_id=1, source_target_pairs={{0,3},{1,0},{2,1},{3,2},{4,7},{5,4},{6,5},{7,6},{8,11},{9,8},{10,9... | collective-permute-start | bytes 737288 | tf_op jit(solution)/shard_map/ppermute | solution.py:779
  7.5 6.8 %collective-permute-start.5 = (bf16[304,128]{1,0:T(8,128)(2,1)S(1)}, bf16[304,128]{1,0:T(8,128)(2,1)S(1)}, u32[]{:S(2)}, u32[]{:S(2)}) collective-permute-start(bf16[304,128]{1,0:T(8,128)(2,1)S(1)} %get-tuple-element.87), channel_id=1, source_target_pairs={{0,24},{8,0},{16,8},{24,16},{1,25},{9,1},{17,9},{25,17},{2,26},{10... | collective-permute-start | bytes 233480 | tf_op jit(solution)/shard_map/ppermute | solution.py:779
  11.5 7.2 %collective-permute-start.4 = (bf16[304,128]{1,0:T(8,128)(2,1)S(1)}, bf16[304,128]{1,0:T(8,128)(2,1)S(1)}, u32[]{:S(2)}, u32[]{:S(2)}) collective-permute-start(bf16[304,128]{1,0:T(8,128)(2,1)S(1)} %get-tuple-element.87), channel_id=1, source_target_pairs={{0,16},{8,24},{16,0},{24,8},{1,17},{9,25},{17,1},{25,9},{2,18},{10... | collective-permute-start | bytes 233480 | tf_op jit(solution)/shard_map/ppermute | solution.py:779
  11.5 7.2 %collective-permute-start.3 = (bf16[304,128]{1,0:T(8,128)(2,1)S(1)}, bf16[304,128]{1,0:T(8,128)(2,1)S(1)}, u32[]{:S(2)}, u32[]{:S(2)}) collective-permute-start(bf16[304,128]{1,0:T(8,128)(2,1)S(1)} %get-tuple-element.87), channel_id=1, source_target_pairs={{0,8},{8,16},{16,24},{24,0},{1,9},{9,17},{17,25},{25,1},{2,10},{10... | collective-permute-start | bytes 233480 | tf_op jit(solution)/shard_map/ppermute | solution.py:779
  18.7 1.3 %collective-permute-start.6 = (bf16[304,128]{1,0:T(8,128)(2,1)S(1)}, bf16[304,128]{1,0:T(8,128)(2,1)S(1)}, u32[]{:S(2)}, u32[]{:S(2)}) collective-permute-start(bf16[304,128]{1,0:T(8,128)(2,1)S(1)} %collective-permute-done.3.rest_1_), channel_id=1, source_target_pairs={{0,4},{4,0},{1,5},{5,1},{2,6},{6,2},{3,7},{7,3},{8,12},{12,8},{9,1... | collective-permute-start | bytes 233480 | tf_op jit(solution)/shard_map/ppermute | solution.py:779
  18.7 1.4 %collective-permute-start.7 = (bf16[304,128]{1,0:T(8,128)(2,1)S(1)}, bf16[304,128]{1,0:T(8,128)(2,1)S(1)}, u32[]{:S(2)}, u32[]{:S(2)}) collective-permute-start(bf16[304,128]{1,0:T(8,128)(2,1)S(1)} %collective-permute-done.4.rest_3_), channel_id=1, source_target_pairs={{0,4},{4,0},{1,5},{5,1},{2,6},{6,2},{3,7},{7,3},{8,12},{12,8},{9,1... | collective-permute-start | bytes 233480 | tf_op jit(solution)/shard_map/ppermute | solution.py:779
  19.2 1.3 %collective-permute-start.8 = (bf16[304,128]{1,0:T(8,128)(2,1)S(1)}, bf16[304,128]{1,0:T(8,128)(2,1)S(1)}, u32[]{:S(2)}, u32[]{:S(2)}) collective-permute-start(bf16[304,128]{1,0:T(8,128)(2,1)S(1)} %collective-permute-done.5.rest_5_), channel_id=1, source_target_pairs={{0,4},{4,0},{1,5},{5,1},{2,6},{6,2},{3,7},{7,3},{8,12},{12,8},{9,1... | collective-permute-start | bytes 233480 | tf_op jit(solution)/shard_map/ppermute | solution.py:779
  34.6 8.3 %collective-permute-start.9 = (bf16[9,3,16,128]{3,2,1,0:T(8,128)(2,1)S(1)}, bf16[9,3,16,128]{3,2,1,0:T(8,128)(2,1)S(1)}, u32[]{:S(2)}, u32[]{:S(2)}) collective-permute-start(bf16[9,3,16,128]{3,2,1,0:T(8,128)(2,1)S(1)} %get-tuple-element.109), channel_id=1, source_target_pairs={{0,1},{1,2},{2,3},{3,0},{4,5},{5,6},{6,7},{7,4},{8,9},{9,10},{10,1... | collective-permute-start | bytes 331784 | tf_op jit(solution)/shard_map/ppermute | solution.py:779
  35.0 7.9 %collective-permute-start.10 = (bf16[9,3,16,128]{3,2,1,0:T(8,128)(2,1)S(1)}, bf16[9,3,16,128]{3,2,1,0:T(8,128)(2,1)S(1)}, u32[]{:S(2)}, u32[]{:S(2)}) collective-permute-start(bf16[9,3,16,128]{3,2,1,0:T(8,128)(2,1)S(1)} %get-tuple-element.110), channel_id=1, source_target_pairs={{0,3},{1,0},{2,1},{3,2},{4,7},{5,4},{6,5},{7,6},{8,11},{9,8},{10,9... | collective-permute-start | bytes 331784 | tf_op jit(solution)/shard_map/ppermute | solution.py:779
  68.8 10.4 %copy-start = (bf16[12,16,16,128]{3,2,1,0:T(8,128)(2,1)S(1)}, bf16[12,16,16,128]{3,2,1,0:T(8,128)(2,1)}, u32[]{:S(2)}) copy-start(bf16[12,16,16,128]{3,2,1,0:T(8,128)(2,1)} %refs_1_.2) | copy-start | bytes 2359300
  73.7 1.6 %collective-permute-start.11 = (bf16[4,304,128]{2,1,0:T(8,128)(2,1)S(1)}, bf16[4,304,128]{2,1,0:T(8,128)(2,1)S(1)}, u32[]{:S(2)}, u32[]{:S(2)}) collective-permute-start(bf16[4,304,128]{2,1,0:T(8,128)(2,1)S(1)} %get-tuple-element.125), channel_id=1, source_target_pairs={{0,4},{4,0},{1,5},{5,1},{2,6},{6,2},{3,7},{7,3},{8,12},{12,8},{9,1... | collective-permute-start | bytes 933896 | tf_op jit(solution)/shard_map/ppermute | solution.py:779
  75.3 12.3 %copy-start.1 = (bf16[12,16,16,128]{3,2,1,0:T(8,128)(2,1)S(1)}, bf16[12,16,16,128]{3,2,1,0:T(8,128)(2,1)}, u32[]{:S(2)}) copy-start(bf16[12,16,16,128]{3,2,1,0:T(8,128)(2,1)} %cot.3) | copy-start | bytes 2359300
  75.4 7.1 %collective-permute-start.12 = (bf16[304,128]{1,0:T(8,128)(2,1)S(1)}, bf16[304,128]{1,0:T(8,128)(2,1)S(1)}, u32[]{:S(2)}, u32[]{:S(2)}) collective-permute-start(bf16[304,128]{1,0:T(8,128)(2,1)S(1)} %get-tuple-element.130), channel_id=1, source_target_pairs={{0,8},{8,16},{16,24},{24,0},{1,9},{9,17},{17,25},{25,1},{2,10},{10... | collective-permute-start | bytes 233480 | tf_op jit(solution)/shard_map/ppermute | solution.py:779
  76.1 9.0 %collective-permute-start.13 = (bf16[304,128]{1,0:T(8,128)(2,1)S(1)}, bf16[304,128]{1,0:T(8,128)(2,1)S(1)}, u32[]{:S(2)}, u32[]{:S(2)}) collective-permute-start(bf16[304,128]{1,0:T(8,128)(2,1)S(1)} %get-tuple-element.131), channel_id=1, source_target_pairs={{0,16},{8,24},{16,0},{24,8},{1,17},{9,25},{17,1},{25,9},{2,18},{10... | collective-permute-start | bytes 233480 | tf_op jit(solution)/shard_map/ppermute | solution.py:779
  77.1 8.0 %collective-permute-start.14 = (bf16[304,128]{1,0:T(8,128)(2,1)S(1)}, bf16[304,128]{1,0:T(8,128)(2,1)S(1)}, u32[]{:S(2)}, u32[]{:S(2)}) collective-permute-start(bf16[304,128]{1,0:T(8,128)(2,1)S(1)} %get-tuple-element.132), channel_id=1, source_target_pairs={{0,24},{8,0},{16,8},{24,16},{1,25},{9,1},{17,9},{25,17},{2,26},{10... | collective-permute-start | bytes 233480 | tf_op jit(solution)/shard_map/ppermute | solution.py:779
  85.1 5.3 %collective-permute-start.17 = (bf16[304,128]{1,0:T(8,128)(2,1)S(1)}, bf16[304,128]{1,0:T(8,128)(2,1)S(1)}, u32[]{:S(2)}, u32[]{:S(2)}) collective-permute-start(bf16[304,128]{1,0:T(8,128)(2,1)S(1)} %shard_map.184.refs_0_), channel_id=1, source_target_pairs={{0,3},{1,0},{2,1},{3,2},{4,7},{5,4},{6,5},{7,6},{8,11},{9,8},{10,9... | collective-permute-start | bytes 233480 | tf_op jit(solution)/shard_map/ppermute | solution.py:779
  85.9 4.8 %collective-permute-start.16 = (bf16[304,128]{1,0:T(8,128)(2,1)S(1)}, bf16[304,128]{1,0:T(8,128)(2,1)S(1)}, u32[]{:S(2)}, u32[]{:S(2)}) collective-permute-start(bf16[304,128]{1,0:T(8,128)(2,1)S(1)} %shard_map.184.refs_0_), channel_id=1, source_target_pairs={{0,2},{1,3},{2,0},{3,1},{4,6},{5,7},{6,4},{7,5},{8,10},{9,11},{10,... | collective-permute-start | bytes 233480 | tf_op jit(solution)/shard_map/ppermute | solution.py:779
  87.0 5.3 %collective-permute-start.15 = (bf16[304,128]{1,0:T(8,128)(2,1)S(1)}, bf16[304,128]{1,0:T(8,128)(2,1)S(1)}, u32[]{:S(2)}, u32[]{:S(2)}) collective-permute-start(bf16[304,128]{1,0:T(8,128)(2,1)S(1)} %shard_map.184.refs_0_), channel_id=1, source_target_pairs={{0,1},{1,2},{2,3},{3,0},{4,5},{5,6},{6,7},{7,4},{8,9},{9,10},{10,1... | collective-permute-start | bytes 233480 | tf_op jit(solution)/shard_map/ppermute | solution.py:779
  93.1 8.9 %all-to-all-start.3 = ((f32[8,4,128]{2,1,0:T(4,128)}), f32[8,4,128]{2,1,0:T(4,128)S(1)}, u32[]{:S(2)}, u32[]{:S(2)}) async-start(f32[8,4,128]{2,1,0:T(4,128)} %get-tuple-element.140), calls=%async_computation.3 | async-start | bytes 32768 | tf_op jit(solution)/shard_map/all_to_all | solution.py:774
  96.4 5.6 %collective-permute-start.18 = (f32[288,128]{1,0:T(8,128)S(1)}, f32[288,128]{1,0:T(8,128)S(1)}, u32[]{:S(2)}, u32[]{:S(2)}) collective-permute-start(f32[288,128]{1,0:T(8,128)S(1)} %get-tuple-element.133.refs_6_), channel_id=1, source_target_pairs={{0,4},{4,0},{1,5},{5,1},{2,6},{6,2},{3,7},{7,3},{8,12},{12,8},{9,1... | collective-permute-start | bytes 442376 | tf_op jit(solution)/shard_map/ppermute | solution.py:779

commit v5 on v4

--- a/solution.py
+++ b/solution.py
@@ -413,32 +413,6 @@
     sums[...] = jnp.concatenate([down(v) for v in total] + [jnp.zeros((8 - MB, C), F32)], axis=0)
 
 
-def lead_side_kernel(lead, after, lat_in, from_left, from_right, lat, side, *flats):
-    scale = lead_scales(lead)
-    for flat in flats:
-        flat[...] = jnp.zeros(flat.shape, F32)
-    for k in range(2):
-        for n in range(S):
-            lat[k, 16 * n : 16 * n + 16, :] = cot_beyond(lat_in, n, k).astype(F32) * scale[n]
-
-    @pl.loop(0, R // 2 + 1)
-    def _(i):
-        for m in range(MB):
-            left = from_left[i, m].astype(F32)
-            right = from_right[i, m].astype(F32)
-            for odd in range(2):
-                for n in range(PER):
-                    s, at = PER * m + n, 8 * odd + 2 * n
-                    flats[odd][14 + 24 * s : 16 + 24 * s, :] = left[at : at + 2] * scale[s]
-                    flats[odd][32 + 24 * s : 34 + 24 * s, :] = right[at : at + 2] * scale[s]
-        for odd in range(2):
-            row = 2 * i + odd
-            flat = flats[odd]
-            for h in range(NH):
-                side[row, 8 * h : 8 * h + 8, :] = flat[8 + 24 * h : 16 + 24 * h, :]
-            side[row, 8 * NH :, :] = jnp.zeros((TH - 8 * NH, C), F32)
-
-
 def block_kernel(*rest):
     pieces, (block, vec) = rest[:-2], rest[-2:]
     fill_forward(block, pieces, 0)
@@ -519,7 +493,7 @@
 
 
 def back_two_kernel(
-    count, pre_two, dn, dn_lat, dn_side, sums_in, pre, block, vec, grad, mid, sums, kept, bias_two, g_all, *flats
+    count, lead, pre_two, dn, lat_in, from_left, from_right, sums_in, pre, block, vec, grad, mid, sums, kept, bias_two, g_all, *flats
 ):
     total = jnp.sum(sums_in[...], axis=0)
     kept[...] = jnp.concatenate([total[g, i : i + 1] for g in range(MB) for i in range(4)], axis=0)
@@ -530,29 +504,40 @@
     for edge in (0, R + 3):
         g_all[edge // 2, edge % 2] = jnp.zeros((T, W3), BF16)
 
-    def make(odd, place, row, inner, inner_row):
+    scale = lead_scales(lead)
+    sides = flats[2:]
+
+    def make(row):
+        odd, i = row % 2, row // 2
+        for m in range(MB):
+            left, right = from_left[i, m].astype(F32), from_right[i, m].astype(F32)
+            for n in range(PER):
+                s, at = PER * m + n, 8 * odd + 2 * n
+                sides[odd][14 + 24 * s : 16 + 24 * s, :] = left[at : at + 2] * scale[s]
+                sides[odd][32 + 24 * s : 34 + 24 * s, :] = right[at : at + 2] * scale[s]
+        if row < R:
+            incoming = lambda n: dn[row, 16 * n : 16 * n + 16, :]
+        else:
+            incoming = lambda n: cot_beyond(lat_in, n, row - R).astype(F32) * scale[n]
         build_back(
             flats[odd],
             g_all,
-            place,
+            place_of(i, odd),
             terms,
             lambda n: pre_two[row, 16 * n : 16 * n + 16, :],
-            lambda n: inner[inner_row, 16 * n : 16 * n + 16, :],
+            incoming,
             lambda h: pre_two[row, TI + 8 * h : TI + 8 * h + 8, :],
-            lambda h: dn_side[row, 8 * h : 8 * h + 8, :],
+            lambda h: sides[odd][8 + 24 * h : 16 + 24 * h, :],
         )
 
     biases = []
 
     def row_of(row):
-        place = place_of(row // 2, row % 2)
+        make(row)
         if row < R:
-            make(row % 2, place, row, dn, row)
-            own = g_all[place + (slice(0, TI), slice(C, 2 * C))]
+            own = g_all[place_of(row // 2, row % 2) + (slice(0, TI), slice(C, 2 * C))]
             grad[row] = own
             biases.append(fold(own.astype(F32)))
-        else:
-            make(row % 2, place, row, dn_lat, row - R)
 
     def conv(low, high, total):
         for n, v in enumerate(conv_rows(g_all, low, high, block[...])):
@@ -865,21 +850,14 @@
         flats,
         flops=conv_flops * 9,
     )
-    dn_lat, dn_side = call(
-        lead_side_kernel,
-        [((2, TI, C), F32), ((R + 2, TH, C), F32)],
-        (lead_time, sums_two, lat_in, cot_left, cot_right),
-        flats,
-        flops=10**8,
-        scalars=1,
-    )
-    sums_two, dn_lat, dn_side = lax.optimization_barrier((sums_two, dn_lat, dn_side))
+    sums_two, cot_left, cot_right = lax.optimization_barrier((sums_two, cot_left, cot_right))
     got_two = spread(sums_two, ALL)
     grad_two, mid, sums_three, stat_two, bias_two = call(
         lambda *refs: back_two_kernel(count, *refs),
         [((R, TI, C), BF16), ((R + 2, T, C), F32), ((devices, MB, 2, C), F32), ((4 * MB, C), F32), ((8, C), F32)],
-        (pre_two, dn, dn_lat, dn_side, got_two, pre_one, two_back, vec),
-        [pltpu.VMEM((10, 2, T, W3), BF16)] + flats,
+        (lead_time, pre_two, dn, lat_in, cot_left, cot_right, got_two, pre_one, two_back, vec),
+        [pltpu.VMEM((10, 2, T, W3), BF16)] + flats * 2,
+        scalars=1,
         flops=conv_flops * 9,
     )
     got_three = spread(sums_three, ALL)

time: 104 us -> 104 us (level)
    pallas_call x20 -> x19, Pallas kernels: 29.4 us -> 29.4 us  [call(): pl.pallas_call(kernel, out_shape=tuple((pltpu.HBM(shape, kind) if n in fa...]
where the time goes in v5:
time: 104 us; the launch traced here: 103 us
  blocking collectives  32.4 us (31%)
  Pallas kernels  29.4 us (28%)
  starting transfers between devices  22.8 us (22%)
  waiting for transfers between devices  17.8 us (17%)
    all_to_all x3, blocking collectives, spread(): return lax.all_to_all(block, axes, 0, 0, tiled=True)  32.4 us
    pallas_call x19, Pallas kernels, call(): pl.pallas_call(kernel, out_shape=tuple((pltpu.HBM(shape, kind) if n in fa...  29.4 us
    ppermute x19, starting transfers between devices, turn(): lax.ppermute(block, axis, [(i, (i + by) % size) for i in range(size)])  19.5 us
    ppermute x19, waiting for transfers between devices, turn(): lax.ppermute(block, axis, [(i, (i + by) % size) for i in range(size)])  13.9 us
    all_to_all x1, waiting for transfers between devices, spread(): return lax.all_to_all(block, axes, 0, 0, tiled=True)  3.97 us
    all_to_all x1, starting transfers between devices, spread(): return lax.all_to_all(block, axes, 0, 0, tiled=True)  3.34 us
  transfers between devices with their start and end apart: 20, of which 11 were waited for; matrix products, arithmetic and copies ran while one was open for 0% of the time, Pallas kernels for 13%

profile of v5, /device:TPU:0, one launch (start us, length us, event | category | flops | bytes accessed | tf_op | source)
XLA Modules:
  0.0 103.2 jit_solution(7019765251647667333)
XLA Ops:
  0.6 0.0 copy-start.2
  0.7 1.1 %shard_map.169 = (bf16[2,304,128]{2,1,0:T(8,128)(2,1)S(1)}, bf16[12,6,16,128]{3,2,1,0:T(8,128)(2,1)S(1)}) custom-call(bf16[12,16,16,128]{3,2,1,0:T(8,128)(2,1)} %refs_1_.2, bf16[12,16,16,128]{3,2,1,0:T(8,128)(2,1)} %cot.3, f32[2,288,128]{2,1,0:T(8,128)} %refs_0_.3, f32[6,32]{1,0:T(8,128)} %refs_3_.1), custom_call_target="tpu_custom_call" | custom-call | bytes 1868544 | tf_op jit(solution)/shard_map/pallas_call | solution.py:45
  1.8 0.5 collective-permute-start
  2.3 1.4 %shard_map.168 = (bf16[12,16,16,128]{3,2,1,0:T(8,128)(2,1)S(1)}, bf16[12,16,16,128]{3,2,1,0:T(8,128)(2,1)S(1)}, bf16[20,3,16,128]{3,2,1,0:T(8,128)(2,1)S(1)}, bf16[20,3,16,128]{3,2,1,0:T(8,128)(2,1)S(1)}) custom-call(bf16[12,16,16,128]{3,2,1,0:T(8,128)(2,1)} %refs_1_.2, bf16[12,16,16,128]{3,2,1,0:T(8,128)(2,1)} %cot.3), custom_call_target="tpu_custom_call" | custom-call | bytes 1572864 | tf_op jit(solution)/shard_map/pallas_call | solution.py:45
  3.7 0.0 collective-permute-done.lat_in.refs_3_
  3.8 2.7 %collective-permute-start.1 = (bf16[20,3,16,128]{3,2,1,0:T(8,128)(2,1)S(1)}, bf16[20,3,16,128]{3,2,1,0:T(8,128)(2,1)S(1)}, u32[]{:S(2)}, u32[]{:S(2)}) collective-permute-start(bf16[20,3,16,128]{3,2,1,0:T(8,128)(2,1)S(1)} %get-tuple-element.83), channel_id=1, source_target_pairs={{0,1},{1,2},{2,3},{3,0},{4,5},{5,6},{6,7},{7,4},{8,9},{9,10},{10,1... | collective-permute-start | bytes 737288 | tf_op jit(solution)/shard_map/ppermute | solution.py:764
  6.5 1.0 collective-permute-start.2
  7.5 4.0 %collective-permute-start.5 = (bf16[304,128]{1,0:T(8,128)(2,1)S(1)}, bf16[304,128]{1,0:T(8,128)(2,1)S(1)}, u32[]{:S(2)}, u32[]{:S(2)}) collective-permute-start(bf16[304,128]{1,0:T(8,128)(2,1)S(1)} %get-tuple-element.85), channel_id=1, source_target_pairs={{0,24},{8,0},{16,8},{24,16},{1,25},{9,1},{17,9},{25,17},{2,26},{10... | collective-permute-start | bytes 233480 | tf_op jit(solution)/shard_map/ppermute | solution.py:764
  11.5 0.0 collective-permute-start.4
  11.5 1.0 collective-permute-start.3
  12.5 0.0 copy-done.2
  12.5 0.9 shard_map.171
  13.4 0.3 shard_map.172
  13.7 0.6 collective-permute-done.5.rest_5_
  14.3 4.4 %collective-permute-done.4.rest_3_ = bf16[304,128]{1,0:T(8,128)(2,1)S(1)} collective-permute-done((bf16[304,128]{1,0:T(8,128)(2,1)S(1)}, bf16[304,128]{1,0:T(8,128)(2,1)S(1)}, u32[]{:S(2)}, u32[]{:S(2)}) %collective-permute-start.4) | collective-permute-done | bytes 77856 | tf_op jit(solution)/shard_map/ppermute | solution.py:764
  18.7 0.0 collective-permute-done.3.rest_1_
  18.7 0.0 collective-permute-start.6
  18.7 0.5 collective-permute-start.7
  19.2 0.0 collective-permute-start.8
  19.2 0.8 collective-permute-done.6.rest_2_
  20.0 0.2 collective-permute-done.7.rest_4_
  20.1 0.4 collective-permute-done.8.rest_6_
  20.5 0.1 shard_map.173
  20.6 0.0 collective-permute-done.1.from_left
  20.6 0.0 collective-permute-done.2.from_right
  20.6 2.5 %shard_map.174 = (bf16[11,2,192,384]{3,2,1,0:T(8,128)(2,1)S(1)}, f32[20,192,128]{2,1,0:T(8,128)S(1)}, f32[32,3,2,128]{3,2,1,0:T(2,128)S(1)}) custom-call(bf16[12,16,16,128]{3,2,1,0:T(8,128)(2,1)S(1)} %get-tuple-element.78.x, bf16[12,6,16,128]{3,2,1,0:T(8,128)(2,1)S(1)} %collective-permute-done.lat_in.refs_3_, ...), custom_call_target="tpu_custom_call" | custom-call | flops 1434451968 | bytes 2367488 | tf_op jit(solution)/shard_map/pallas_call | solution.py:45
  23.2 11.4 %all_to_all.20.after.refs_2_ = f32[32,3,2,128]{3,2,1,0:T(2,128)S(1)} all-to-all(f32[32,3,2,128]{3,2,1,0:T(2,128)S(1)} %get-tuple-element.98), channel_id=1, replica_groups=mesh['dp'=4,'lat'=2,'lon'=4] {'dp','lat','lon'}, dimensions={0} | all-to-all | bytes 196608 | tf_op jit(solution)/shard_map/all_to_all | solution.py:759
  34.6 0.4 collective-permute-start.9
  35.0 2.5 %collective-permute-start.10 = (bf16[9,3,16,128]{3,2,1,0:T(8,128)(2,1)S(1)}, bf16[9,3,16,128]{3,2,1,0:T(8,128)(2,1)S(1)}, u32[]{:S(2)}, u32[]{:S(2)}) collective-permute-start(bf16[9,3,16,128]{3,2,1,0:T(8,128)(2,1)S(1)} %get-tuple-element.108), channel_id=1, source_target_pairs={{0,3},{1,0},{2,1},{3,2},{4,7},{5,4},{6,5},{7,6},{8,11},{9,8},{10,9... | collective-permute-start | bytes 331784 | tf_op jit(solution)/shard_map/ppermute | solution.py:764
  37.5 1.3 %shard_map.175.refs_1_ = f32[20,112,128]{2,1,0:T(8,128)S(1)} custom-call(f32[32,3,2,128]{3,2,1,0:T(2,128)S(1)} %all_to_all.20.after.refs_2_, bf16[12,16,16,128]{3,2,1,0:T(8,128)(2,1)S(1)} %get-tuple-element.78.x, bf16[12,6,16,128]{3,2,1,0:T(8,128)(2,1)S(1)} %collective-permute-done.lat_in.refs_3_, ...), custom_call_target="tpu_custom_call" | custom-call | flops 956301312 | bytes 2465792 | tf_op jit(solution)/shard_map/pallas_call | solution.py:45
  38.9 0.4 shard_map.176
  39.3 3.6 %shard_map.177 = (bf16[10,2,304,384]{3,2,1,0:T(8,128)(2,1)S(1)}, f32[18,304,128]{2,1,0:T(8,128)S(1)}, f32[32,3,4,128]{3,2,1,0:T(4,128)S(1)}, f32[8,128]{1,0:T(8,128)S(1)}) custom-call(f32[20,192,128]{2,1,0:T(8,128)S(1)} %get-tuple-element.95.refs_0_.refs_7_, f32[20,112,128]{2,1,0:T(8,128)S(1)} %shard_map.175.refs_1_, ...), custom_call_target="tpu_custom_call" | custom-call | flops 2151677952 | bytes 5582848 | tf_op jit(solution)/shard_map/pallas_call | solution.py:45
  42.8 0.0 collective-permute-done.9.refs_4_
  42.8 0.0 collective-permute-done.10.refs_5_
  42.9 11.2 %all_to_all.21.refs_6_ = f32[32,3,4,128]{3,2,1,0:T(4,128)S(1)} all-to-all(f32[32,3,4,128]{3,2,1,0:T(4,128)S(1)} %get-tuple-element.111), channel_id=1, replica_groups=mesh['dp'=4,'lat'=2,'lon'=4] {'dp','lat','lon'}, dimensions={0} | all-to-all | bytes 393216 | tf_op jit(solution)/shard_map/all_to_all | solution.py:759
  54.0 4.8 %shard_map.178 = (bf16[16,192,128]{2,1,0:T(8,128)(2,1)S(1)}, f32[18,304,128]{2,1,0:T(8,128)S(1)}, f32[32,3,2,128]{3,2,1,0:T(2,128)S(1)}, f32[12,128]{1,0:T(8,128)S(1)}, f32[8,128]{1,0:T(8,128)S(1)}) custom-call(s32[12]{0:T(128)S(1)} %copy-done.2, f32[18,304,128]{2,1,0:T(8,128)S(1)} %get-tuple-element.105.refs_1_.refs_2_, ...), custom_call_target="tpu_custom_call" | custom-call | flops 2151677952 | bytes 7847984 | tf_op jit(solution)/shard_map/pallas_call | solution.py:45
  58.9 9.8 %all_to_all.22.refs_4_ = f32[32,3,2,128]{3,2,1,0:T(2,128)S(1)} all-to-all(f32[32,3,2,128]{3,2,1,0:T(2,128)S(1)} %get-tuple-element.115), channel_id=1, replica_groups=mesh['dp'=4,'lat'=2,'lon'=4] {'dp','lat','lon'}, dimensions={0} | all-to-all | bytes 196608 | tf_op jit(solution)/shard_map/all_to_all | solution.py:759
  68.7 4.9 %shard_map.179 = (bf16[9,2,192,384]{3,2,1,0:T(8,128)(2,1)S(1)}, f32[8,128]{1,0:T(8,128)}, f32[8,128]{1,0:T(8,128)S(1)}, f32[4,304,128]{2,1,0:T(8,128)S(1)}, bf16[4,304,128]{2,1,0:T(8,128)(2,1)S(1)}) custom-call(f32[20,192,128]{2,1,0:T(8,128)S(1)} %get-tuple-element.95.refs_0_.refs_7_, f32[20,112,128]{2,1,0:T(8,128)S(1)} %shard_map.175.refs_1_, ...), custom_call_target="tpu_custom_call" | custom-call | flops 2151677952 | bytes 14729216 | tf_op jit(solution)/shard_map/pallas_call | solution.py:45
  73.6 0.0 collective-permute-start.11
  73.6 1.6 %collective-permute-done.11.got = bf16[4,304,128]{2,1,0:T(8,128)(2,1)S(1)} collective-permute-done((bf16[4,304,128]{2,1,0:T(8,128)(2,1)S(1)}, bf16[4,304,128]{2,1,0:T(8,128)(2,1)S(1)}, u32[]{:S(2)}, u32[]{:S(2)}) %collective-permute-start.11) | collective-permute-done | bytes 311328 | tf_op jit(solution)/shard_map/ppermute | solution.py:764
  75.2 0.1 shard_map.180
  75.3 0.7 collective-permute-start.12
  76.0 1.0 collective-permute-start.13
  77.0 2.2 %collective-permute-start.14 = (bf16[304,128]{1,0:T(8,128)(2,1)S(1)}, bf16[304,128]{1,0:T(8,128)(2,1)S(1)}, u32[]{:S(2)}, u32[]{:S(2)}) collective-permute-start(bf16[304,128]{1,0:T(8,128)(2,1)S(1)} %get-tuple-element.128), channel_id=1, source_target_pairs={{0,24},{8,0},{16,8},{24,16},{1,25},{9,1},{17,9},{25,17},{2,26},{10... | collective-permute-start | bytes 233480 | tf_op jit(solution)/shard_map/ppermute | solution.py:764
  79.2 0.0 copy-done
  79.2 1.7 %shard_map.181.outputs = bf16[12,16,16,128]{3,2,1,0:T(8,128)(2,1)} custom-call(bf16[304,128]{1,0:T(8,128)(2,1)S(1)} %get-tuple-element.122.refs_0_.after, bf16[12,16,16,128]{3,2,1,0:T(8,128)(2,1)S(1)} %copy-done, f32[18,304,128]{2,1,0:T(8,128)S(1)} %get-tuple-element.105.refs_1_.refs_2_, f32[12,128]{1,0:T(8,128)S(1)} %get-tuple-element.123.refs_3_.refs_10_, ...), custom_call_target="tpu_custom_call" | custom-call | flops 100000000 | bytes 3680256 | tf_op jit(solution)/shard_map/pallas_call | solution.py:45
  80.8 1.6 %collective-permute-done.12.refs_1_ = bf16[304,128]{1,0:T(8,128)(2,1)S(1)} collective-permute-done((bf16[304,128]{1,0:T(8,128)(2,1)S(1)}, bf16[304,128]{1,0:T(8,128)(2,1)S(1)}, u32[]{:S(2)}, u32[]{:S(2)}) %collective-permute-start.12) | collective-permute-done | bytes 77856 | tf_op jit(solution)/shard_map/ppermute | solution.py:764
  82.4 2.5 %collective-permute-done.13.refs_2_ = bf16[304,128]{1,0:T(8,128)(2,1)S(1)} collective-permute-done((bf16[304,128]{1,0:T(8,128)(2,1)S(1)}, bf16[304,128]{1,0:T(8,128)(2,1)S(1)}, u32[]{:S(2)}, u32[]{:S(2)}) %collective-permute-start.13) | collective-permute-done | bytes 77856 | tf_op jit(solution)/shard_map/ppermute | solution.py:764
  85.0 0.0 collective-permute-done.14.refs_3_
  85.0 0.1 shard_map.183.refs_0_
  85.0 0.7 collective-permute-start.17
  85.8 1.1 %collective-permute-start.16 = (bf16[304,128]{1,0:T(8,128)(2,1)S(1)}, bf16[304,128]{1,0:T(8,128)(2,1)S(1)}, u32[]{:S(2)}, u32[]{:S(2)}) collective-permute-start(bf16[304,128]{1,0:T(8,128)(2,1)S(1)} %shard_map.183.refs_0_), channel_id=1, source_target_pairs={{0,2},{1,3},{2,0},{3,1},{4,6},{5,7},{6,4},{7,5},{8,10},{9,11},{10,... | collective-permute-start | bytes 233480 | tf_op jit(solution)/shard_map/ppermute | solution.py:764
  86.9 0.6 collective-permute-start.15
  87.5 2.9 %shard_map.182.grad_inputs = bf16[12,16,16,128]{3,2,1,0:T(8,128)(2,1)} custom-call(s32[12]{0:T(128)S(1)} %copy-done.2, bf16[304,128]{1,0:T(8,128)(2,1)S(1)} %get-tuple-element.122.refs_0_.after, bf16[9,2,192,384]{3,2,1,0:T(8,128)(2,1)S(1)} %get-tuple-element.124.g_inner, bf16[12,16,16,128]{3,2,1,0:T(8,128)(2,1)S(1)} %copy-done.1, ...), custom_call_target="tpu_custom_call" | custom-call | flops 1434451968 | bytes 4304944 | tf_op jit(solution)/shard_map/pallas_call | solution.py:45
  90.4 0.0 collective-permute-done.17.refs_3_
  90.4 0.2 collective-permute-done.16.refs_2_
  90.6 1.6 %collective-permute-done.15.refs_1_ = bf16[304,128]{1,0:T(8,128)(2,1)S(1)} collective-permute-done((bf16[304,128]{1,0:T(8,128)(2,1)S(1)}, bf16[304,128]{1,0:T(8,128)(2,1)S(1)}, u32[]{:S(2)}, u32[]{:S(2)}) %collective-permute-start.15) | collective-permute-done | bytes 77856 | tf_op jit(solution)/shard_map/ppermute | solution.py:764
  92.2 0.7 shard_map.184
  93.0 3.3 %all-to-all-start.3 = ((f32[8,4,128]{2,1,0:T(4,128)}), f32[8,4,128]{2,1,0:T(4,128)S(1)}, u32[]{:S(2)}, u32[]{:S(2)}) async-start(f32[8,4,128]{2,1,0:T(4,128)} %get-tuple-element.136), calls=%async_computation.3 | async-start | bytes 32768 | tf_op jit(solution)/shard_map/all_to_all | solution.py:759
  96.3 0.4 collective-permute-start.18
  96.7 1.2 %shard_map.185 = (f32[2,288,128]{2,1,0:T(8,128)S(1)}, f32[2,288,128]{2,1,0:T(8,128)S(1)}, f32[2,288,128]{2,1,0:T(8,128)S(1)}, f32[6,32]{1,0:T(8,128)S(1)}, f32[6,32]{1,0:T(8,128)S(1)}, /*index=5*/f32[6,32]{1,0:T(8,128)S(1)}) custom-call(f32[2,288,128]{2,1,0:T(8,128)} %refs_0_.3, f32[2,288,128]{2,1,0:T(8,128)} %refs_1_.3, f32[2,288,128]{2,1,0:T(8,128)} %refs_2_.1, ...), custom_call_target="tpu_custom_call" | custom-call | flops 10000000000 | bytes 1034496 | tf_op jit(solution)/shard_map/pallas_call | solution.py:45
  97.9 4.0 %all-to-all-done.3.refs_8_ = f32[8,4,128]{2,1,0:T(4,128)S(1)} async-done(((f32[8,4,128]{2,1,0:T(4,128)}), f32[8,4,128]{2,1,0:T(4,128)S(1)}, u32[]{:S(2)}, u32[]{:S(2)}) %all-to-all-start.3) | async-done | bytes 16416 | tf_op jit(solution)/shard_map/all_to_all | solution.py:759
  101.9 0.0 collective-permute-done.18.refs_7_
  101.9 1.4 %shard_map.186 = (f32[1,1]{1,0:T(1,128)}, f32[2,288,128]{2,1,0:T(8,128)}, f32[2,288,128]{2,1,0:T(8,128)}, f32[2,288,128]{2,1,0:T(8,128)}, bf16[2,288,128]{2,1,0:...) custom-call(f32[2,288,128]{2,1,0:T(8,128)S(1)} %get-tuple-element.130.refs_0_, ...), custom_call_target="tpu_custom_call" | custom-call | bytes 1212672 | tf_op jit(solution)/shard_map/pallas_call | solution.py:45
  (4 shorter events, 0.1 us)
Async XLA Ops:
  0.6 11.9 %copy-start.2 = (s32[12]{0:T(128)S(1)}, s32[12]{0:T(128)}, u32[]{:S(2)}) copy-start(s32[12]{0:T(128)} %lead.3) | copy-start | bytes 148
  1.8 1.9 %collective-permute-start = (bf16[12,6,16,128]{3,2,1,0:T(8,128)(2,1)S(1)}, bf16[12,6,16,128]{3,2,1,0:T(8,128)(2,1)S(1)}, u32[]{:S(2)}, u32[]{:S(2)}) collective-permute-start(bf16[12,6,16,128]{3,2,1,0:T(8,128)(2,1)S(1)} %get-tuple-element.79), channel_id=1, source_target_pairs={{0,4},{4,0},{1,5},{5,1},{2,6},{6,2},{3,7},{7,3},{8,12},{12,8},{9,1... | collective-permute-start | bytes 884744 | tf_op jit(solution)/shard_map/ppermute | solution.py:764
  3.8 16.8 %collective-permute-start.1 = (bf16[20,3,16,128]{3,2,1,0:T(8,128)(2,1)S(1)}, bf16[20,3,16,128]{3,2,1,0:T(8,128)(2,1)S(1)}, u32[]{:S(2)}, u32[]{:S(2)}) collective-permute-start(bf16[20,3,16,128]{3,2,1,0:T(8,128)(2,1)S(1)} %get-tuple-element.83), channel_id=1, source_target_pairs={{0,1},{1,2},{2,3},{3,0},{4,5},{5,6},{6,7},{7,4},{8,9},{9,10},{10,1... | collective-permute-start | bytes 737288 | tf_op jit(solution)/shard_map/ppermute | solution.py:764
  6.5 14.1 %collective-permute-start.2 = (bf16[20,3,16,128]{3,2,1,0:T(8,128)(2,1)S(1)}, bf16[20,3,16,128]{3,2,1,0:T(8,128)(2,1)S(1)}, u32[]{:S(2)}, u32[]{:S(2)}) collective-permute-start(bf16[20,3,16,128]{3,2,1,0:T(8,128)(2,1)S(1)} %get-tuple-element.84), channel_id=1, source_target_pairs={{0,3},{1,0},{2,1},{3,2},{4,7},{5,4},{6,5},{7,6},{8,11},{9,8},{10,9... | collective-permute-start | bytes 737288 | tf_op jit(solution)/shard_map/ppermute | solution.py:764
  7.5 6.8 %collective-permute-start.5 = (bf16[304,128]{1,0:T(8,128)(2,1)S(1)}, bf16[304,128]{1,0:T(8,128)(2,1)S(1)}, u32[]{:S(2)}, u32[]{:S(2)}) collective-permute-start(bf16[304,128]{1,0:T(8,128)(2,1)S(1)} %get-tuple-element.85), channel_id=1, source_target_pairs={{0,24},{8,0},{16,8},{24,16},{1,25},{9,1},{17,9},{25,17},{2,26},{10... | collective-permute-start | bytes 233480 | tf_op jit(solution)/shard_map/ppermute | solution.py:764
  11.5 7.2 %collective-permute-start.4 = (bf16[304,128]{1,0:T(8,128)(2,1)S(1)}, bf16[304,128]{1,0:T(8,128)(2,1)S(1)}, u32[]{:S(2)}, u32[]{:S(2)}) collective-permute-start(bf16[304,128]{1,0:T(8,128)(2,1)S(1)} %get-tuple-element.85), channel_id=1, source_target_pairs={{0,16},{8,24},{16,0},{24,8},{1,17},{9,25},{17,1},{25,9},{2,18},{10... | collective-permute-start | bytes 233480 | tf_op jit(solution)/shard_map/ppermute | solution.py:764
  11.5 7.2 %collective-permute-start.3 = (bf16[304,128]{1,0:T(8,128)(2,1)S(1)}, bf16[304,128]{1,0:T(8,128)(2,1)S(1)}, u32[]{:S(2)}, u32[]{:S(2)}) collective-permute-start(bf16[304,128]{1,0:T(8,128)(2,1)S(1)} %get-tuple-element.85), channel_id=1, source_target_pairs={{0,8},{8,16},{16,24},{24,0},{1,9},{9,17},{17,25},{25,1},{2,10},{10... | collective-permute-start | bytes 233480 | tf_op jit(solution)/shard_map/ppermute | solution.py:764
  18.7 1.3 %collective-permute-start.6 = (bf16[304,128]{1,0:T(8,128)(2,1)S(1)}, bf16[304,128]{1,0:T(8,128)(2,1)S(1)}, u32[]{:S(2)}, u32[]{:S(2)}) collective-permute-start(bf16[304,128]{1,0:T(8,128)(2,1)S(1)} %collective-permute-done.3.rest_1_), channel_id=1, source_target_pairs={{0,4},{4,0},{1,5},{5,1},{2,6},{6,2},{3,7},{7,3},{8,12},{12,8},{9,1... | collective-permute-start | bytes 233480 | tf_op jit(solution)/shard_map/ppermute | solution.py:764
  18.7 1.4 %collective-permute-start.7 = (bf16[304,128]{1,0:T(8,128)(2,1)S(1)}, bf16[304,128]{1,0:T(8,128)(2,1)S(1)}, u32[]{:S(2)}, u32[]{:S(2)}) collective-permute-start(bf16[304,128]{1,0:T(8,128)(2,1)S(1)} %collective-permute-done.4.rest_3_), channel_id=1, source_target_pairs={{0,4},{4,0},{1,5},{5,1},{2,6},{6,2},{3,7},{7,3},{8,12},{12,8},{9,1... | collective-permute-start | bytes 233480 | tf_op jit(solution)/shard_map/ppermute | solution.py:764
  19.2 1.3 %collective-permute-start.8 = (bf16[304,128]{1,0:T(8,128)(2,1)S(1)}, bf16[304,128]{1,0:T(8,128)(2,1)S(1)}, u32[]{:S(2)}, u32[]{:S(2)}) collective-permute-start(bf16[304,128]{1,0:T(8,128)(2,1)S(1)} %collective-permute-done.5.rest_5_), channel_id=1, source_target_pairs={{0,4},{4,0},{1,5},{5,1},{2,6},{6,2},{3,7},{7,3},{8,12},{12,8},{9,1... | collective-permute-start | bytes 233480 | tf_op jit(solution)/shard_map/ppermute | solution.py:764
  34.6 8.2 %collective-permute-start.9 = (bf16[9,3,16,128]{3,2,1,0:T(8,128)(2,1)S(1)}, bf16[9,3,16,128]{3,2,1,0:T(8,128)(2,1)S(1)}, u32[]{:S(2)}, u32[]{:S(2)}) collective-permute-start(bf16[9,3,16,128]{3,2,1,0:T(8,128)(2,1)S(1)} %get-tuple-element.107), channel_id=1, source_target_pairs={{0,1},{1,2},{2,3},{3,0},{4,5},{5,6},{6,7},{7,4},{8,9},{9,10},{10,1... | collective-permute-start | bytes 331784 | tf_op jit(solution)/shard_map/ppermute | solution.py:764
  35.0 7.9 %collective-permute-start.10 = (bf16[9,3,16,128]{3,2,1,0:T(8,128)(2,1)S(1)}, bf16[9,3,16,128]{3,2,1,0:T(8,128)(2,1)S(1)}, u32[]{:S(2)}, u32[]{:S(2)}) collective-permute-start(bf16[9,3,16,128]{3,2,1,0:T(8,128)(2,1)S(1)} %get-tuple-element.108), channel_id=1, source_target_pairs={{0,3},{1,0},{2,1},{3,2},{4,7},{5,4},{6,5},{7,6},{8,11},{9,8},{10,9... | collective-permute-start | bytes 331784 | tf_op jit(solution)/shard_map/ppermute | solution.py:764
  68.7 10.5 %copy-start = (bf16[12,16,16,128]{3,2,1,0:T(8,128)(2,1)S(1)}, bf16[12,16,16,128]{3,2,1,0:T(8,128)(2,1)}, u32[]{:S(2)}) copy-start(bf16[12,16,16,128]{3,2,1,0:T(8,128)(2,1)} %refs_1_.2) | copy-start | bytes 2359300
  73.6 1.6 %collective-permute-start.11 = (bf16[4,304,128]{2,1,0:T(8,128)(2,1)S(1)}, bf16[4,304,128]{2,1,0:T(8,128)(2,1)S(1)}, u32[]{:S(2)}, u32[]{:S(2)}) collective-permute-start(bf16[4,304,128]{2,1,0:T(8,128)(2,1)S(1)} %get-tuple-element.121), channel_id=1, source_target_pairs={{0,4},{4,0},{1,5},{5,1},{2,6},{6,2},{3,7},{7,3},{8,12},{12,8},{9,1... | collective-permute-start | bytes 933896 | tf_op jit(solution)/shard_map/ppermute | solution.py:764
  75.2 12.3 %copy-start.1 = (bf16[12,16,16,128]{3,2,1,0:T(8,128)(2,1)S(1)}, bf16[12,16,16,128]{3,2,1,0:T(8,128)(2,1)}, u32[]{:S(2)}) copy-start(bf16[12,16,16,128]{3,2,1,0:T(8,128)(2,1)} %cot.3) | copy-start | bytes 2359300
  75.3 7.1 %collective-permute-start.12 = (bf16[304,128]{1,0:T(8,128)(2,1)S(1)}, bf16[304,128]{1,0:T(8,128)(2,1)S(1)}, u32[]{:S(2)}, u32[]{:S(2)}) collective-permute-start(bf16[304,128]{1,0:T(8,128)(2,1)S(1)} %get-tuple-element.126), channel_id=1, source_target_pairs={{0,8},{8,16},{16,24},{24,0},{1,9},{9,17},{17,25},{25,1},{2,10},{10... | collective-permute-start | bytes 233480 | tf_op jit(solution)/shard_map/ppermute | solution.py:764
  76.0 9.0 %collective-permute-start.13 = (bf16[304,128]{1,0:T(8,128)(2,1)S(1)}, bf16[304,128]{1,0:T(8,128)(2,1)S(1)}, u32[]{:S(2)}, u32[]{:S(2)}) collective-permute-start(bf16[304,128]{1,0:T(8,128)(2,1)S(1)} %get-tuple-element.127), channel_id=1, source_target_pairs={{0,16},{8,24},{16,0},{24,8},{1,17},{9,25},{17,1},{25,9},{2,18},{10... | collective-permute-start | bytes 233480 | tf_op jit(solution)/shard_map/ppermute | solution.py:764
  77.0 8.0 %collective-permute-start.14 = (bf16[304,128]{1,0:T(8,128)(2,1)S(1)}, bf16[304,128]{1,0:T(8,128)(2,1)S(1)}, u32[]{:S(2)}, u32[]{:S(2)}) collective-permute-start(bf16[304,128]{1,0:T(8,128)(2,1)S(1)} %get-tuple-element.128), channel_id=1, source_target_pairs={{0,24},{8,0},{16,8},{24,16},{1,25},{9,1},{17,9},{25,17},{2,26},{10... | collective-permute-start | bytes 233480 | tf_op jit(solution)/shard_map/ppermute | solution.py:764
  85.0 5.3 %collective-permute-start.17 = (bf16[304,128]{1,0:T(8,128)(2,1)S(1)}, bf16[304,128]{1,0:T(8,128)(2,1)S(1)}, u32[]{:S(2)}, u32[]{:S(2)}) collective-permute-start(bf16[304,128]{1,0:T(8,128)(2,1)S(1)} %shard_map.183.refs_0_), channel_id=1, source_target_pairs={{0,3},{1,0},{2,1},{3,2},{4,7},{5,4},{6,5},{7,6},{8,11},{9,8},{10,9... | collective-permute-start | bytes 233480 | tf_op jit(solution)/shard_map/ppermute | solution.py:764
  85.8 4.8 %collective-permute-start.16 = (bf16[304,128]{1,0:T(8,128)(2,1)S(1)}, bf16[304,128]{1,0:T(8,128)(2,1)S(1)}, u32[]{:S(2)}, u32[]{:S(2)}) collective-permute-start(bf16[304,128]{1,0:T(8,128)(2,1)S(1)} %shard_map.183.refs_0_), channel_id=1, source_target_pairs={{0,2},{1,3},{2,0},{3,1},{4,6},{5,7},{6,4},{7,5},{8,10},{9,11},{10,... | collective-permute-start | bytes 233480 | tf_op jit(solution)/shard_map/ppermute | solution.py:764
  86.9 5.3 %collective-permute-start.15 = (bf16[304,128]{1,0:T(8,128)(2,1)S(1)}, bf16[304,128]{1,0:T(8,128)(2,1)S(1)}, u32[]{:S(2)}, u32[]{:S(2)}) collective-permute-start(bf16[304,128]{1,0:T(8,128)(2,1)S(1)} %shard_map.183.refs_0_), channel_id=1, source_target_pairs={{0,1},{1,2},{2,3},{3,0},{4,5},{5,6},{6,7},{7,4},{8,9},{9,10},{10,1... | collective-permute-start | bytes 233480 | tf_op jit(solution)/shard_map/ppermute | solution.py:764
  93.0 8.9 %all-to-all-start.3 = ((f32[8,4,128]{2,1,0:T(4,128)}), f32[8,4,128]{2,1,0:T(4,128)S(1)}, u32[]{:S(2)}, u32[]{:S(2)}) async-start(f32[8,4,128]{2,1,0:T(4,128)} %get-tuple-element.136), calls=%async_computation.3 | async-start | bytes 32768 | tf_op jit(solution)/shard_map/all_to_all | solution.py:759
  96.3 5.6 %collective-permute-start.18 = (f32[288,128]{1,0:T(8,128)S(1)}, f32[288,128]{1,0:T(8,128)S(1)}, u32[]{:S(2)}, u32[]{:S(2)}) collective-permute-start(f32[288,128]{1,0:T(8,128)S(1)} %get-tuple-element.129.refs_6_), channel_id=1, source_target_pairs={{0,4},{4,0},{1,5},{5,1},{2,6},{6,2},{3,7},{7,3},{8,12},{12,8},{9,1... | collective-permute-start | bytes 442376 | tf_op jit(solution)/shard_map/ppermute | solution.py:764
